TPU v7x, 128 devices: a whole 4x4x4 slice. The times are simulated.
128 devices in a mesh: gx: 8 (over x, core), gy: 16 (over z, y).
Axes of the slice: x: 4, y: 4, z: 4, core: 2. Of those that a mesh axis runs over, the one named last changes fastest.
Arguments:
- traction: bfloat16 [3, 289, 8, 16, 512], P(None, None, 'gx', 'gy'), may hold values from -6 to 6
- self_operator: bfloat16 [289, 289], replicated, may hold values from -0.375 to 0.375
- translation: bfloat16 [289, 289], replicated, may hold values from -0.09375 to 0.09375
- rotations: bfloat16 [16, 289, 289], replicated
- own_cell: int32 [8, 16, 9, 128], P('gx', 'gy'), may hold values from 0 to 511
- partner_cell: int32 [8, 16, 9, 128], P('gx', 'gy'), may hold values from 0 to 511
- rot_index: int32 [8, 16, 9, 128, 1], P('gx', 'gy'), may hold values from 0 to 15; in each aligned block of 128 rows (0 to 127, 128 to 255, ..., all dimensions but the last counted through in order) at most 16 rows name the same one
- block_count: int32 [8, 16, 9], P('gx', 'gy'), may hold values from 1 to 128, as said below
Outputs:
- velocity: bfloat16 [3, 289, 8, 16, 512], P(None, None, 'gx', 'gy')
Inputs may be any that keep to these rules, and one draw needn't show every extreme that they name: `rot_index`: in each owner pair block of 128 slots no rotation index is named by more than 16 slots, and in every draw some block reaches 16. `block_count`: some block of some region is full in every draw; regions differ in density.
All inputs are finite; a program needn't handle non-finite values.
Results may differ from a plain program's by a relative error of at most 0.0036.
Values may be sent and summed in bfloat16 or wider, within the bound.
No kernel may reach another device: no remote copies, remote signals or barrier semaphores. Data moves between devices by JAX's collectives and lax.ppermute only.
A program may use at most 128 MiB of HBM per device.

v0:
```python
import jax
import jax.numpy as jnp
from jax import lax
from jax.sharding import PartitionSpec as P

CAP = 144


def from_behind(block, axis, distance):
    devices = range(lax.axis_size(axis))
    route = [((i - distance) % len(devices), i) for i in devices]
    return lax.ppermute(block, axis, route)


def with_halo(block, sides, width):
    for axis, dim in sides:
        count = lax.axis_size(axis)
        forward = [(i, i + 1) for i in range(count - 1)]
        forward.append((count - 1, 0))
        backward = [(target, source) for source, target in forward]
        low = lax.ppermute(
            lax.slice_in_dim(block, block.shape[dim] - width, None, axis=dim), axis, forward
        )
        high = lax.ppermute(lax.slice_in_dim(block, 0, width, axis=dim), axis, backward)
        block = jnp.concatenate([low, block, high], axis=dim)
    return block


def parity_signs(size_k):
    positions = jnp.arange(size_k, dtype=jnp.int32)
    squares = positions * positions
    degree = jnp.sum((positions[:, None] >= squares[None, :]).astype(jnp.int32), axis=1) - 1
    return (1 - 2 * (degree % 2)).astype(jnp.float32)


def group_table(rot_flat, live_flat, rot_count, capacity):
    slot_total = rot_flat.shape[0]
    rot_onehot = (rot_flat[:, None] == jnp.arange(rot_count, dtype=jnp.int32)[None, :]).astype(
        jnp.float32
    )
    lower = (
        jnp.arange(slot_total, dtype=jnp.int32)[:, None]
        > jnp.arange(slot_total, dtype=jnp.int32)[None, :]
    ).astype(jnp.float32)
    before = jnp.dot(lower, rot_onehot, precision=lax.Precision.HIGHEST)
    position = (jnp.sum(before * rot_onehot, axis=1) + 0.5).astype(jnp.int32)
    target = rot_flat * capacity + position
    table = (target[:, None] == jnp.arange(rot_count * capacity, dtype=jnp.int32)[None, :]).astype(
        jnp.float32
    )
    weights = jnp.dot(live_flat, table, precision=lax.Precision.HIGHEST)
    return (table, weights)


def cell_table(cell_index, cell_count):
    return (
        cell_index[:, :, None] == jnp.arange(cell_count, dtype=jnp.int32)[None, None, :]
    ).astype(jnp.float32)


def pick_cells(coefs, cell_onehot):
    picked = jnp.einsum(
        "xkon,obn->xkob",
        coefs,
        cell_onehot.astype(jnp.bfloat16),
        preferred_element_type=jnp.float32,
    )
    return picked.astype(jnp.bfloat16).reshape(coefs.shape[0], coefs.shape[1], -1)


def to_groups(slot_values, table, rot_count, capacity):
    grouped = jnp.einsum(
        "xks,sg->xkg", slot_values, table.astype(jnp.bfloat16), preferred_element_type=jnp.float32
    )
    return grouped.astype(jnp.bfloat16).reshape(
        slot_values.shape[0], slot_values.shape[1], rot_count, capacity
    )


def to_slots(group_values, table):
    return jnp.einsum("xkg,sg->xks", group_values, table, precision=lax.Precision.HIGHEST)


def pair_chain(grouped, rotations, translation, parity, weights, with_parity):
    turned = jnp.einsum(
        "rkl,clrn->rckn", rotations, grouped, preferred_element_type=jnp.float32
    ).astype(jnp.bfloat16)
    if with_parity:
        sign_flip = parity[None, None, :, None]
        flipped = turned * sign_flip.astype(jnp.bfloat16)
        toward = (
            jnp.einsum("kl,rcln->rckn", translation, flipped, preferred_element_type=jnp.float32)
            * sign_flip
        ).astype(jnp.bfloat16)
    else:
        toward = jnp.einsum(
            "kl,rcln->rckn", translation, turned, preferred_element_type=jnp.float32
        ).astype(jnp.bfloat16)
    back = (
        jnp.einsum("rlk,rcln->ckrn", rotations, toward, preferred_element_type=jnp.float32)
        * weights[None, None]
    )
    return back.reshape(back.shape[0], back.shape[1], -1)


def move_gy(values, offset):
    return from_behind(values, "gy", offset)


def move_gx(values, offset):
    return from_behind(values, "gx", offset)


def local(
    traction, self_operator, translation, rotations, own_cell, partner_cell, rot_index, block_count
):
    size_k = traction.shape[1]
    cell_count = traction.shape[4]
    slot_count = own_cell.shape[3]
    rot_count = rotations.shape[0]
    capacity = CAP
    parity = parity_signs(size_k)
    own_here = traction[:, :, 0, 0, :]
    neighbours = with_halo(traction, (("gx", 2), ("gy", 3)), 1)
    near_coefs = neighbours.reshape(3, size_k, 9, cell_count)
    live_int = (
        jnp.arange(slot_count, dtype=jnp.int32)[None, :] < block_count[0, 0, :, None]
    ).astype(jnp.int32)
    live_flat = live_int.astype(jnp.float32).reshape(-1)
    rot_flat = rot_index[0, 0, :, :, 0].reshape(-1)
    table, weights = group_table(rot_flat, live_flat, rot_count, capacity)
    grid_weights = weights.reshape(rot_count, capacity)
    own_onehot = cell_table(own_cell[0, 0], cell_count)
    partner_onehot = cell_table(partner_cell[0, 0], cell_count)
    own_slots = (
        jnp.einsum(
            "xkn,obn->xkob",
            own_here,
            own_onehot.astype(jnp.bfloat16),
            preferred_element_type=jnp.float32,
        )
        .astype(jnp.bfloat16)
        .reshape(3, size_k, -1)
    )
    partner_slots = pick_cells(near_coefs, partner_onehot)
    self_term = jnp.einsum(
        "kl,cln->ckn", self_operator, own_here, preferred_element_type=jnp.float32
    )
    both_groups = to_groups(
        jnp.concatenate([partner_slots, own_slots], axis=0), table, rot_count, capacity
    )
    back_own = pair_chain(both_groups[:3], rotations, translation, parity, grid_weights, False)
    back_partner = pair_chain(both_groups[3:], rotations, translation, parity, grid_weights, True)
    slot_terms = to_slots(jnp.concatenate([back_own, back_partner], axis=0), table).reshape(
        6, size_k, 9, slot_count
    )
    own_sum = jnp.einsum(
        "xkob,obn->xkn", slot_terms[:3], own_onehot, precision=lax.Precision.HIGHEST
    )
    outgoing = jnp.einsum(
        "xkob,obn->xkon", slot_terms[3:], partner_onehot, precision=lax.Precision.HIGHEST
    )
    outgoing = outgoing.reshape(3, size_k, 3, 3, cell_count)
    row_sums = (
        outgoing[:, :, :, 1] + move_gy(outgoing[:, :, :, 0], -1) + move_gy(outgoing[:, :, :, 2], 1)
    )
    gotten = row_sums[:, :, 1] + move_gx(row_sums[:, :, 0], -1) + move_gx(row_sums[:, :, 2], 1)
    summed = self_term + own_sum + gotten
    return summed.astype(jnp.bfloat16).reshape(3, size_k, 1, 1, cell_count)


def solution(mesh):
    return jax.shard_map(
        local,
        mesh=mesh,
        in_specs=(
            P(None, None, "gx", "gy", None),
            P(),
            P(),
            P(),
            P("gx", "gy", None, None),
            P("gx", "gy", None, None),
            P("gx", "gy", None, None, None),
            P("gx", "gy", None),
        ),
        out_specs=P(None, None, "gx", "gy", None),
        check_vma=False,
    )
```

profile of v0, /device:TPU:0, one launch (start us, length us, event | category | flops | bytes accessed | tf_op | source)
XLA Modules:
  0.0 455.1 jit_solution(9759067669675258836)
XLA Ops:
  3.0 11.2 %collective-permute-done = bf16[3,289,1,1,512]{4,1,3,2,0:T(8,128)(2,1)S(1)} collective-permute-done((bf16[3,289,1,1,512]{4,1,3,2,0:T(8,128)(2,1)}, bf16[3,289,1,1,512]{4,1,3,2,0:T(8,128)(2,1)S(1)}, u32[]{:S(2)}, u32[]{:S(2)}) %collective-permute-start) | collective-permute-done | bytes 887840 | tf_op jit(solution)/shard_map/ppermute | solution.py:21
  18.4 6.6 %collective-permute-start.3 = (bf16[3,289,3,1,512]{4,1,3,2,0:T(8,128)(2,1)}, bf16[3,289,3,1,512]{4,1,3,2,0:T(8,128)(2,1)}, u32[]{:S(2)}, u32[]{:S(2)}) collective-permute-start(bf16[3,289,3,1,512]{4,1,3,2,0:T(8,128)(2,1)} %constant_dynamic-update-slice_fusion), channel_id=1, source_target_pairs={{1,0},{2,1},{3,2},{4,3},{5,4},{6,5},{7,6},{8,7},{9,8},{10,9},{11,1... | collective-permute-start | bytes 7990280 | tf_op jit(solution)/shard_map/ppermute | solution.py:24
  30.2 5.5 %fusion.6 = f32[1,16,144]{2,0,1:T(1,128)S(1)} fusion(f32[1152,1,1]{0,1,2:T(1,128)} %reshape.114, s32[16,144]{1,0:T(8,128)S(1)} %multiply_add_fusion, s32[1152]{0:T(1024)S(1)} %convert_add_fusion), kind=kOutput, calls=%fused_computation.10 | convolution fusion | flops 34504704 | bytes 27648 | tf_op jit(solution)/shard_map/dot_general | solution.py:51
  40.3 4.4 copy.39
  44.7 4.3 copy.41
  49.7 32.2 %collective-permute-done.3 = bf16[3,289,3,1,512]{4,1,3,2,0:T(8,128)(2,1)} collective-permute-done((bf16[3,289,3,1,512]{4,1,3,2,0:T(8,128)(2,1)}, bf16[3,289,3,1,512]{4,1,3,2,0:T(8,128)(2,1)}, u32[]{:S(2)}, u32[]{:S(2)}) %collective-permute-start.3) | collective-permute-done | bytes 2663456 | tf_op jit(solution)/shard_map/ppermute | solution.py:24
  81.9 5.5 %collective-permute-done.2 = bf16[3,289,3,1,512]{4,1,3,2,0:T(8,128)(2,1)} collective-permute-done((bf16[3,289,3,1,512]{4,1,3,2,0:T(8,128)(2,1)}, bf16[3,289,3,1,512]{4,1,3,2,0:T(8,128)(2,1)}, u32[]{:S(2)}, u32[]{:S(2)}) %collective-permute-start.2) | collective-permute-done | bytes 2663456 | tf_op jit(solution)/shard_map/ppermute | solution.py:21
  87.4 7.0 %pad_maximum_fusion = bf16[3,289,3,3,512]{4,1,3,2,0:T(8,128)(2,1)} fusion(bf16[3,289,3,1,512]{4,1,3,2,0:T(8,128)(2,1)} %collective-permute-done.3, bf16[3,289,3,1,512]{4,1,3,2,0:T(8,128)(2,1)} %constant_dynamic-update-slice_fusion, bf16[3,289,3,1,512]{4,1,3,2,0:T(8,128)(2,1)} %collective-permute-done.2), kind=kLoop, calls=%fused_computation.12 | loop fusion | flops 7990272 | bytes 15980544 | tf_op jit(solution)/shard_map/concatenate | solution.py:25
  94.4 7.1 %copy.37 = bf16[3,289,3,3,512]{4,1,0,3,2:T(8,128)(2,1)} copy(bf16[3,289,3,3,512]{4,1,3,2,0:T(8,128)(2,1)} %pad_maximum_fusion) | data formatting | bytes 15980544 | tf_op jit(solution)/shard_map/concatenate | solution.py:25
  101.6 7.0 %convert_bitcast_fusion.1 = bf16[3,289,9,128]{3,1,0,2:T(8,128)(2,1)} fusion(bf16[3,289,9,512]{3,1,0,2:T(8,128)(2,1)} %bitcast.160, s32[9,128]{1,0:T(8,128)S(1)} %bitcast.165), kind=kOutput, calls=%fused_computation.62 | convolution fusion | flops 1025523072 | bytes 9992448 | tf_op jit(solution)/shard_map/xkon,obn->xkob/dot_general | solution.py:62
  108.6 4.2 copy.38
  117.1 13.5 %convolution_convert_fusion = bf16[6,289,2304]{2,1,0:T(8,128)(2,1)S(1)} fusion(s32[1152]{0:T(1024)} %copy-done.9, bf16[3,289,1152]{2,1,0:T(8,128)(2,1)} %copy.41, bf16[3,289,1152]{2,1,0:T(8,128)(2,1)} %copy.40), kind=kOutput, calls=%fused_computation.13 | convolution fusion | flops 9218748416 | bytes 11990016 | tf_op jit(solution)/shard_map/xks,sg->xkg/dot_general | solution.py:72
  134.3 6.6 %copy.42 = bf16[3,289,2304]{1,2,0:T(8,128)(2,1)} copy(bf16[3,289,2304]{2,1,0:T(8,128)(2,1)} %get-tuple-element.11) | data formatting | bytes 7990272 | tf_op jit(solution)/shard_map/slice | solution.py:152
  140.9 10.4 %fusion.21 = bf16[16,3,144,289]{3,2,1,0:T(8,128)(2,1)} fusion(bf16[3,289,16,144]{1,3,2,0:T(8,128)(2,1)} %bitcast.162, bf16[16,289,289,1]{2,0,1,3:T(8,128)(2,1)S(1)} %bitcast.148, bf16[289,289]{1,0:T(8,128)(2,1)} %param.10), kind=kOutput, calls=%fused_computation.28 | convolution fusion | flops 2311186176 | bytes 10829986 | tf_op jit(solution)/shard_map/kl,rcln->rckn/dot_general | solution.py:96
  151.3 5.9 %multiply_bitcast_fusion.1 = f32[3,289,16,144]{1,3,0,2:T(8,128)S(1)} fusion(f32[16,144]{1,0:T(8,128)} %bitcast.163, bf16[16,3,144,289]{3,2,1,0:T(8,128)(2,1)} %fusion.21, bf16[16,289,289,1]{2,0,1,3:T(8,128)(2,1)S(1)} %bitcast.151), kind=kOutput, calls=%fused_computation.6 | convolution fusion | flops 1156591872 | bytes 14667296 | tf_op jit(solution)/shard_map/rlk,rcln->ckrn/dot_general | solution.py:100
  157.2 4.9 %copy.46 = f32[3,289,16,144]{1,3,2,0:T(8,128)} copy(f32[3,289,16,144]{1,3,0,2:T(8,128)S(1)} %multiply_bitcast_fusion.1) | data formatting | bytes 15980544 | tf_op jit(solution)/shard_map/mul | solution.py:100
  162.2 9.6 %copy.52 = f32[3,289,2304]{2,1,0:T(8,128)} copy(f32[3,289,2304]{1,2,0:T(8,128)} %bitcast.154) | data formatting | bytes 15980544 | tf_op jit(solution)/shard_map/reshape | solution.py:103
  171.8 6.7 %copy.47 = bf16[3,289,2304]{1,2,0:T(8,128)(2,1)} copy(bf16[3,289,2304]{2,1,0:T(8,128)(2,1)} %get-tuple-element.12) | data formatting | bytes 7990272 | tf_op jit(solution)/shard_map/slice | solution.py:153
  178.5 11.4 %fusion.17 = f32[16,3,144,289]{3,2,1,0:T(8,128)} fusion(bf16[3,289,16,144]{1,3,2,0:T(8,128)(2,1)} %bitcast.161, bf16[289]{0:T(512)(128)(2,1)} %get-tuple-element.5, bf16[16,289,289,1]{2,0,1,3:T(8,128)(2,1)S(1)} %bitcast.150, bf16[289,289]{1,0:T(8,128)(2,1)} %param.10), kind=kOutput, calls=%fused_computation.24 | convolution fusion | flops 2313183744 | bytes 14825700 | tf_op jit(solution)/shard_map/kl,rcln->rckn/dot_general | solution.py:92
  189.8 11.8 %multiply_bitcast_fusion = f32[3,289,16,144]{1,3,0,2:T(8,128)} fusion(f32[16,144]{1,0:T(8,128)} %bitcast.164, f32[16,3,144,289]{3,2,1,0:T(8,128)} %fusion.17, f32[289]{0:T(512)S(1)} %get-tuple-element.6, bf16[16,289,289,1]{2,0,1,3:T(8,128)(2,1)S(1)} %bitcast.149), kind=kOutput, calls=%fused_computation.4 | convolution fusion | flops 1160587008 | bytes 18663588 | tf_op jit(solution)/shard_map/rlk,rcln->ckrn/dot_general | solution.py:100
  201.7 9.1 %copy.51 = f32[3,289,16,144]{1,3,2,0:T(8,128)} copy(f32[3,289,16,144]{1,3,0,2:T(8,128)} %multiply_bitcast_fusion) | data formatting | bytes 15980544 | tf_op jit(solution)/shard_map/mul | solution.py:100
  210.8 9.7 %copy.53 = f32[3,289,2304]{2,1,0:T(8,128)} copy(f32[3,289,2304]{1,2,0:T(8,128)} %bitcast.155) | data formatting | bytes 15980544 | tf_op jit(solution)/shard_map/reshape | solution.py:103
  220.4 41.3 %fusion = f32[6,289,1152]{2,1,0:T(8,128)S(1)} fusion(f32[3,289,2304]{2,1,0:T(8,128)} %copy.53, f32[3,289,2304]{2,1,0:T(8,128)} %copy.52, s32[1152]{0:T(1024)S(1)} %copy-done.10), kind=kOutput, calls=%fused_computation | convolution fusion | flops 55235411968 | bytes 23975424 | tf_op jit(solution)/shard_map/xkg,sg->xks/dot_general | solution.py:81
  265.4 6.0 %copy.56 = f32[3,289,1152]{1,2,0:T(8,128)} copy(f32[3,289,1152]{2,1,0:T(8,128)} %get-tuple-element.10) | data formatting | bytes 7990272 | tf_op jit(solution)/shard_map/slice | solution.py:161
  271.5 14.9 %fusion.15 = f32[9,512,3,289]{1,3,2,0:T(8,128)} fusion(f32[3,289,9,128]{1,3,2,0:T(8,128)} %bitcast.157, s32[9,128]{1,0:T(8,128)S(1)} %bitcast.166), kind=kOutput, calls=%fused_computation.22 | convolution fusion | flops 6137118720 | bytes 19980288 | tf_op jit(solution)/shard_map/xkob,obn->xkon/dot_general | solution.py:160
  286.4 7.9 %slice_bitcast_fusion.1 = (f32[3,289,3,512]{3,1,0,2:T(8,128)}, f32[3,289,3,512]{3,1,0,2:T(8,128)S(1)}) fusion(f32[3,289,3,3,512]{4,1,0,3,2:T(8,128)} %bitcast.152), kind=kLoop, calls=%fused_computation.15 | loop fusion | bytes 21307392 | tf_op jit(solution)/shard_map/squeeze | solution.py:165
  296.3 114.5 %collective-permute-done.4 = f32[3,289,3,512]{3,1,0,2:T(8,128)S(1)} collective-permute-done((f32[3,289,3,512]{3,1,0,2:T(8,128)}, f32[3,289,3,512]{3,1,0,2:T(8,128)S(1)}, u32[]{:S(2)}, u32[]{:S(2)}) %collective-permute-start.4) | collective-permute-done | bytes 5326880 | tf_op jit(solution)/shard_map/ppermute | solution.py:12
  414.3 7.8 %fusion.9 = f32[3,289,3,512]{3,1,0,2:T(8,128)S(1)} fusion(f32[3,289,3,512]{3,1,0,2:T(8,128)} %collective-permute-done.5, f32[3,289,3,512]{3,1,0,2:T(8,128)} %copy-done.4, f32[3,289,3,3,512]{4,1,0,3,2:T(8,128)} %bitcast.153), kind=kLoop, calls=%fused_computation.18 | loop fusion | flops 2663424 | bytes 21307392 | tf_op jit(solution)/shard_map/add | solution.py:165
  429.0 6.2 %copy.54 = f32[3,289,1152]{1,2,0:T(8,128)} copy(f32[3,289,1152]{2,1,0:T(8,128)} %get-tuple-element.9) | data formatting | bytes 7990272 | tf_op jit(solution)/shard_map/slice | solution.py:158
  435.1 7.5 %fusion.62 = f32[3,289,512,1]{2,1,3,0:T(8,128)S(1)} fusion(f32[3,289,9,128]{1,3,2,0:T(8,128)} %bitcast.156, s32[9,128]{1,0:T(8,128)} %bitcast.169), kind=kOutput, calls=%fused_computation.59 | convolution fusion | flops 6137118720 | bytes 5775360 | tf_op jit(solution)/shard_map/xkob,obn->xkn/dot_general | solution.py:157
  442.7 4.8 %collective-permute-done.6 = f32[3,289,512]{2,1,0:T(8,128)} collective-permute-done((f32[3,289,512]{2,1,0:T(8,128)}, f32[3,289,512]{2,1,0:T(8,128)}, u32[]{:S(2)}, u32[]{:S(2)}) %collective-permute-start.6) | collective-permute-done | bytes 1775648 | tf_op jit(solution)/shard_map/ppermute | solution.py:12
  450.6 4.3 fusion.78
  (59 shorter events, 44.9 us)
Async XLA Ops:
  0.0 140.9 %copy-start = (bf16[16,289,289]{2,0,1:T(8,128)(2,1)S(1)}, bf16[16,289,289]{2,0,1:T(8,128)(2,1)}, u32[]{:S(2)}) copy-start(bf16[16,289,289]{2,0,1:T(8,128)(2,1)} %param.11) | copy-start | bytes 8018020
  0.0 25.0 %copy-start.11 = (s32[1,1,9,128]{3,1,2,0:T(1,128)S(1)}, s32[1,1,9,128]{3,1,2,0:T(1,128)}, u32[]{:S(2)}) copy-start(s32[1,1,9,128]{3,1,2,0:T(1,128)} %param.12) | copy-start | bytes 13828
  0.0 25.6 %copy-start.12 = (s32[1,1,9,128]{3,1,2,0:T(1,128)S(1)}, s32[1,1,9,128]{3,1,2,0:T(1,128)}, u32[]{:S(2)}) copy-start(s32[1,1,9,128]{3,1,2,0:T(1,128)} %param.13) | copy-start | bytes 13828
  0.0 26.2 %copy-start.13 = (s32[1,1,9]{2,1,0:T(1,128)S(1)}, s32[1,1,9]{2,1,0:T(1,128)}, u32[]{:S(2)}) copy-start(s32[1,1,9]{2,1,0:T(1,128)} %param.15) | copy-start | bytes 112
  0.0 14.2 %collective-permute-start = (bf16[3,289,1,1,512]{4,1,3,2,0:T(8,128)(2,1)}, bf16[3,289,1,1,512]{4,1,3,2,0:T(8,128)(2,1)S(1)}, u32[]{:S(2)}, u32[]{:S(2)}) collective-permute-start(bf16[3,289,1,1,512]{4,1,3,2,0:T(8,128)(2,1)} %param.8), channel_id=1, source_target_pairs={{0,16},{16,32},{32,48},{48,64},{64,80},{80,96},{96,112},{112,0},{1... | collective-permute-start | bytes 2663432 | tf_op jit(solution)/shard_map/ppermute | solution.py:21
  0.0 17.3 %collective-permute-start.1 = (bf16[3,289,1,1,512]{4,1,3,2,0:T(8,128)(2,1)}, bf16[3,289,1,1,512]{4,1,3,2,0:T(8,128)(2,1)S(1)}, u32[]{:S(2)}, u32[]{:S(2)}) collective-permute-start(bf16[3,289,1,1,512]{4,1,3,2,0:T(8,128)(2,1)} %param.8), channel_id=1, source_target_pairs={{16,0},{32,16},{48,32},{64,48},{80,64},{96,80},{112,96},{0,112},{1... | collective-permute-start | bytes 2663432 | tf_op jit(solution)/shard_map/ppermute | solution.py:24
  18.4 63.5 %collective-permute-start.3 = (bf16[3,289,3,1,512]{4,1,3,2,0:T(8,128)(2,1)}, bf16[3,289,3,1,512]{4,1,3,2,0:T(8,128)(2,1)}, u32[]{:S(2)}, u32[]{:S(2)}) collective-permute-start(bf16[3,289,3,1,512]{4,1,3,2,0:T(8,128)(2,1)} %constant_dynamic-update-slice_fusion), channel_id=1, source_target_pairs={{1,0},{2,1},{3,2},{4,3},{5,4},{6,5},{7,6},{8,7},{9,8},{10,9},{11,1... | collective-permute-start | bytes 7990280 | tf_op jit(solution)/shard_map/ppermute | solution.py:24
  25.0 62.4 %collective-permute-start.2 = (bf16[3,289,3,1,512]{4,1,3,2,0:T(8,128)(2,1)}, bf16[3,289,3,1,512]{4,1,3,2,0:T(8,128)(2,1)}, u32[]{:S(2)}, u32[]{:S(2)}) collective-permute-start(bf16[3,289,3,1,512]{4,1,3,2,0:T(8,128)(2,1)} %constant_dynamic-update-slice_fusion), channel_id=1, source_target_pairs={{0,1},{1,2},{2,3},{3,4},{4,5},{5,6},{6,7},{7,8},{8,9},{9,10},{10,1... | collective-permute-start | bytes 7990280 | tf_op jit(solution)/shard_map/ppermute | solution.py:21
  30.2 6.1 %copy-start.9 = (s32[1152]{0:T(1024)}, s32[1152]{0:T(1024)S(1)}, u32[]{:S(2)}) copy-start(s32[1152]{0:T(1024)S(1)} %convert_add_fusion) | copy-start | bytes 13828
  94.4 7.2 %copy-start.7 = (s32[1,1,9,128]{3,2,1,0:T(8,128)S(1)}, s32[1,1,9,128]{3,2,1,0:T(8,128)}, u32[]{:S(2)}) copy-start(s32[1,1,9,128]{3,2,1,0:T(8,128)} %copy.121) | copy-start | bytes 13828
  210.8 9.7 %copy-start.10 = (s32[1152]{0:T(1024)S(1)}, s32[1152]{0:T(1024)}, u32[]{:S(2)}) copy-start(s32[1152]{0:T(1024)} %copy-done.9) | copy-start | bytes 13828
  265.4 6.0 %copy-start.8 = (s32[1,1,9,128]{3,2,1,0:T(8,128)S(1)}, s32[1,1,9,128]{3,2,1,0:T(8,128)}, u32[]{:S(2)}) copy-start(s32[1,1,9,128]{3,2,1,0:T(8,128)} %copy.121) | copy-start | bytes 13828
  294.3 116.6 %collective-permute-start.4 = (f32[3,289,3,512]{3,1,0,2:T(8,128)}, f32[3,289,3,512]{3,1,0,2:T(8,128)S(1)}, u32[]{:S(2)}, u32[]{:S(2)}) collective-permute-start(f32[3,289,3,512]{3,1,0,2:T(8,128)} %get-tuple-element.7), channel_id=1, source_target_pairs={{1,0},{2,1},{3,2},{4,3},{5,4},{6,5},{7,6},{8,7},{9,8},{10,9},{11,1... | collective-permute-start | bytes 15980552 | tf_op jit(solution)/shard_map/ppermute | solution.py:12
  294.6 119.7 %collective-permute-start.5 = (f32[3,289,3,512]{3,1,0,2:T(8,128)S(1)}, f32[3,289,3,512]{3,1,0,2:T(8,128)}, u32[]{:S(2)}, u32[]{:S(2)}) collective-permute-start(f32[3,289,3,512]{3,1,0,2:T(8,128)S(1)} %get-tuple-element.8), channel_id=1, source_target_pairs={{15,0},{0,1},{1,2},{2,3},{3,4},{4,5},{5,6},{6,7},{7,8},{8,9},{9,10... | collective-permute-start | bytes 15980552 | tf_op jit(solution)/shard_map/ppermute | solution.py:12
  410.8 2.4 copy-start.4
  422.1 2.4 copy-start.2
  424.5 2.7 copy-start.5
  424.5 2.7 copy-start.6
  426.6 20.9 %collective-permute-start.6 = (f32[3,289,512]{2,1,0:T(8,128)}, f32[3,289,512]{2,1,0:T(8,128)}, u32[]{:S(2)}, u32[]{:S(2)}) collective-permute-start(f32[3,289,512]{2,1,0:T(8,128)} %get-tuple-element.13), channel_id=1, source_target_pairs={{16,0},{32,16},{48,32},{64,48},{80,64},{96,80},{112,96},{0,112},{1... | collective-permute-start | bytes 5326856 | tf_op jit(solution)/shard_map/ppermute | solution.py:12
  426.6 24.0 %collective-permute-start.7 = (f32[3,289,512]{2,1,0:T(8,128)}, f32[3,289,512]{2,1,0:T(8,128)}, u32[]{:S(2)}, u32[]{:S(2)}) collective-permute-start(f32[3,289,512]{2,1,0:T(8,128)} %get-tuple-element.14), channel_id=1, source_target_pairs={{112,0},{0,16},{16,32},{32,48},{48,64},{64,80},{80,96},{96,112},{1... | collective-permute-start | bytes 5326856 | tf_op jit(solution)/shard_map/ppermute | solution.py:12
  435.1 15.5 %copy-start.3 = (f32[3,512,289]{1,2,0:T(8,128)S(1)}, f32[3,512,289]{1,2,0:T(8,128)}, u32[]{:S(2)}) copy-start(f32[3,512,289]{1,2,0:T(8,128)} %fusion.80) | copy-start | bytes 5326852
  435.1 19.7 %copy-start.1 = (bf16[16,289,289]{2,0,1:T(8,128)(2,1)S(1)}, bf16[16,289,289]{2,0,1:T(8,128)(2,1)}, u32[]{:S(2)}) copy-start(bf16[16,289,289]{2,0,1:T(8,128)(2,1)} %param.11) | copy-start | bytes 8018020
where the time goes:
time: 462 us; the launch traced here: 455 us
  waiting for transfers between devices  172 us (37%)
  matrix products  136 us (29%)
  local copies, waits for them, and re-layouts  112 us (24%)
  other arithmetic  21.8 us (5%)
  starting transfers between devices  12.1 us (3%)
    ppermute x4, waiting for transfers between devices, from_behind(): return lax.ppermute(block, axis, route)  124 us
    dot_general x1, matrix products, to_slots(): jnp.einsum('xkg,sg->xks', group_values, table, precision=lax.Precision.HI...  41.3 us
    ppermute x2, waiting for transfers between devices, with_halo(): lax.ppermute(lax.slice_in_dim(block, 0, width, axis=dim), axis, backward)  32.2 us
    reshape x2, local copies, waits for them, and re-layouts, pair_chain(): return back.reshape(back.shape[0], back.shape[1], -1)  19.3 us
    dot_general x2, matrix products, pair_chain(): jnp.einsum('rlk,rcln->ckrn', rotations, toward, preferred_element_type=jn...  17.8 us
    ppermute x2, waiting for transfers between devices, with_halo(): lax.ppermute(lax.slice_in_dim(block, block.shape[dim] - width, None, axis...  16.7 us
    dot_general x1, matrix products, local(): jnp.einsum('xkob,obn->xkon', slot_terms[3:], partner_onehot, precision=la...  14.9 us
    mul x2, local copies, waits for them, and re-layouts, pair_chain(): jnp.einsum('rlk,rcln->ckrn', rotations, toward, preferred_element_type=jn...  14 us
  transfers between devices with their start and end apart: 8, of which 7 were waited for; matrix products, arithmetic and copies ran while one was open for 10% of the time, Pallas kernels for 0%

commit v1 on v0

v1 whole, which is shorter than its diff:
```python
import functools

import jax
import jax.numpy as jnp
from jax import lax
from jax.experimental import pallas as pl
from jax.experimental.pallas import tpu as pltpu
from jax.sharding import PartitionSpec as P

BF = jnp.bfloat16
F32 = jnp.float32

K = 289
MAIN = 256
REST = K - MAIN
TAIL = 128
WIDE = 3 * MAIN + TAIL
CELLS = 512
SLOTS = 128
NR = 16
CAP = 16
PAIR = 2 * SLOTS
GROUP = 2 * CAP
ROWS = NR * GROUP
OWN, PARTNER, ROT, META = 0, 9, 18, 32
VMEM_LIMIT = 48 * 1024 * 1024


def nt(a, b):
    return lax.dot_general(a, b, (((1,), (1,)), ((), ())), preferred_element_type=F32)


def nn(a, b):
    return jnp.dot(a, b, preferred_element_type=F32)


def iota(shape, dim):
    return lax.broadcasted_iota(jnp.int32, shape, dim)


def where_one(condition):
    return jnp.where(condition, 1.0, 0.0).astype(BF)


def eye(size):
    return where_one(iota((size, size), 0) == iota((size, size), 1))


def spread(c):
    return where_one(iota((TAIL, REST), 0) == iota((TAIL, REST), 1) + c * REST)


def offset_of(dx, dy):
    return (dx + 1) * 3 + dy + 1


def parity_lanes(width, start):
    k = iota((1, width), 1) + start
    degree = jnp.zeros((1, width), jnp.int32)
    for level in range(1, 17):
        degree = degree + jnp.where(k >= level * level, 1, 0)
    return 1.0 - 2.0 * (degree % 2).astype(F32)


def side_signs(width, start):
    signs = jnp.broadcast_to(parity_lanes(width, start), (GROUP, width))
    return jnp.where(iota((GROUP, width), 0) >= CAP, signs, 1.0)


def pick_table(own_side, partner_side):
    cells = iota((CELLS, SLOTS), 0)
    return jnp.concatenate([where_one(cells == own_side), where_one(cells == partner_side)], axis=1)


def tail_of(parts):
    total = None
    for c, part in enumerate(parts):
        term = nn(spread(c), part)
        total = term if total is None else total + term
    return total.astype(BF)


def positions(rots):
    marks = [where_one(iota((NR, SLOTS), 0) == rot) for rot in rots]
    earlier = where_one(iota((SLOTS, SLOTS), 0) < iota((SLOTS, SLOTS), 1))
    ranks = nn(jnp.concatenate(marks, axis=0), earlier)
    places = []
    for j, mark in enumerate(marks):
        base = (iota((NR, SLOTS), 0) * GROUP + (j % 2) * CAP + 1).astype(F32)
        values = mark.astype(F32) * (ranks[j * NR : (j + 1) * NR] + base)
        places.append(jnp.sum(values, axis=0, keepdims=True).astype(jnp.int32) - 1)
    return places


def apply_dense(mains, tail, main_ref, to_tail_ref, from_tail_ref, tail_ref):
    size = mains[0].shape[0]
    middle = nt(jnp.concatenate(mains, axis=0), main_ref[:MAIN, :MAIN])
    out_tail = nt(tail, tail_ref[...])
    outs = []
    for c in range(3):
        outs.append(middle[c * size : (c + 1) * size] + nt(tail, from_tail_ref[c]))
        out_tail = out_tail + nt(mains[c], to_tail_ref[c])
    return outs, out_tail


def split_lanes(block):
    return [block[:, c * MAIN : (c + 1) * MAIN] for c in range(3)], block[:, 3 * MAIN :]


def prep_kernel(rot_ref, trans_ref, self_ref, rot_tail, *pieces):
    fold = where_one((iota((TAIL, REST), 0) % REST == iota((TAIL, REST), 1)) & (iota((TAIL, REST), 0) < 3 * REST))
    same = (iota((TAIL, TAIL), 0) // REST) == (iota((TAIL, TAIL), 1) // REST)

    def tail_block(block):
        return jnp.where(same, nt(nn(fold, block).astype(BF), fold), 0.0).astype(BF)

    for r in range(NR):
        rot_tail[r] = tail_block(rot_ref[r, MAIN:, MAIN:])
    for source, (to_tail, from_tail, tail) in ((trans_ref, pieces[:3]), (self_ref, pieces[3:])):
        for c in range(3):
            to_tail[c] = nn(spread(c), source[MAIN:, :MAIN]).astype(BF)
            from_tail[c] = nt(source[:MAIN, MAIN:], spread(c)).astype(BF)
        tail[...] = tail_block(source[MAIN:, MAIN:])


def pick_kernel(rows, count, *refs):
    sources, meta, left, right = refs[:count], refs[count], refs[count + 1], refs[count + 2]
    to_left, to_right = refs[count + 3 :]
    for i, (source, dy) in enumerate(zip(sources, rows)):
        for ex, target, out in ((-1, left, to_left), (1, right, to_right)):
            o = offset_of(-ex, dy)
            table = pick_table(
                target[1, PARTNER + o : PARTNER + o + 1, :], meta[dy + 1, OWN + 8 - o : OWN + 9 - o, :]
            )
            for c in range(3):
                out[i, c] = nn(source[c], table).astype(BF)


def phase_kernel(sources, whole, first, last, *refs):
    m = len(sources)
    arrays = refs[: (m if last is False else 2)]
    refs = refs[len(arrays) :]
    meta, left, right, rot_ref, rot_tail, trans_ref, t1, t2, t3 = refs[:9]
    refs = refs[9:]
    if first:
        self_ref, s1, s2, s3 = refs[:4]
        refs = refs[4:]
    else:
        acc_in = refs[0]
        refs = refs[1:]
    out, picked, grouped, turned, places_to = refs[:5]
    acc = refs[5] if last else out

    def meta_row(dx, dy, row):
        return (left, meta, right)[dx + 1][dy + 1, row : row + 1, :]

    def slot_rows(dx, dy, mine, theirs):
        o = offset_of(dx, dy)
        return meta_row(0, 0, mine + o), meta_row(dx, dy, theirs + 8 - o)

    if first:
        unit = eye(CELLS)
        here = arrays[0]
        mains = [nt(unit, here[c, :MAIN, :]).astype(BF) for c in range(3)]
        tail = nt(unit, tail_of([here[c, MAIN:, :] for c in range(3)])).astype(BF)
        outs, out_tail = apply_dense(mains, tail, self_ref, s1, s2, s3)
        for c in range(3):
            acc[:, c * MAIN : (c + 1) * MAIN] = outs[c]
        acc[:, 3 * MAIN :] = out_tail

    rots = []
    for dx, dy in sources:
        rots.extend(slot_rows(dx, dy, ROT, ROT))
    places = positions(rots)

    for s, (dx, dy) in enumerate(sources):
        if s < whole:
            table = pick_table(*slot_rows(dx, dy, PARTNER, OWN))
            for c in range(3):
                picked[c] = nn(arrays[s][c], table).astype(BF)
            taken = [picked[c] for c in range(3)]
        elif last:
            side, which = arrays[0 if dx < 0 else 1], (0 if dy < 0 else 1)
            taken = [side[which, c] for c in range(3)]
        else:
            taken = [arrays[s][0, c] for c in range(3)]
        row_ids = iota((ROWS, SLOTS), 0)
        own_place, partner_place = places[2 * s], places[2 * s + 1]
        place = jnp.concatenate([where_one(row_ids == own_place), where_one(row_ids == partner_place)], axis=1)
        lanes = slice(s * GROUP, (s + 1) * GROUP)
        for c in range(3):
            grouped[:, lanes, c * MAIN : (c + 1) * MAIN] = (
                nt(place, taken[c][:MAIN]).astype(BF).reshape(NR, GROUP, MAIN)
            )
        grouped[:, lanes, 3 * MAIN :] = (
            nt(place, tail_of([t[MAIN:] for t in taken])).astype(BF).reshape(NR, GROUP, TAIL)
        )
        own_to, partner_to = slot_rows(dx, dy, OWN, PARTNER)
        to = jnp.concatenate([own_to, partner_to], axis=1) + 1
        digits = jnp.concatenate([to // 32, to % 32, jnp.zeros((6, PAIR), jnp.int32)], axis=0)
        back = nt(digits.astype(F32).astype(BF), place)
        goal = (back[0:1] * 32.0 + back[1:2]).astype(jnp.int32) - 1
        places_to[:, s * ROWS : (s + 1) * ROWS] = where_one(iota((CELLS, ROWS), 0) == goal)

    size = m * GROUP
    main_signs = side_signs(MAIN, 0)
    tail_signs = side_signs(TAIL, MAIN)

    def turn(r, source, target, dot):
        block = source[r]
        mains, tail = split_lanes(block)
        turned_main = dot(jnp.concatenate(mains, axis=0), rot_ref[r, :MAIN, :MAIN])
        turned_main = (turned_main.reshape(3 * m, GROUP, MAIN) * main_signs[None]).reshape(3 * size, MAIN)
        for c in range(3):
            target[r, :, c * MAIN : (c + 1) * MAIN] = turned_main[c * size : (c + 1) * size].astype(BF)
        target[r, :, 3 * MAIN :] = dot(tail, rot_tail[r]).astype(BF)

    for r in range(NR):
        turn(r, grouped, turned, nt)

    step = 4

    def translate(i, carry):
        block = turned[pl.ds(i * step, step)].reshape(step * size, WIDE)
        mains, tail = split_lanes(block)
        outs, out_tail = apply_dense(mains, tail, trans_ref, t1, t2, t3)
        for c in range(3):
            grouped[pl.ds(i * step, step), :, c * MAIN : (c + 1) * MAIN] = (
                outs[c].astype(BF).reshape(step, size, MAIN)
            )
        grouped[pl.ds(i * step, step), :, 3 * MAIN :] = out_tail.astype(BF).reshape(step, size, TAIL)
        return carry

    lax.fori_loop(0, NR // step, translate, 0)

    for r in range(NR):
        turn(r, grouped, turned, nn)

    columns = [slice(c * MAIN, (c + 1) * MAIN) for c in range(3)] + [slice(3 * MAIN, WIDE)]
    for lanes in columns:
        total = acc[:, lanes] if first else acc_in[:, lanes]
        for s in range(m):
            back = turned[:, s * GROUP : (s + 1) * GROUP, lanes].reshape(ROWS, lanes.stop - lanes.start)
            total = total + nn(places_to[:, s * ROWS : (s + 1) * ROWS], back)
        acc[:, lanes] = total

    if last:
        unit = eye(MAIN)
        tail = acc[:, 3 * MAIN :].astype(BF)
        for c in range(3):
            out[c, :MAIN, :] = nt(unit, acc[:, c * MAIN : (c + 1) * MAIN].astype(BF)).astype(BF)
            gather = where_one(iota((REST, TAIL), 1) == iota((REST, TAIL), 0) + c * REST)
            out[c, MAIN:, :] = nt(gather, tail).astype(BF)


def vmem_call(kernel, out_shape, scratch=(), flops=0):
    return pl.pallas_call(
        kernel,
        out_shape=out_shape,
        scratch_shapes=list(scratch),
        compiler_params=pltpu.CompilerParams(vmem_limit_bytes=VMEM_LIMIT),
        cost_estimate=pl.CostEstimate(flops=flops, bytes_accessed=8_000_000, transcendentals=0),
    )


def phase_call(sources, whole, first, last):
    m = len(sources)
    if last:
        out = jax.ShapeDtypeStruct((3, K, CELLS), BF)
    else:
        out = jax.ShapeDtypeStruct((CELLS, WIDE), F32)
    scratch = [
        pltpu.VMEM((3, K, PAIR), BF),
        pltpu.VMEM((NR, m * GROUP, WIDE), BF),
        pltpu.VMEM((NR, m * GROUP, WIDE), BF),
        pltpu.VMEM((CELLS, m * ROWS), BF),
    ]
    if last:
        scratch.append(pltpu.VMEM((CELLS, WIDE), F32))
    kernel = functools.partial(phase_kernel, sources, whole, first, last)
    return vmem_call(kernel, out, scratch, flops=m * 4_000_000_000)


def shift(block, axis, distance):
    count = lax.axis_size(axis)
    return lax.ppermute(block, axis, [((i - distance) % count, i) for i in range(count)])


def local(traction, self_operator, translation, rotations, own_cell, partner_cell, rot_index, block_count):
    here = traction.reshape(3, K, CELLS)
    live = iota((9, SLOTS), 1) < block_count.reshape(9, 1)
    rot = jnp.where(live, rot_index.reshape(9, SLOTS), NR)
    meta = jnp.concatenate(
        [own_cell.reshape(9, SLOTS), partner_cell.reshape(9, SLOTS), rot, jnp.zeros((META - 27, SLOTS), jnp.int32)]
    )
    meta_low, meta_high = shift(meta, "gy", 1), shift(meta, "gy", -1)
    low, high = shift(here, "gy", 1), shift(here, "gy", -1)
    meta = jnp.stack([meta_low, meta, meta_high])
    left, right = shift(meta, "gx", 1), shift(meta, "gx", -1)
    metas = (meta, left, right)

    picked = jax.ShapeDtypeStruct((1, 3, K, PAIR), BF)
    to_left, to_right = vmem_call(
        functools.partial(pick_kernel, (0,), 1), (picked, picked), flops=1_000_000_000
    )(here, *metas)
    from_left, from_right = shift(to_right, "gx", 1), shift(to_left, "gx", -1)

    dense = [
        jax.ShapeDtypeStruct((3, TAIL, MAIN), BF),
        jax.ShapeDtypeStruct((3, MAIN, TAIL), BF),
        jax.ShapeDtypeStruct((TAIL, TAIL), BF),
    ]
    rot_tail, t1, t2, t3, s1, s2, s3 = vmem_call(
        prep_kernel, [jax.ShapeDtypeStruct((NR, TAIL, TAIL), BF)] + dense + dense, flops=100_000_000
    )(rotations, translation, self_operator)
    weights = (rotations, rot_tail, translation, t1, t2, t3)

    acc = phase_call(((0, 0), (-1, 0), (1, 0)), 1, True, False)(
        here, from_left, from_right, *metas, *weights, self_operator, s1, s2, s3
    )

    picked = jax.ShapeDtypeStruct((2, 3, K, PAIR), BF)
    to_left, to_right = vmem_call(
        functools.partial(pick_kernel, (-1, 1), 2), (picked, picked), flops=2_000_000_000
    )(low, high, *metas)
    from_left, from_right = shift(to_right, "gx", 1), shift(to_left, "gx", -1)

    acc = phase_call(((0, -1), (0, 1)), 2, False, False)(low, high, *metas, *weights, acc)
    velocity = phase_call(((-1, -1), (-1, 1), (1, -1), (1, 1)), 0, False, True)(
        from_left, from_right, *metas, *weights, acc
    )
    return velocity.reshape(3, K, 1, 1, CELLS)


def solution(mesh):
    return jax.shard_map(
        local,
        mesh=mesh,
        in_specs=(
            P(None, None, "gx", "gy", None),
            P(),
            P(),
            P(),
            P("gx", "gy", None, None),
            P("gx", "gy", None, None),
            P("gx", "gy", None, None, None),
            P("gx", "gy", None),
        ),
        out_specs=P(None, None, "gx", "gy", None),
        check_vma=False,
    )
```

time: 462 us -> 83.4 us (0.18); the launches traced: 455 us -> 83.1 us
  waiting for transfers between devices: 172 us -> 15.5 us
  matrix products: 136 us -> 0 us
  local copies, waits for them, and re-layouts: 112 us -> 5.66 us
  Pallas kernels: 0 us -> 40.1 us
  other arithmetic: 21.8 us -> 0.91 us
  starting transfers between devices: 12.1 us -> 20.9 us
    ppermute x8 -> x10, waiting for transfers between devices: 172 us -> 15.5 us  [shift(): lax.ppermute(block, axis, [((i - distance) % count, i) for i in range(cou...]
    dot_general x13 -> x0, matrix products: 136 us -> none  [the longest x1 41.3 us: to_slots(): jnp.einsum('xkg,sg->xks', group_values, table, precision=lax.Precision.HI...]
    pallas_call x0 -> x6, Pallas kernels: none -> 40.1 us  [the longest x1 14.6 us: local(): phase_call(((-1, -1), (-1, 1), (1, -1), (1, 1)), 0, False, True)]
    slice x6 -> x0, local copies, waits for them, and re-layouts: 32.9 us -> none  [the longest x2 10.3 us: local(): both_groups[:3]]
    reshape x4 -> x0, local copies, waits for them, and re-layouts: 27.8 us -> none  [the longest x2 19.3 us: pair_chain(): return back.reshape(back.shape[0], back.shape[1], -1)]
    mul x2 -> x0, local copies, waits for them, and re-layouts: 14 us -> none  [pair_chain(): jnp.einsum('rlk,rcln->ckrn', rotations, toward, preferred_element_type=jn...]
    squeeze x2 -> x0, local copies, waits for them, and re-layouts: 10 us -> none  [the longest x1 7.9 us: local(): outgoing[:, :, :, 0]]
    convert_element_type x3 -> x0, local copies, waits for them, and re-layouts: 9.25 us -> none  [the longest x1 4.41 us: local(): own_slots = jnp.einsum('xkn,obn->xkob', own_here, own_onehot.astype(jnp.b...]
  transfers between devices with their start and end apart: 8 -> 10, of which waited for: 7 -> 2; matrix products, arithmetic and copies ran while one was open for 10% -> 5% of each run, Pallas kernels for 0% -> 31%
where the time goes in v1:
time: 83.4 us; the launch traced here: 83.1 us
  Pallas kernels  40.1 us (48%)
  starting transfers between devices  20.9 us (25%)
  waiting for transfers between devices  15.5 us (19%)
  local copies, waits for them, and re-layouts  5.66 us (7%)
  other arithmetic  0.91 us (1%)
    ppermute x10, starting transfers between devices, shift(): lax.ppermute(block, axis, [((i - distance) % count, i) for i in range(cou...  20.9 us
    ppermute x10, waiting for transfers between devices, shift(): lax.ppermute(block, axis, [((i - distance) % count, i) for i in range(cou...  15.5 us
    pallas_call x1, Pallas kernels, local(): phase_call(((-1, -1), (-1, 1), (1, -1), (1, 1)), 0, False, True)  14.6 us
    pallas_call x1, Pallas kernels, local(): phase_call(((0, 0), (-1, 0), (1, 0)), 1, True, False)  12.3 us
    pallas_call x1, Pallas kernels, local(): phase_call(((0, -1), (0, 1)), 2, False, False)  9.74 us
    unnamed x16, local copies, waits for them, and re-layouts  3.95 us
  transfers between devices with their start and end apart: 10, of which 2 were waited for; matrix products, arithmetic and copies ran while one was open for 5% of the time, Pallas kernels for 31%

profile of v1, /device:TPU:0, one launch (start us, length us, event | category | flops | bytes accessed | tf_op | source)
XLA Modules:
  0.0 83.1 jit_solution(6651687421631758760)
XLA Ops:
  0.0 1.7 %collective-permute-start = (bf16[3,289,512]{2,1,0:T(8,128)(2,1)}, bf16[3,289,512]{2,1,0:T(8,128)(2,1)S(1)}, u32[]{:S(2)}, u32[]{:S(2)}) collective-permute-start(bf16[3,289,512]{2,1,0:T(8,128)(2,1)} %bitcast.15), channel_id=1, source_target_pairs={{15,0},{0,1},{1,2},{2,3},{3,4},{4,5},{5,6},{6,7},{7,8},{8,9},{9,10... | collective-permute-start | bytes 2663432 | tf_op jit(solution)/shard_map/ppermute | solution.py:286
  1.7 4.9 %collective-permute-start.1 = (bf16[3,289,512]{2,1,0:T(8,128)(2,1)}, bf16[3,289,512]{2,1,0:T(8,128)(2,1)S(1)}, u32[]{:S(2)}, u32[]{:S(2)}) collective-permute-start(bf16[3,289,512]{2,1,0:T(8,128)(2,1)} %bitcast.16), channel_id=1, source_target_pairs={{1,0},{2,1},{3,2},{4,3},{5,4},{6,5},{7,6},{8,7},{9,8},{10,9},{11,1... | collective-permute-start | bytes 2663432 | tf_op jit(solution)/shard_map/ppermute | solution.py:286
  6.6 0.1 pad.6.clone
  6.7 0.7 copy_bitcast_fusion
  7.4 0.8 bitcast_select_fusion
  8.1 0.1 add_add_fusion
  8.2 0.0 collective-permute-start.2
  8.2 5.3 %collective-permute-start.3 = (s32[32,128]{1,0:T(8,128)S(1)}, s32[32,128]{1,0:T(8,128)S(1)}, u32[]{:S(2)}, u32[]{:S(2)}) collective-permute-start(s32[32,128]{1,0:T(8,128)S(1)} %add_add_fusion), channel_id=1, source_target_pairs={{1,0},{2,1},{3,2},{4,3},{5,4},{6,5},{7,6},{8,7},{9,8},{10,9},{11,1... | collective-permute-start | bytes 49160 | tf_op jit(solution)/shard_map/ppermute | solution.py:286
  13.6 0.1 fusion
  13.6 13.7 %collective-permute-done.2 = s32[32,128]{1,0:T(8,128)S(1)} collective-permute-done((s32[32,128]{1,0:T(8,128)S(1)}, s32[32,128]{1,0:T(8,128)S(1)}, u32[]{:S(2)}, u32[]{:S(2)}) %collective-permute-start.2) | collective-permute-done | bytes 16416 | tf_op jit(solution)/shard_map/ppermute | solution.py:286
  27.3 0.0 collective-permute-start.4
  27.3 2.9 %collective-permute-start.5 = (s32[3,32,128]{2,1,0:T(8,128)S(1)}, s32[3,32,128]{2,1,0:T(8,128)S(1)}, u32[]{:S(2)}, u32[]{:S(2)}) collective-permute-start(s32[3,32,128]{2,1,0:T(8,128)S(1)} %pad_add_fusion.refs_2_.refs_1_.refs_3_), channel_id=1, source_target_pairs={{16,0},{32,16},{48,32},{64,48},{80,64},{96,80},{112,96},{0,112},{1... | collective-permute-start | bytes 147464 | tf_op jit(solution)/shard_map/ppermute | solution.py:286
  30.3 1.8 %collective-permute-done.4.refs_3_.refs_2_.refs_4_ = s32[3,32,128]{2,1,0:T(8,128)S(1)} collective-permute-done((s32[3,32,128]{2,1,0:T(8,128)S(1)}, s32[3,32,128]{2,1,0:T(8,128)S(1)}, u32[]{:S(2)}, u32[]{:S(2)}) %collective-permute-start.4) | collective-permute-done | bytes 49184 | tf_op jit(solution)/shard_map/ppermute | solution.py:286
  32.1 0.0 collective-permute-done.5.refs_4_.refs_3_.refs_5_
  32.1 1.2 %copy-done.3 = bf16[3,289,1,1,512]{4,1,3,2,0:T(8,128)(2,1)S(1)} copy-done((bf16[3,289,1,1,512]{4,1,3,2,0:T(8,128)(2,1)S(1)}, bf16[3,289,1,1,512]{4,1,3,2,0:T(8,128)(2,1)}, u32[]{:S(2)}) %copy-start.3) | copy-done | bytes 887832
  33.2 0.7 shard_map.84
  33.9 0.4 collective-permute-start.8
  34.3 2.6 %collective-permute-start.9 = (bf16[1,3,289,256]{3,2,1,0:T(8,128)(2,1)S(1)}, bf16[1,3,289,256]{3,2,1,0:T(8,128)(2,1)S(1)}, u32[]{:S(2)}, u32[]{:S(2)}) collective-permute-start(bf16[1,3,289,256]{3,2,1,0:T(8,128)(2,1)S(1)} %get-tuple-element.23), channel_id=1, source_target_pairs={{16,0},{32,16},{48,32},{64,48},{80,64},{96,80},{112,96},{0,112},{1... | collective-permute-start | bytes 1331720 | tf_op jit(solution)/shard_map/ppermute | solution.py:286
  36.9 0.8 copy.21.rot_ref.refs_6_.refs_5_
  37.7 1.6 %shard_map.83 = (bf16[16,128,128]{2,1,0:T(8,128)(2,1)S(1)}, bf16[3,128,256]{2,1,0:T(8,128)(2,1)S(1)}, bf16[3,256,128]{2,1,0:T(8,128)(2,1)S(1)}, bf16[128,128]{1,...) custom-call(bf16[16,289,289]{2,1,0:T(8,128)(2,1)S(1)} %copy.21.rot_r, ...), custom_call_target="tpu_custom_call" | custom-call | flops 100000000 | bytes 8000000 | tf_op jit(solution)/shard_map/pallas_call | solution.py:313
  39.3 1.1 %shard_map.82 = (bf16[2,3,289,256]{3,2,1,0:T(8,128)(2,1)S(1)}, bf16[2,3,289,256]{3,2,1,0:T(8,128)(2,1)S(1)}) custom-call(bf16[3,289,512]{2,1,0:T(8,128)(2,1)S(1)} %collective-permute-done.refs_0_, bf16[3,289,512]{2,1,0:T(8,128)(2,1)S(1)} %collective-permute-done.1.refs_1_, s32[3,32,128]{2,1,0:T(8,128)S(1)} %pad_add_fusion.refs_2_.refs_1_.refs_3_, ...), custom_call_target="tpu_custom_call" | custom-call | flops 2000000000 | bytes 8000000 | tf_op jit(solution)/shard_map/pallas_call | solution.py:323
  40.5 0.0 copy-start.4
  40.5 0.7 copy.14
  41.2 0.0 collective-permute-start.6
  41.2 0.7 copy.15
  41.9 2.9 %collective-permute-start.7 = (bf16[2,3,289,256]{3,0,2,1:T(2,128)(2,1)S(1)}, bf16[2,3,289,256]{3,0,2,1:T(2,128)(2,1)S(1)}, u32[]{:S(2)}, u32[]{:S(2)}) collective-permute-start(bf16[2,3,289,256]{3,0,2,1:T(2,128)(2,1)S(1)} %copy.15), channel_id=1, source_target_pairs={{16,0},{32,16},{48,32},{64,48},{80,64},{96,80},{112,96},{0,112},{1... | collective-permute-start | bytes 2663432 | tf_op jit(solution)/shard_map/ppermute | solution.py:286
  44.9 12.3 %shard_map.85.refs_11_ = f32[512,896]{1,0:T(8,128)S(1)} custom-call(bf16[3,289,512]{2,1,0:T(8,128)(2,1)S(1)} %bitcast.18, bf16[1,3,289,256]{3,2,1,0:T(8,128)(2,1)S(1)} %collective-permute-done.8.refs_1_, bf16[1,3,289,256]{3,2,1,0:T(8,128)(2,1)S(1)} %collective-permute-done.9.refs_2_, s32[3,32,128]{2,1,0:T(8,128)S(1)} %pad_add_fusion.refs_2_.refs_1_.refs_3_, ...), custom_call_target="tpu_custom_call" | custom-call | flops 12000000000 | bytes 8000000 | tf_op jit(solution)/shard_map/pallas_call | solution.py:318
  57.2 1.3 %copy-done.5 = f32[512,896]{1,0:T(8,128)} copy-done((f32[512,896]{1,0:T(8,128)}, f32[512,896]{1,0:T(8,128)S(1)}, u32[]{:S(2)}) %copy-start.5) | copy-done | bytes 1835032
  58.5 9.7 %shard_map.86.refs_11_ = f32[512,896]{1,0:T(8,128)S(1)} custom-call(bf16[3,289,512]{2,1,0:T(8,128)(2,1)S(1)} %collective-permute-done.refs_0_, bf16[3,289,512]{2,1,0:T(8,128)(2,1)S(1)} %collective-permute-done.1.refs_1_, s32[3,32,128]{2,1,0:T(8,128)S(1)} %pad_add_fusion.refs_2_.refs_1_.refs_3_, ...), custom_call_target="tpu_custom_call" | custom-call | flops 8000000000 | bytes 8000000 | tf_op jit(solution)/shard_map/pallas_call | solution.py:328
  68.3 0.1 copy.19.refs_0_
  68.4 0.1 copy.20.refs_1_
  68.5 14.6 %shard_map.87 = bf16[3,289,512]{2,1,0:T(8,128)(2,1)} custom-call(bf16[2,3,289,256]{3,2,1,0:T(8,128)(2,1)S(1)} %copy.19.refs_0_, bf16[2,3,289,256]{3,2,1,0:T(8,128)(2,1)S(1)} %copy.20.refs_1_, s32[3,32,128]{2,1,0:T(8,128)S(1)} %pad_add_fusion.refs_2_.refs_1_.refs_3_, s32[3,32,128]{2,1,0:T(8,128)S(1)} %collective-permute-done.4.refs_3_.refs_2_.refs_4_, ...), custom_call_target="tpu_custom_call" | custom-call | flops 16000000000 | bytes 8000000 | tf_op jit(solution)/shard_map/pallas_call | solution.py:329
  (20 shorter events, 0.0 us)
Async XLA Ops:
  0.0 39.3 %collective-permute-start = (bf16[3,289,512]{2,1,0:T(8,128)(2,1)}, bf16[3,289,512]{2,1,0:T(8,128)(2,1)S(1)}, u32[]{:S(2)}, u32[]{:S(2)}) collective-permute-start(bf16[3,289,512]{2,1,0:T(8,128)(2,1)} %bitcast.15), channel_id=1, source_target_pairs={{15,0},{0,1},{1,2},{2,3},{3,4},{4,5},{5,6},{6,7},{7,8},{8,9},{9,10... | collective-permute-start | bytes 2663432 | tf_op jit(solution)/shard_map/ppermute | solution.py:286
  1.7 37.7 %collective-permute-start.1 = (bf16[3,289,512]{2,1,0:T(8,128)(2,1)}, bf16[3,289,512]{2,1,0:T(8,128)(2,1)S(1)}, u32[]{:S(2)}, u32[]{:S(2)}) collective-permute-start(bf16[3,289,512]{2,1,0:T(8,128)(2,1)} %bitcast.16), channel_id=1, source_target_pairs={{1,0},{2,1},{3,2},{4,3},{5,4},{6,5},{7,6},{8,7},{9,8},{10,9},{11,1... | collective-permute-start | bytes 2663432 | tf_op jit(solution)/shard_map/ppermute | solution.py:286
  8.2 19.1 %collective-permute-start.2 = (s32[32,128]{1,0:T(8,128)S(1)}, s32[32,128]{1,0:T(8,128)S(1)}, u32[]{:S(2)}, u32[]{:S(2)}) collective-permute-start(s32[32,128]{1,0:T(8,128)S(1)} %add_add_fusion), channel_id=1, source_target_pairs={{15,0},{0,1},{1,2},{2,3},{3,4},{4,5},{5,6},{6,7},{7,8},{8,9},{9,10... | collective-permute-start | bytes 49160 | tf_op jit(solution)/shard_map/ppermute | solution.py:286
  8.2 19.1 %collective-permute-start.3 = (s32[32,128]{1,0:T(8,128)S(1)}, s32[32,128]{1,0:T(8,128)S(1)}, u32[]{:S(2)}, u32[]{:S(2)}) collective-permute-start(s32[32,128]{1,0:T(8,128)S(1)} %add_add_fusion), channel_id=1, source_target_pairs={{1,0},{2,1},{3,2},{4,3},{5,4},{6,5},{7,6},{8,7},{9,8},{10,9},{11,1... | collective-permute-start | bytes 49160 | tf_op jit(solution)/shard_map/ppermute | solution.py:286
  27.3 4.7 %collective-permute-start.4 = (s32[3,32,128]{2,1,0:T(8,128)S(1)}, s32[3,32,128]{2,1,0:T(8,128)S(1)}, u32[]{:S(2)}, u32[]{:S(2)}) collective-permute-start(s32[3,32,128]{2,1,0:T(8,128)S(1)} %pad_add_fusion.refs_2_.refs_1_.refs_3_), channel_id=1, source_target_pairs={{112,0},{0,16},{16,32},{32,48},{48,64},{64,80},{80,96},{96,112},{1... | collective-permute-start | bytes 147464 | tf_op jit(solution)/shard_map/ppermute | solution.py:286
  27.3 4.7 %collective-permute-start.5 = (s32[3,32,128]{2,1,0:T(8,128)S(1)}, s32[3,32,128]{2,1,0:T(8,128)S(1)}, u32[]{:S(2)}, u32[]{:S(2)}) collective-permute-start(s32[3,32,128]{2,1,0:T(8,128)S(1)} %pad_add_fusion.refs_2_.refs_1_.refs_3_), channel_id=1, source_target_pairs={{16,0},{32,16},{48,32},{64,48},{80,64},{96,80},{112,96},{0,112},{1... | collective-permute-start | bytes 147464 | tf_op jit(solution)/shard_map/ppermute | solution.py:286
  32.1 1.2 %copy-start.3 = (bf16[3,289,1,1,512]{4,1,3,2,0:T(8,128)(2,1)S(1)}, bf16[3,289,1,1,512]{4,1,3,2,0:T(8,128)(2,1)}, u32[]{:S(2)}) copy-start(bf16[3,289,1,1,512]{4,1,3,2,0:T(8,128)(2,1)} %param.8) | copy-start | bytes 2663428
  33.2 3.7 %copy-start.6 = (bf16[16,289,289]{2,0,1:T(8,128)(2,1)S(1)}, bf16[16,289,289]{2,0,1:T(8,128)(2,1)}, u32[]{:S(2)}) copy-start(bf16[16,289,289]{2,0,1:T(8,128)(2,1)} %param.11) | copy-start | bytes 8018020
  33.9 11.0 %collective-permute-start.8 = (bf16[1,3,289,256]{3,2,1,0:T(8,128)(2,1)S(1)}, bf16[1,3,289,256]{3,2,1,0:T(8,128)(2,1)S(1)}, u32[]{:S(2)}, u32[]{:S(2)}) collective-permute-start(bf16[1,3,289,256]{3,2,1,0:T(8,128)(2,1)S(1)} %get-tuple-element.22), channel_id=1, source_target_pairs={{112,0},{0,16},{16,32},{32,48},{48,64},{64,80},{80,96},{96,112},{1... | collective-permute-start | bytes 1331720 | tf_op jit(solution)/shard_map/ppermute | solution.py:286
  34.3 3.4 %copy-start.1 = (bf16[289,289]{1,0:T(8,128)(2,1)S(1)}, bf16[289,289]{1,0:T(8,128)(2,1)}, u32[]{:S(2)}) copy-start(bf16[289,289]{1,0:T(8,128)(2,1)} %refs_12_.1) | copy-start | bytes 501130
  34.3 3.4 %copy-start.2 = (bf16[289,289]{1,0:T(8,128)(2,1)S(1)}, bf16[289,289]{1,0:T(8,128)(2,1)}, u32[]{:S(2)}) copy-start(bf16[289,289]{1,0:T(8,128)(2,1)} %refs_7_.3) | copy-start | bytes 501130
  34.3 10.6 %collective-permute-start.9 = (bf16[1,3,289,256]{3,2,1,0:T(8,128)(2,1)S(1)}, bf16[1,3,289,256]{3,2,1,0:T(8,128)(2,1)S(1)}, u32[]{:S(2)}, u32[]{:S(2)}) collective-permute-start(bf16[1,3,289,256]{3,2,1,0:T(8,128)(2,1)S(1)} %get-tuple-element.23), channel_id=1, source_target_pairs={{16,0},{32,16},{48,32},{64,48},{80,64},{96,80},{112,96},{0,112},{1... | collective-permute-start | bytes 1331720 | tf_op jit(solution)/shard_map/ppermute | solution.py:286
  37.7 2.8 %copy-start = (bf16[16,289,289]{2,1,0:T(8,128)(2,1)}, bf16[16,289,289]{2,1,0:T(8,128)(2,1)S(1)}, u32[]{:S(2)}) copy-start(bf16[16,289,289]{2,1,0:T(8,128)(2,1)S(1)} %copy.21.rot_ref.refs_6_.refs_5_) | copy-start | bytes 8018020
  40.5 4.4 %copy-start.4 = (bf16[3,289,1,1,512]{4,1,3,2,0:T(8,128)(2,1)S(1)}, bf16[3,289,1,1,512]{4,1,3,2,0:T(8,128)(2,1)}, u32[]{:S(2)}) copy-start(bf16[3,289,1,1,512]{4,1,3,2,0:T(8,128)(2,1)} %param.8) | copy-start | bytes 2663428
  41.2 27.1 %collective-permute-start.6 = (bf16[2,3,289,256]{3,0,2,1:T(2,128)(2,1)S(1)}, bf16[2,3,289,256]{3,0,2,1:T(2,128)(2,1)S(1)}, u32[]{:S(2)}, u32[]{:S(2)}) collective-permute-start(bf16[2,3,289,256]{3,0,2,1:T(2,128)(2,1)S(1)} %copy.14), channel_id=1, source_target_pairs={{112,0},{0,16},{16,32},{32,48},{48,64},{64,80},{80,96},{96,112},{1... | collective-permute-start | bytes 2663432 | tf_op jit(solution)/shard_map/ppermute | solution.py:286
  41.9 26.5 %collective-permute-start.7 = (bf16[2,3,289,256]{3,0,2,1:T(2,128)(2,1)S(1)}, bf16[2,3,289,256]{3,0,2,1:T(2,128)(2,1)S(1)}, u32[]{:S(2)}, u32[]{:S(2)}) collective-permute-start(bf16[2,3,289,256]{3,0,2,1:T(2,128)(2,1)S(1)} %copy.15), channel_id=1, source_target_pairs={{16,0},{32,16},{48,32},{64,48},{80,64},{96,80},{112,96},{0,112},{1... | collective-permute-start | bytes 2663432 | tf_op jit(solution)/shard_map/ppermute | solution.py:286
  57.2 1.3 %copy-start.5 = (f32[512,896]{1,0:T(8,128)}, f32[512,896]{1,0:T(8,128)S(1)}, u32[]{:S(2)}) copy-start(f32[512,896]{1,0:T(8,128)S(1)} %shard_map.85.refs_11_) | copy-start | bytes 5505028

commit v2 on v1

--- a/solution.py
+++ b/solution.py
@@ -123,24 +123,27 @@
         tail[...] = tail_block(source[MAIN:, MAIN:])
 
 
+def meta_row(metas, dx, dy, row):
+    return metas[dy + 1][dx + 1, row : row + 1, :]
+
+
 def pick_kernel(rows, count, *refs):
-    sources, meta, left, right = refs[:count], refs[count], refs[count + 1], refs[count + 2]
+    sources, metas = refs[:count], refs[count : count + 3]
     to_left, to_right = refs[count + 3 :]
     for i, (source, dy) in enumerate(zip(sources, rows)):
-        for ex, target, out in ((-1, left, to_left), (1, right, to_right)):
+        for ex, out in ((-1, to_left), (1, to_right)):
             o = offset_of(-ex, dy)
-            table = pick_table(
-                target[1, PARTNER + o : PARTNER + o + 1, :], meta[dy + 1, OWN + 8 - o : OWN + 9 - o, :]
-            )
+            table = pick_table(meta_row(metas, ex, 0, PARTNER + o), meta_row(metas, 0, dy, OWN + 8 - o))
             for c in range(3):
-                out[i, c] = nn(source[c], table).astype(BF)
+                out[3 * i + c] = nn(source[c], table).astype(BF)
 
 
 def phase_kernel(sources, whole, first, last, *refs):
     m = len(sources)
     arrays = refs[: (m if last is False else 2)]
     refs = refs[len(arrays) :]
-    meta, left, right, rot_ref, rot_tail, trans_ref, t1, t2, t3 = refs[:9]
+    metas = refs[:3]
+    rot_ref, rot_tail, trans_ref, t1, t2, t3 = refs[3:9]
     refs = refs[9:]
     if first:
         self_ref, s1, s2, s3 = refs[:4]
@@ -151,12 +154,9 @@
     out, picked, grouped, turned, places_to = refs[:5]
     acc = refs[5] if last else out
 
-    def meta_row(dx, dy, row):
-        return (left, meta, right)[dx + 1][dy + 1, row : row + 1, :]
-
     def slot_rows(dx, dy, mine, theirs):
         o = offset_of(dx, dy)
-        return meta_row(0, 0, mine + o), meta_row(dx, dy, theirs + 8 - o)
+        return meta_row(metas, 0, 0, mine + o), meta_row(metas, dx, dy, theirs + 8 - o)
 
     if first:
         unit = eye(CELLS)
@@ -181,9 +181,9 @@
             taken = [picked[c] for c in range(3)]
         elif last:
             side, which = arrays[0 if dx < 0 else 1], (0 if dy < 0 else 1)
-            taken = [side[which, c] for c in range(3)]
+            taken = [side[3 * which + c] for c in range(3)]
         else:
-            taken = [arrays[s][0, c] for c in range(3)]
+            taken = [arrays[s][c] for c in range(3)]
         row_ids = iota((ROWS, SLOTS), 0)
         own_place, partner_place = places[2 * s], places[2 * s + 1]
         place = jnp.concatenate([where_one(row_ids == own_place), where_one(row_ids == partner_place)], axis=1)
@@ -293,16 +293,14 @@
     meta = jnp.concatenate(
         [own_cell.reshape(9, SLOTS), partner_cell.reshape(9, SLOTS), rot, jnp.zeros((META - 27, SLOTS), jnp.int32)]
     )
-    meta_low, meta_high = shift(meta, "gy", 1), shift(meta, "gy", -1)
     low, high = shift(here, "gy", 1), shift(here, "gy", -1)
-    meta = jnp.stack([meta_low, meta, meta_high])
-    left, right = shift(meta, "gx", 1), shift(meta, "gx", -1)
-    metas = (meta, left, right)
-
-    picked = jax.ShapeDtypeStruct((1, 3, K, PAIR), BF)
+    meta = jnp.stack([shift(meta, "gx", 1), meta, shift(meta, "gx", -1)])
+    metas = (shift(meta, "gy", 1), meta, shift(meta, "gy", -1))
+
+    picked = jax.ShapeDtypeStruct((3, K, PAIR), BF)
     to_left, to_right = vmem_call(
         functools.partial(pick_kernel, (0,), 1), (picked, picked), flops=1_000_000_000
-    )(here, *metas)
+    )(here, meta, meta, meta)
     from_left, from_right = shift(to_right, "gx", 1), shift(to_left, "gx", -1)
 
     dense = [
@@ -316,10 +314,10 @@
     weights = (rotations, rot_tail, translation, t1, t2, t3)
 
     acc = phase_call(((0, 0), (-1, 0), (1, 0)), 1, True, False)(
-        here, from_left, from_right, *metas, *weights, self_operator, s1, s2, s3
-    )
-
-    picked = jax.ShapeDtypeStruct((2, 3, K, PAIR), BF)
+        here, from_left, from_right, meta, meta, meta, *weights, self_operator, s1, s2, s3
+    )
+
+    picked = jax.ShapeDtypeStruct((6, K, PAIR), BF)
     to_left, to_right = vmem_call(
         functools.partial(pick_kernel, (-1, 1), 2), (picked, picked), flops=2_000_000_000
     )(low, high, *metas)

time: 83.4 us -> 74.6 us (0.89)
  waiting for transfers between devices: 15.5 us -> 11.7 us
  starting transfers between devices: 20.9 us -> 17.5 us
  local copies, waits for them, and re-layouts: 5.66 us -> 4.03 us
    ppermute x10, waiting for transfers between devices: 15.5 us -> 11.7 us  [shift(): lax.ppermute(block, axis, [((i - distance) % count, i) for i in range(cou...]
    ppermute x10, starting transfers between devices: 20.9 us -> 17.5 us  [shift(): lax.ppermute(block, axis, [((i - distance) % count, i) for i in range(cou...]
    pallas_call x2 -> x0, local copies, waits for them, and re-layouts: 1.37 us -> none  [local(): vmem_call(functools.partial(pick_kernel, (-1, 1), 2), (picked, picked), f...]
  transfers between devices with their start and end apart: 10 -> 10, of which waited for: 2 -> 2; matrix products, arithmetic and copies ran while one was open for 5% -> 3% of each run, Pallas kernels for 31% -> 34%
where the time goes in v2:
time: 74.6 us; the launch traced here: 74.3 us
  Pallas kernels  40 us (54%)
  starting transfers between devices  17.5 us (23%)
  waiting for transfers between devices  11.7 us (16%)
  local copies, waits for them, and re-layouts  4.03 us (5%)
  other arithmetic  0.91 us (1%)
    ppermute x10, starting transfers between devices, shift(): lax.ppermute(block, axis, [((i - distance) % count, i) for i in range(cou...  17.5 us
    pallas_call x1, Pallas kernels, local(): phase_call(((-1, -1), (-1, 1), (1, -1), (1, 1)), 0, False, True)  14.5 us
    pallas_call x1, Pallas kernels, local(): phase_call(((0, 0), (-1, 0), (1, 0)), 1, True, False)  12.4 us
    ppermute x10, waiting for transfers between devices, shift(): lax.ppermute(block, axis, [((i - distance) % count, i) for i in range(cou...  11.7 us
    pallas_call x1, Pallas kernels, local(): phase_call(((0, -1), (0, 1)), 2, False, False)  9.76 us
    unnamed x16, local copies, waits for them, and re-layouts  3.95 us
    pallas_call x1, Pallas kernels, local(): vmem_call(prep_kernel, [jax.ShapeDtypeStruct((NR, TAIL, TAIL), BF)] + den...  1.58 us
  transfers between devices with their start and end apart: 10, of which 2 were waited for; matrix products, arithmetic and copies ran while one was open for 3% of the time, Pallas kernels for 34%

profile of v2, /device:TPU:0, one launch (start us, length us, event | category | flops | bytes accessed | tf_op | source)
XLA Modules:
  0.0 74.3 jit_solution(14447955173225080904)
XLA Ops:
  0.0 1.7 %collective-permute-start = (bf16[3,289,512]{2,1,0:T(8,128)(2,1)}, bf16[3,289,512]{2,1,0:T(8,128)(2,1)S(1)}, u32[]{:S(2)}, u32[]{:S(2)}) collective-permute-start(bf16[3,289,512]{2,1,0:T(8,128)(2,1)} %bitcast.15), channel_id=1, source_target_pairs={{15,0},{0,1},{1,2},{2,3},{3,4},{4,5},{5,6},{6,7},{7,8},{8,9},{9,10... | collective-permute-start | bytes 2663432 | tf_op jit(solution)/shard_map/ppermute | solution.py:286
  1.7 4.9 %collective-permute-start.1 = (bf16[3,289,512]{2,1,0:T(8,128)(2,1)}, bf16[3,289,512]{2,1,0:T(8,128)(2,1)S(1)}, u32[]{:S(2)}, u32[]{:S(2)}) collective-permute-start(bf16[3,289,512]{2,1,0:T(8,128)(2,1)} %bitcast.16), channel_id=1, source_target_pairs={{1,0},{2,1},{3,2},{4,3},{5,4},{6,5},{7,6},{8,7},{9,8},{10,9},{11,1... | collective-permute-start | bytes 2663432 | tf_op jit(solution)/shard_map/ppermute | solution.py:286
  6.6 0.1 pad.6.clone
  6.7 0.7 copy_bitcast_fusion
  7.4 0.8 %bitcast_select_fusion = s32[9,128]{1,0:T(8,128)S(1)} fusion(s32[1,1,9,128,1]{3,4,2,1,0:T(1,128)} %param.14, s32[9]{0:T(128)} %bitcast.21), kind=kLoop, calls=%fused_computation.2 | loop fusion | flops 2304 | bytes 9252 | tf_op jit(solution)/shard_map/jit(_where)/select_n | solution.py:292
  8.1 0.1 add_add_fusion
  8.2 0.0 collective-permute-start.2
  8.2 3.0 %collective-permute-start.3 = (s32[32,128]{1,0:T(8,128)S(1)}, s32[32,128]{1,0:T(8,128)S(1)}, u32[]{:S(2)}, u32[]{:S(2)}) collective-permute-start(s32[32,128]{1,0:T(8,128)S(1)} %add_add_fusion), channel_id=1, source_target_pairs={{16,0},{32,16},{48,32},{64,48},{80,64},{96,80},{112,96},{0,112},{1... | collective-permute-start | bytes 49160 | tf_op jit(solution)/shard_map/ppermute | solution.py:286
  11.2 0.1 fusion
  11.2 1.3 %collective-permute-done.2 = s32[32,128]{1,0:T(8,128)S(1)} collective-permute-done((s32[32,128]{1,0:T(8,128)S(1)}, s32[32,128]{1,0:T(8,128)S(1)}, u32[]{:S(2)}, u32[]{:S(2)}) %collective-permute-start.2) | collective-permute-done | bytes 16416 | tf_op jit(solution)/shard_map/ppermute | solution.py:286
  12.6 0.0 collective-permute-done.3
  12.6 1.2 %copy-done.3 = bf16[3,289,1,1,512]{4,1,3,2,0:T(8,128)(2,1)S(1)} copy-done((bf16[3,289,1,1,512]{4,1,3,2,0:T(8,128)(2,1)S(1)}, bf16[3,289,1,1,512]{4,1,3,2,0:T(8,128)(2,1)}, u32[]{:S(2)}) %copy-start.3) | copy-done | bytes 887832
  13.8 0.7 shard_map.84
  14.4 0.7 collective-permute-start.8
  15.1 2.6 %collective-permute-start.9 = (bf16[3,289,256]{2,1,0:T(8,128)(2,1)S(1)}, bf16[3,289,256]{2,1,0:T(8,128)(2,1)S(1)}, u32[]{:S(2)}, u32[]{:S(2)}) collective-permute-start(bf16[3,289,256]{2,1,0:T(8,128)(2,1)S(1)} %get-tuple-element.23), channel_id=1, source_target_pairs={{16,0},{32,16},{48,32},{64,48},{80,64},{96,80},{112,96},{0,112},{1... | collective-permute-start | bytes 1331720 | tf_op jit(solution)/shard_map/ppermute | solution.py:286
  17.7 0.0 collective-permute-start.4
  17.7 10.3 %collective-permute-done.4.refs_2_ = s32[3,32,128]{2,1,0:T(8,128)S(1)} collective-permute-done((s32[3,32,128]{2,1,0:T(8,128)S(1)}, s32[3,32,128]{2,1,0:T(8,128)S(1)}, u32[]{:S(2)}, u32[]{:S(2)}) %collective-permute-start.4) | collective-permute-done | bytes 49184 | tf_op jit(solution)/shard_map/ppermute | solution.py:286
  28.0 1.7 %collective-permute-start.5 = (s32[3,32,128]{2,1,0:T(8,128)S(1)}, s32[3,32,128]{2,1,0:T(8,128)S(1)}, u32[]{:S(2)}, u32[]{:S(2)}) collective-permute-start(s32[3,32,128]{2,1,0:T(8,128)S(1)} %pad_add_fusion.refs_3_.refs_1_.refs_2_.refs_4_.refs_5_), channel_id=1, source_target_pairs={{1,0},{2,1},{3,2},{4,3},{5,4},{6,5},{7,6},{8,7},{9,8},{10,9},{11,1... | collective-permute-start | bytes 147464 | tf_op jit(solution)/shard_map/ppermute | solution.py:286
  29.8 0.8 %copy.12.rot_ref.refs_6_.refs_5_ = bf16[16,289,289]{2,1,0:T(8,128)(2,1)S(1)} copy(bf16[16,289,289]{2,0,1:T(8,128)(2,1)S(1)} %copy-done.6) | data formatting | bytes 5345344 | tf_op args[3]
  30.6 1.6 %shard_map.83 = (bf16[16,128,128]{2,1,0:T(8,128)(2,1)S(1)}, bf16[3,128,256]{2,1,0:T(8,128)(2,1)S(1)}, bf16[3,256,128]{2,1,0:T(8,128)(2,1)S(1)}, bf16[128,128]{1,...) custom-call(bf16[16,289,289]{2,1,0:T(8,128)(2,1)S(1)} %copy.12.rot_r, ...), custom_call_target="tpu_custom_call" | custom-call | flops 100000000 | bytes 8000000 | tf_op jit(solution)/shard_map/pallas_call | solution.py:311
  32.2 0.0 copy-start.4
  32.2 0.0 collective-permute-done.5.refs_4_
  32.2 0.0 collective-permute-done.refs_0_
  32.2 0.0 collective-permute-done.1.refs_1_
  32.2 1.1 %shard_map.82 = (bf16[6,289,256]{2,1,0:T(8,128)(2,1)S(1)}, bf16[6,289,256]{2,1,0:T(8,128)(2,1)S(1)}) custom-call(bf16[3,289,512]{2,1,0:T(8,128)(2,1)S(1)} %collective-permute-done.refs_0_, bf16[3,289,512]{2,1,0:T(8,128)(2,1)S(1)} %collective-permute-done.1.refs_1_, s32[3,32,128]{2,1,0:T(8,128)S(1)} %collective-permute-done.4.refs_2_, ...), custom_call_target="tpu_custom_call" | custom-call | flops 2000000000 | bytes 8000000 | tf_op jit(solution)/shard_map/pallas_call | solution.py:321
  33.4 0.0 collective-permute-start.6
  33.4 2.9 %collective-permute-start.7 = (bf16[6,289,256]{2,1,0:T(8,128)(2,1)S(1)}, bf16[6,289,256]{2,1,0:T(8,128)(2,1)S(1)}, u32[]{:S(2)}, u32[]{:S(2)}) collective-permute-start(bf16[6,289,256]{2,1,0:T(8,128)(2,1)S(1)} %get-tuple-element.17), channel_id=1, source_target_pairs={{16,0},{32,16},{48,32},{64,48},{80,64},{96,80},{112,96},{0,112},{1... | collective-permute-start | bytes 2663432 | tf_op jit(solution)/shard_map/ppermute | solution.py:286
  36.3 12.4 %shard_map.85.refs_11_ = f32[512,896]{1,0:T(8,128)S(1)} custom-call(bf16[3,289,512]{2,1,0:T(8,128)(2,1)S(1)} %bitcast.18, bf16[3,289,256]{2,1,0:T(8,128)(2,1)S(1)} %collective-permute-done.8.refs_1_, bf16[3,289,256]{2,1,0:T(8,128)(2,1)S(1)} %collective-permute-done.9.refs_2_, s32[3,32,128]{2,1,0:T(8,128)S(1)} %pad_add_fusion.refs_3_.refs_1_.refs_2_.refs_4_.refs_5_, ...), custom_call_target="tpu_custom_call" | custom-call | flops 12000000000 | bytes 8000000 | tf_op jit(solution)/shard_map/pallas_call | solution.py:316
  48.7 1.3 %copy-done.5 = f32[512,896]{1,0:T(8,128)} copy-done((f32[512,896]{1,0:T(8,128)}, f32[512,896]{1,0:T(8,128)S(1)}, u32[]{:S(2)}) %copy-start.5) | copy-done | bytes 1835032
  50.0 9.8 %shard_map.86.refs_11_ = f32[512,896]{1,0:T(8,128)S(1)} custom-call(bf16[3,289,512]{2,1,0:T(8,128)(2,1)S(1)} %collective-permute-done.refs_0_, bf16[3,289,512]{2,1,0:T(8,128)(2,1)S(1)} %collective-permute-done.1.refs_1_, s32[3,32,128]{2,1,0:T(8,128)S(1)} %collective-permute-done.4.refs_2_, ...), custom_call_target="tpu_custom_call" | custom-call | flops 8000000000 | bytes 8000000 | tf_op jit(solution)/shard_map/pallas_call | solution.py:326
  59.7 0.0 collective-permute-done.6.refs_0_
  59.8 14.5 %shard_map.87 = bf16[3,289,512]{2,1,0:T(8,128)(2,1)} custom-call(bf16[6,289,256]{2,1,0:T(8,128)(2,1)S(1)} %collective-permute-done.6.refs_0_, bf16[6,289,256]{2,1,0:T(8,128)(2,1)S(1)} %collective-permute-done.7.refs_1_, s32[3,32,128]{2,1,0:T(8,128)S(1)} %collective-permute-done.4.refs_2_, ...), custom_call_target="tpu_custom_call" | custom-call | flops 16000000000 | bytes 8000000 | tf_op jit(solution)/shard_map/pallas_call | solution.py:327
  (16 shorter events, 0.0 us)
Async XLA Ops:
  0.0 32.2 %collective-permute-start = (bf16[3,289,512]{2,1,0:T(8,128)(2,1)}, bf16[3,289,512]{2,1,0:T(8,128)(2,1)S(1)}, u32[]{:S(2)}, u32[]{:S(2)}) collective-permute-start(bf16[3,289,512]{2,1,0:T(8,128)(2,1)} %bitcast.15), channel_id=1, source_target_pairs={{15,0},{0,1},{1,2},{2,3},{3,4},{4,5},{5,6},{6,7},{7,8},{8,9},{9,10... | collective-permute-start | bytes 2663432 | tf_op jit(solution)/shard_map/ppermute | solution.py:286
  1.7 30.5 %collective-permute-start.1 = (bf16[3,289,512]{2,1,0:T(8,128)(2,1)}, bf16[3,289,512]{2,1,0:T(8,128)(2,1)S(1)}, u32[]{:S(2)}, u32[]{:S(2)}) collective-permute-start(bf16[3,289,512]{2,1,0:T(8,128)(2,1)} %bitcast.16), channel_id=1, source_target_pairs={{1,0},{2,1},{3,2},{4,3},{5,4},{6,5},{7,6},{8,7},{9,8},{10,9},{11,1... | collective-permute-start | bytes 2663432 | tf_op jit(solution)/shard_map/ppermute | solution.py:286
  8.2 4.4 %collective-permute-start.2 = (s32[32,128]{1,0:T(8,128)S(1)}, s32[32,128]{1,0:T(8,128)S(1)}, u32[]{:S(2)}, u32[]{:S(2)}) collective-permute-start(s32[32,128]{1,0:T(8,128)S(1)} %add_add_fusion), channel_id=1, source_target_pairs={{112,0},{0,16},{16,32},{32,48},{48,64},{64,80},{80,96},{96,112},{1... | collective-permute-start | bytes 49160 | tf_op jit(solution)/shard_map/ppermute | solution.py:286
  8.2 4.4 %collective-permute-start.3 = (s32[32,128]{1,0:T(8,128)S(1)}, s32[32,128]{1,0:T(8,128)S(1)}, u32[]{:S(2)}, u32[]{:S(2)}) collective-permute-start(s32[32,128]{1,0:T(8,128)S(1)} %add_add_fusion), channel_id=1, source_target_pairs={{16,0},{32,16},{48,32},{64,48},{80,64},{96,80},{112,96},{0,112},{1... | collective-permute-start | bytes 49160 | tf_op jit(solution)/shard_map/ppermute | solution.py:286
  12.6 1.2 %copy-start.3 = (bf16[3,289,1,1,512]{4,1,3,2,0:T(8,128)(2,1)S(1)}, bf16[3,289,1,1,512]{4,1,3,2,0:T(8,128)(2,1)}, u32[]{:S(2)}) copy-start(bf16[3,289,1,1,512]{4,1,3,2,0:T(8,128)(2,1)} %param.8) | copy-start | bytes 2663428
  13.8 16.0 %copy-start.6 = (bf16[16,289,289]{2,0,1:T(8,128)(2,1)S(1)}, bf16[16,289,289]{2,0,1:T(8,128)(2,1)}, u32[]{:S(2)}) copy-start(bf16[16,289,289]{2,0,1:T(8,128)(2,1)} %param.11) | copy-start | bytes 8018020
  14.4 21.9 %collective-permute-start.8 = (bf16[3,289,256]{2,1,0:T(8,128)(2,1)S(1)}, bf16[3,289,256]{2,1,0:T(8,128)(2,1)S(1)}, u32[]{:S(2)}, u32[]{:S(2)}) collective-permute-start(bf16[3,289,256]{2,1,0:T(8,128)(2,1)S(1)} %get-tuple-element.22), channel_id=1, source_target_pairs={{112,0},{0,16},{16,32},{32,48},{48,64},{64,80},{80,96},{96,112},{1... | collective-permute-start | bytes 1331720 | tf_op jit(solution)/shard_map/ppermute | solution.py:286
  15.1 15.4 %copy-start.1 = (bf16[289,289]{1,0:T(8,128)(2,1)S(1)}, bf16[289,289]{1,0:T(8,128)(2,1)}, u32[]{:S(2)}) copy-start(bf16[289,289]{1,0:T(8,128)(2,1)} %refs_12_.1) | copy-start | bytes 501130
  15.1 15.4 %copy-start.2 = (bf16[289,289]{1,0:T(8,128)(2,1)S(1)}, bf16[289,289]{1,0:T(8,128)(2,1)}, u32[]{:S(2)}) copy-start(bf16[289,289]{1,0:T(8,128)(2,1)} %refs_7_.3) | copy-start | bytes 501130
  15.1 21.2 %collective-permute-start.9 = (bf16[3,289,256]{2,1,0:T(8,128)(2,1)S(1)}, bf16[3,289,256]{2,1,0:T(8,128)(2,1)S(1)}, u32[]{:S(2)}, u32[]{:S(2)}) collective-permute-start(bf16[3,289,256]{2,1,0:T(8,128)(2,1)S(1)} %get-tuple-element.23), channel_id=1, source_target_pairs={{16,0},{32,16},{48,32},{64,48},{80,64},{96,80},{112,96},{0,112},{1... | collective-permute-start | bytes 1331720 | tf_op jit(solution)/shard_map/ppermute | solution.py:286
  17.7 10.3 %collective-permute-start.4 = (s32[3,32,128]{2,1,0:T(8,128)S(1)}, s32[3,32,128]{2,1,0:T(8,128)S(1)}, u32[]{:S(2)}, u32[]{:S(2)}) collective-permute-start(s32[3,32,128]{2,1,0:T(8,128)S(1)} %pad_add_fusion.refs_3_.refs_1_.refs_2_.refs_4_.refs_5_), channel_id=1, source_target_pairs={{15,0},{0,1},{1,2},{2,3},{3,4},{4,5},{5,6},{6,7},{7,8},{8,9},{9,10... | collective-permute-start | bytes 147464 | tf_op jit(solution)/shard_map/ppermute | solution.py:286
  28.0 4.2 %collective-permute-start.5 = (s32[3,32,128]{2,1,0:T(8,128)S(1)}, s32[3,32,128]{2,1,0:T(8,128)S(1)}, u32[]{:S(2)}, u32[]{:S(2)}) collective-permute-start(s32[3,32,128]{2,1,0:T(8,128)S(1)} %pad_add_fusion.refs_3_.refs_1_.refs_2_.refs_4_.refs_5_), channel_id=1, source_target_pairs={{1,0},{2,1},{3,2},{4,3},{5,4},{6,5},{7,6},{8,7},{9,8},{10,9},{11,1... | collective-permute-start | bytes 147464 | tf_op jit(solution)/shard_map/ppermute | solution.py:286
  30.6 2.8 %copy-start = (bf16[16,289,289]{2,1,0:T(8,128)(2,1)}, bf16[16,289,289]{2,1,0:T(8,128)(2,1)S(1)}, u32[]{:S(2)}) copy-start(bf16[16,289,289]{2,1,0:T(8,128)(2,1)S(1)} %copy.12.rot_ref.refs_6_.refs_5_) | copy-start | bytes 8018020
  32.2 4.2 %copy-start.4 = (bf16[3,289,1,1,512]{4,1,3,2,0:T(8,128)(2,1)S(1)}, bf16[3,289,1,1,512]{4,1,3,2,0:T(8,128)(2,1)}, u32[]{:S(2)}) copy-start(bf16[3,289,1,1,512]{4,1,3,2,0:T(8,128)(2,1)} %param.8) | copy-start | bytes 2663428
  33.4 26.4 %collective-permute-start.6 = (bf16[6,289,256]{2,1,0:T(8,128)(2,1)S(1)}, bf16[6,289,256]{2,1,0:T(8,128)(2,1)S(1)}, u32[]{:S(2)}, u32[]{:S(2)}) collective-permute-start(bf16[6,289,256]{2,1,0:T(8,128)(2,1)S(1)} %get-tuple-element.16), channel_id=1, source_target_pairs={{112,0},{0,16},{16,32},{32,48},{48,64},{64,80},{80,96},{96,112},{1... | collective-permute-start | bytes 2663432 | tf_op jit(solution)/shard_map/ppermute | solution.py:286
  33.4 26.4 %collective-permute-start.7 = (bf16[6,289,256]{2,1,0:T(8,128)(2,1)S(1)}, bf16[6,289,256]{2,1,0:T(8,128)(2,1)S(1)}, u32[]{:S(2)}, u32[]{:S(2)}) collective-permute-start(bf16[6,289,256]{2,1,0:T(8,128)(2,1)S(1)} %get-tuple-element.17), channel_id=1, source_target_pairs={{16,0},{32,16},{48,32},{64,48},{80,64},{96,80},{112,96},{0,112},{1... | collective-permute-start | bytes 2663432 | tf_op jit(solution)/shard_map/ppermute | solution.py:286
  48.7 1.3 %copy-start.5 = (f32[512,896]{1,0:T(8,128)}, f32[512,896]{1,0:T(8,128)S(1)}, u32[]{:S(2)}) copy-start(f32[512,896]{1,0:T(8,128)S(1)} %shard_map.85.refs_11_) | copy-start | bytes 5505028

commit v3 on v2

--- a/solution.py
+++ b/solution.py
@@ -12,6 +12,7 @@
 
 K = 289
 MAIN = 256
+CUT = 192
 REST = K - MAIN
 TAIL = 128
 WIDE = 3 * MAIN + TAIL
@@ -23,7 +24,8 @@
 GROUP = 2 * CAP
 ROWS = NR * GROUP
 OWN, PARTNER, ROT, META = 0, 9, 18, 32
-VMEM_LIMIT = 48 * 1024 * 1024
+COLUMNS = (slice(0, 256), slice(256, 512), slice(512, 768), slice(768, 896))
+VMEM_LIMIT = 28 * 1024 * 1024
 
 
 def nt(a, b):
@@ -92,15 +94,12 @@
     return places
 
 
-def apply_dense(mains, tail, main_ref, to_tail_ref, from_tail_ref, tail_ref):
-    size = mains[0].shape[0]
-    middle = nt(jnp.concatenate(mains, axis=0), main_ref[:MAIN, :MAIN])
-    out_tail = nt(tail, tail_ref[...])
-    outs = []
-    for c in range(3):
-        outs.append(middle[c * size : (c + 1) * size] + nt(tail, from_tail_ref[c]))
-        out_tail = out_tail + nt(mains[c], to_tail_ref[c])
-    return outs, out_tail
+def apply_dense(block, main_ref, tail_ref):
+    tail = block[:, 3 * MAIN :]
+    outs = [
+        nt(jnp.concatenate([block[:, c * MAIN : (c + 1) * MAIN], tail], axis=1), main_ref[c]) for c in range(3)
+    ]
+    return outs + [nt(block, tail_ref[...])]
 
 
 def split_lanes(block):
@@ -116,15 +115,17 @@
 
     for r in range(NR):
         rot_tail[r] = tail_block(rot_ref[r, MAIN:, MAIN:])
-    for source, (to_tail, from_tail, tail) in ((trans_ref, pieces[:3]), (self_ref, pieces[3:])):
+    for source, (main, tail) in ((trans_ref, pieces[:2]), (self_ref, pieces[2:])):
         for c in range(3):
-            to_tail[c] = nn(spread(c), source[MAIN:, :MAIN]).astype(BF)
-            from_tail[c] = nt(source[:MAIN, MAIN:], spread(c)).astype(BF)
-        tail[...] = tail_block(source[MAIN:, MAIN:])
+            main[c, :, :MAIN] = source[:MAIN, :MAIN]
+            main[c, :, MAIN:] = nt(source[:MAIN, MAIN:], spread(c)).astype(BF)
+            tail[:, c * MAIN : (c + 1) * MAIN] = nn(spread(c), source[MAIN:, :MAIN]).astype(BF)
+        tail[:, 3 * MAIN :] = tail_block(source[MAIN:, MAIN:])
 
 
 def meta_row(metas, dx, dy, row):
-    return metas[dy + 1][dx + 1, row : row + 1, :]
+    meta = metas[dy + 1]
+    return meta[dx + 1 if meta.shape[0] == 3 else 0, row : row + 1, :]
 
 
 def pick_kernel(rows, count, *refs):
@@ -138,16 +139,37 @@
                 out[3 * i + c] = nn(source[c], table).astype(BF)
 
 
-def phase_kernel(sources, whole, first, last, *refs):
+def column_source(kind, arrays, s, dx, dy):
+    if kind == "here":
+        return [[arrays[0][c]] for c in range(3)]
+    if kind == "sides":
+        return [[arrays[s][c]] for c in range(3)]
+    if kind == "rows":
+        return [[arrays[2 * s][c], arrays[2 * s + 1][c]] for c in range(3)]
+    low, high = arrays[:2] if dx < 0 else arrays[2:]
+    which = 0 if dy < 0 else 3
+    return [[low[which + c], high[which + c]] for c in range(3)]
+
+
+PHASES = {
+    "here": (((0, 0),), 1),
+    "sides": (((-1, 0), (1, 0)), 2),
+    "rows": (((0, -1), (0, 1)), 4),
+    "corners": (((-1, -1), (-1, 1), (1, -1), (1, 1)), 4),
+}
+
+
+def phase_kernel(kind, *refs):
+    sources, inputs = PHASES[kind]
+    first, last, whole = kind == "here", kind == "corners", kind in ("here", "rows")
     m = len(sources)
-    arrays = refs[: (m if last is False else 2)]
-    refs = refs[len(arrays) :]
+    arrays, refs = refs[:inputs], refs[inputs:]
     metas = refs[:3]
-    rot_ref, rot_tail, trans_ref, t1, t2, t3 = refs[3:9]
-    refs = refs[9:]
+    rot_ref, rot_tail, trans_main, trans_tail = refs[3:7]
+    refs = refs[7:]
     if first:
-        self_ref, s1, s2, s3 = refs[:4]
-        refs = refs[4:]
+        self_main, self_tail = refs[:2]
+        refs = refs[2:]
     else:
         acc_in = refs[0]
         refs = refs[1:]
@@ -161,12 +183,10 @@
     if first:
         unit = eye(CELLS)
         here = arrays[0]
-        mains = [nt(unit, here[c, :MAIN, :]).astype(BF) for c in range(3)]
-        tail = nt(unit, tail_of([here[c, MAIN:, :] for c in range(3)])).astype(BF)
-        outs, out_tail = apply_dense(mains, tail, self_ref, s1, s2, s3)
-        for c in range(3):
-            acc[:, c * MAIN : (c + 1) * MAIN] = outs[c]
-        acc[:, 3 * MAIN :] = out_tail
+        parts = [nt(unit, here[c, :MAIN, :]).astype(BF) for c in range(3)]
+        parts.append(nt(unit, tail_of([here[c, MAIN:, :] for c in range(3)])).astype(BF))
+        for lanes, part in zip(COLUMNS, apply_dense(jnp.concatenate(parts, axis=1), self_main, self_tail)):
+            acc[:, lanes] = part
 
     rots = []
     for dx, dy in sources:
@@ -174,16 +194,17 @@
     places = positions(rots)
 
     for s, (dx, dy) in enumerate(sources):
-        if s < whole:
+        taken = column_source(kind, arrays, s, dx, dy)
+        if whole:
             table = pick_table(*slot_rows(dx, dy, PARTNER, OWN))
             for c in range(3):
-                picked[c] = nn(arrays[s][c], table).astype(BF)
+                start = 0
+                for piece in taken[c]:
+                    picked[c, start : start + piece.shape[0]] = nn(piece, table).astype(BF)
+                    start += piece.shape[0]
             taken = [picked[c] for c in range(3)]
-        elif last:
-            side, which = arrays[0 if dx < 0 else 1], (0 if dy < 0 else 1)
-            taken = [side[3 * which + c] for c in range(3)]
         else:
-            taken = [arrays[s][c] for c in range(3)]
+            taken = [jnp.concatenate(pieces, axis=0) for pieces in taken]
         row_ids = iota((ROWS, SLOTS), 0)
         own_place, partner_place = places[2 * s], places[2 * s + 1]
         place = jnp.concatenate([where_one(row_ids == own_place), where_one(row_ids == partner_place)], axis=1)
@@ -218,31 +239,18 @@
     for r in range(NR):
         turn(r, grouped, turned, nt)
 
-    step = 4
-
-    def translate(i, carry):
-        block = turned[pl.ds(i * step, step)].reshape(step * size, WIDE)
-        mains, tail = split_lanes(block)
-        outs, out_tail = apply_dense(mains, tail, trans_ref, t1, t2, t3)
-        for c in range(3):
-            grouped[pl.ds(i * step, step), :, c * MAIN : (c + 1) * MAIN] = (
-                outs[c].astype(BF).reshape(step, size, MAIN)
-            )
-        grouped[pl.ds(i * step, step), :, 3 * MAIN :] = out_tail.astype(BF).reshape(step, size, TAIL)
-        return carry
-
-    lax.fori_loop(0, NR // step, translate, 0)
+    block = turned[...].reshape(NR * size, WIDE)
+    for lanes, part in zip(COLUMNS, apply_dense(block, trans_main, trans_tail)):
+        grouped[:, :, lanes] = part.astype(BF).reshape(NR, size, lanes.stop - lanes.start)
 
     for r in range(NR):
         turn(r, grouped, turned, nn)
 
-    columns = [slice(c * MAIN, (c + 1) * MAIN) for c in range(3)] + [slice(3 * MAIN, WIDE)]
-    for lanes in columns:
-        total = acc[:, lanes] if first else acc_in[:, lanes]
-        for s in range(m):
-            back = turned[:, s * GROUP : (s + 1) * GROUP, lanes].reshape(ROWS, lanes.stop - lanes.start)
-            total = total + nn(places_to[:, s * ROWS : (s + 1) * ROWS], back)
-        acc[:, lanes] = total
+    for lanes in COLUMNS:
+        width = lanes.stop - lanes.start
+        back = [turned[:, s * GROUP : (s + 1) * GROUP, lanes].reshape(ROWS, width) for s in range(m)]
+        total = nn(places_to[...], jnp.concatenate(back, axis=0))
+        acc[:, lanes] = total + (acc[:, lanes] if first else acc_in[:, lanes])
 
     if last:
         unit = eye(MAIN)
@@ -263,8 +271,8 @@
     )
 
 
-def phase_call(sources, whole, first, last):
-    m = len(sources)
+def phase_call(kind):
+    m, last = len(PHASES[kind][0]), kind == "corners"
     if last:
         out = jax.ShapeDtypeStruct((3, K, CELLS), BF)
     else:
@@ -277,7 +285,7 @@
     ]
     if last:
         scratch.append(pltpu.VMEM((CELLS, WIDE), F32))
-    kernel = functools.partial(phase_kernel, sources, whole, first, last)
+    kernel = functools.partial(phase_kernel, kind)
     return vmem_call(kernel, out, scratch, flops=m * 4_000_000_000)
 
 
@@ -293,40 +301,41 @@
     meta = jnp.concatenate(
         [own_cell.reshape(9, SLOTS), partner_cell.reshape(9, SLOTS), rot, jnp.zeros((META - 27, SLOTS), jnp.int32)]
     )
-    low, high = shift(here, "gy", 1), shift(here, "gy", -1)
+    low_a, high_a = shift(here[:, :CUT], "gy", 1), shift(here[:, :CUT], "gy", -1)
+    low_b, high_b = shift(here[:, CUT:], "gy", 1), shift(here[:, CUT:], "gy", -1)
+    mine = meta[None]
     meta = jnp.stack([shift(meta, "gx", 1), meta, shift(meta, "gx", -1)])
-    metas = (shift(meta, "gy", 1), meta, shift(meta, "gy", -1))
-
-    picked = jax.ShapeDtypeStruct((3, K, PAIR), BF)
-    to_left, to_right = vmem_call(
-        functools.partial(pick_kernel, (0,), 1), (picked, picked), flops=1_000_000_000
-    )(here, meta, meta, meta)
-    from_left, from_right = shift(to_right, "gx", 1), shift(to_left, "gx", -1)
+    meta_low, meta_high = shift(meta, "gy", 1), shift(meta, "gy", -1)
 
     dense = [
-        jax.ShapeDtypeStruct((3, TAIL, MAIN), BF),
-        jax.ShapeDtypeStruct((3, MAIN, TAIL), BF),
-        jax.ShapeDtypeStruct((TAIL, TAIL), BF),
+        jax.ShapeDtypeStruct((3, MAIN, MAIN + TAIL), BF),
+        jax.ShapeDtypeStruct((TAIL, WIDE), BF),
     ]
-    rot_tail, t1, t2, t3, s1, s2, s3 = vmem_call(
+    rot_tail, *dense = vmem_call(
         prep_kernel, [jax.ShapeDtypeStruct((NR, TAIL, TAIL), BF)] + dense + dense, flops=100_000_000
     )(rotations, translation, self_operator)
-    weights = (rotations, rot_tail, translation, t1, t2, t3)
-
-    acc = phase_call(((0, 0), (-1, 0), (1, 0)), 1, True, False)(
-        here, from_left, from_right, meta, meta, meta, *weights, self_operator, s1, s2, s3
-    )
-
-    picked = jax.ShapeDtypeStruct((6, K, PAIR), BF)
-    to_left, to_right = vmem_call(
-        functools.partial(pick_kernel, (-1, 1), 2), (picked, picked), flops=2_000_000_000
-    )(low, high, *metas)
-    from_left, from_right = shift(to_right, "gx", 1), shift(to_left, "gx", -1)
-
-    acc = phase_call(((0, -1), (0, 1)), 2, False, False)(low, high, *metas, *weights, acc)
-    velocity = phase_call(((-1, -1), (-1, 1), (1, -1), (1, 1)), 0, False, True)(
-        from_left, from_right, *metas, *weights, acc
-    )
+    weights = (rotations, rot_tail, *dense[:2])
+
+    def pick(sources, rows, metas):
+        picked = jax.ShapeDtypeStruct((3 * len(rows), sources[0].shape[1], PAIR), BF)
+        to_left, to_right = vmem_call(
+            functools.partial(pick_kernel, rows, len(rows)), (picked, picked), flops=1_000_000_000
+        )(*sources, *metas)
+        return to_left, shift(to_right, "gx", 1), shift(to_left, "gx", -1)
+
+    after = lax.optimization_barrier
+    acc = phase_call("here")(here, mine, mine, mine, *weights, *dense[2:])
+    meta, meta_low, meta_high, acc = after((meta, meta_low, meta_high, acc))
+    _, from_left, from_right = pick((here,), (0,), (meta, meta, meta))
+    done, left_a, right_a = pick((low_a, high_a), (-1, 1), (meta_low, meta, meta_high))
+    meta, done = after((meta, done))
+    acc = phase_call("sides")(from_left, from_right, meta, meta, meta, *weights, acc)
+    meta_low, meta_high, acc = after((meta_low, meta_high, acc))
+    done, left_b, right_b = pick((low_b, high_b), (-1, 1), (meta_low, meta, meta_high))
+    meta, done = after((meta, done))
+    metas = (meta_low, meta, meta_high)
+    acc = phase_call("rows")(low_a, low_b, high_a, high_b, *metas, *weights, acc)
+    velocity = phase_call("corners")(left_a, left_b, right_a, right_b, *metas, *weights, acc)
     return velocity.reshape(3, K, 1, 1, CELLS)
 
 

time: 74.6 us -> 69.7 us (0.934)
  Pallas kernels: 40 us -> 31 us
  starting transfers between devices: 17.5 us -> 23.3 us
  waiting for transfers between devices: 11.7 us -> 9.33 us
    pallas_call x5 -> x7, Pallas kernels: 38.4 us -> 29.3 us  [the longest x1 10.8 us: local(): phase_call('corners')]
    ppermute x10 -> x14, starting transfers between devices: 17.5 us -> 23.3 us  [shift(): lax.ppermute(block, axis, [((i - distance) % count, i) for i in range(cou...]
    ppermute x10 -> x14, waiting for transfers between devices: 11.7 us -> 9.33 us  [shift(): lax.ppermute(block, axis, [((i - distance) % count, i) for i in range(cou...]
    slice x0 -> x2, local copies, waits for them, and re-layouts: none -> 1.12 us  [the longest x1 1.1 us: local(): here[:, :CUT]]
    unnamed x16 -> x8, local copies, waits for them, and re-layouts: 3.95 us -> 3.56 us
  transfers between devices with their start and end apart: 10 -> 14, of which waited for: 2 -> 4; matrix products, arithmetic and copies ran while one was open for 3% -> 6% of each run, Pallas kernels for 34% -> 28%
where the time goes in v3:
time: 69.7 us; the launch traced here: 69.5 us
  Pallas kernels  31 us (44%)
  starting transfers between devices  23.3 us (33%)
  waiting for transfers between devices  9.33 us (13%)
  local copies, waits for them, and re-layouts  4.76 us (7%)
  other arithmetic  0.91 us (1%)
    ppermute x14, starting transfers between devices, shift(): lax.ppermute(block, axis, [((i - distance) % count, i) for i in range(cou...  23.3 us
    pallas_call x1, Pallas kernels, local(): phase_call('corners')  10.8 us
    ppermute x14, waiting for transfers between devices, shift(): lax.ppermute(block, axis, [((i - distance) % count, i) for i in range(cou...  9.33 us
    pallas_call x1, Pallas kernels, local(): phase_call('rows')(low_a, low_b, high_a, high_b, *metas, *weights, acc)  6.06 us
    pallas_call x1, Pallas kernels, local(): phase_call('sides')(from_left, from_right, meta, meta, meta, *weights, acc)  5.22 us
    pallas_call x1, Pallas kernels, local(): acc = phase_call('here')(here, mine, mine, mine, *weights, *dense[2:])  5.13 us
    unnamed x8, local copies, waits for them, and re-layouts  3.56 us
    pallas_call x3, Pallas kernels, pick(): vmem_call(functools.partial(pick_kernel, rows, len(rows)), (picked, picke...  2.04 us
  transfers between devices with their start and end apart: 14, of which 4 were waited for; matrix products, arithmetic and copies ran while one was open for 6% of the time, Pallas kernels for 28%

profile of v3, /device:TPU:0, one launch (start us, length us, event | category | flops | bytes accessed | tf_op | source)
XLA Modules:
  0.0 69.5 jit_solution(9347898253541261182)
XLA Ops:
  0.0 0.1 pad.6.clone
  0.1 0.7 %copy_bitcast_fusion = (s32[9,128]{1,0:T(8,128)S(1)}, s32[9,128]{1,0:T(8,128)S(1)}) fusion(s32[1,1,9,128]{3,1,2,0:T(1,128)} %param.13, s32[1,1,9,128]{3,1,2,0:T(1,128)} %param.12), kind=kLoop, calls=%fused_computation.3 | loop fusion | bytes 18432
  0.8 0.8 %bitcast_select_fusion = s32[9,128]{1,0:T(8,128)S(1)} fusion(s32[1,1,9,128,1]{3,4,2,1,0:T(1,128)} %param.14, s32[9]{0:T(128)} %bitcast.21), kind=kLoop, calls=%fused_computation.2 | loop fusion | flops 2304 | bytes 9252 | tf_op jit(solution)/shard_map/jit(_where)/select_n | solution.py:300
  1.5 0.1 add_add_fusion
  1.6 3.0 %collective-permute-start.3 = (s32[32,128]{1,0:T(8,128)S(1)}, s32[32,128]{1,0:T(8,128)S(1)}, u32[]{:S(2)}, u32[]{:S(2)}) collective-permute-start(s32[32,128]{1,0:T(8,128)S(1)} %add_add_fusion), channel_id=1, source_target_pairs={{16,0},{32,16},{48,32},{64,48},{80,64},{96,80},{112,96},{0,112},{1... | collective-permute-start | bytes 49160 | tf_op jit(solution)/shard_map/ppermute | solution.py:294
  4.6 1.1 %slice.10 = bf16[3,192,512]{2,1,0:T(8,128)(2,1)S(1)} slice(bf16[3,289,512]{2,1,0:T(8,128)(2,1)} %bitcast.15), slice={[0:3], [0:192], [0:512]} | slice | bytes 1179648 | tf_op jit(solution)/shard_map/slice | solution.py:304
  5.7 1.7 %collective-permute-start = (bf16[3,192,512]{2,1,0:T(8,128)(2,1)S(1)}, bf16[3,192,512]{2,1,0:T(8,128)(2,1)S(1)}, u32[]{:S(2)}, u32[]{:S(2)}) collective-permute-start(bf16[3,192,512]{2,1,0:T(8,128)(2,1)S(1)} %slice.10), channel_id=1, source_target_pairs={{15,0},{0,1},{1,2},{2,3},{3,4},{4,5},{5,6},{6,7},{7,8},{8,9},{9,10... | collective-permute-start | bytes 1769480 | tf_op jit(solution)/shard_map/ppermute | solution.py:294
  7.4 5.0 %collective-permute-start.1 = (bf16[3,192,512]{2,1,0:T(8,128)(2,1)S(1)}, bf16[3,192,512]{2,1,0:T(8,128)(2,1)S(1)}, u32[]{:S(2)}, u32[]{:S(2)}) collective-permute-start(bf16[3,192,512]{2,1,0:T(8,128)(2,1)S(1)} %slice.10), channel_id=1, source_target_pairs={{1,0},{2,1},{3,2},{4,3},{5,4},{6,5},{7,6},{8,7},{9,8},{10,9},{11,1... | collective-permute-start | bytes 1769480 | tf_op jit(solution)/shard_map/ppermute | solution.py:294
  12.4 0.1 fusion.refs_1_.refs_2_.refs_3_
  12.5 2.8 %copy.10.rot_ref.refs_4_.refs_5_.refs_7_ = bf16[16,289,289]{2,1,0:T(8,128)(2,1)S(1)} copy(bf16[16,289,289]{2,0,1:T(8,128)(2,1)} %param.11) | data formatting | bytes 5345344 | tf_op args[3]
  15.4 1.7 %shard_map.82 = (bf16[16,128,128]{2,1,0:T(8,128)(2,1)S(1)}, bf16[3,256,384]{2,1,0:T(8,128)(2,1)S(1)}, bf16[128,896]{1,0:T(8,128)(2,1)S(1)}, bf16[3,256,384]{2,1,0:T(8,128)(2,1)S(1)}, bf16[128,896]{1,0:T(8,128)(2,1)S(1)}) custom-call(bf16[16,289,289]{2,1,0:T(8,128)(2,1)S(1)} %copy.10.rot_ref.refs_4_.refs_5_.refs_7_, bf16[289,289]{1,0:T(8,128)(2,1)S(1)} %copy-done.1, ...), custom_call_target="tpu_custom_call" | custom-call | flops 100000000 | bytes 8000000 | tf_op jit(solution)/shard_map/pallas_call | solution.py:314
  17.1 0.1 collective-permute-start.4
  17.2 5.3 %collective-permute-start.5 = (s32[3,32,128]{2,1,0:T(8,128)S(1)}, s32[3,32,128]{2,1,0:T(8,128)S(1)}, u32[]{:S(2)}, u32[]{:S(2)}) collective-permute-start(s32[3,32,128]{2,1,0:T(8,128)S(1)} %pad_add_fusion.refs_3_.refs_1_.refs_2_.refs_4_.refs_5_), channel_id=1, source_target_pairs={{1,0},{2,1},{3,2},{4,3},{5,4},{6,5},{7,6},{8,7},{9,8},{10,9},{11,1... | collective-permute-start | bytes 147464 | tf_op jit(solution)/shard_map/ppermute | solution.py:294
  22.6 5.1 %shard_map.83.refs_9_ = f32[512,896]{1,0:T(8,128)S(1)} custom-call(bf16[3,289,512]{2,1,0:T(8,128)(2,1)S(1)} %bitcast.16, s32[1,32,128]{2,1,0:T(8,128)S(1)} %fusion.refs_1_.refs_2_.refs_3_, s32[1,32,128]{2,1,0:T(8,128)S(1)} %fusion.refs_1_.refs_2_.refs_3_, s32[1,32,128]{2,1,0:T(8,128)S(1)} %fusion.refs_1_.refs_2_.refs_3_, ...), custom_call_target="tpu_custom_call" | custom-call | flops 4000000000 | bytes 8000000 | tf_op jit(solution)/shard_map/pallas_call | solution.py:327
  27.7 0.7 shard_map.85
  28.4 0.0 collective-permute-start.10
  28.4 0.5 collective-permute-start.9
  28.9 0.1 collective-permute-start.7
  29.0 5.3 %collective-permute-start.8 = (bf16[3,97,512]{2,1,0:T(8,128)(2,1)S(1)}, bf16[3,97,512]{2,1,0:T(8,128)(2,1)S(1)}, u32[]{:S(2)}, u32[]{:S(2)}) collective-permute-start(bf16[3,97,512]{2,1,0:T(8,128)(2,1)S(1)} %slice.11), channel_id=1, source_target_pairs={{1,0},{2,1},{3,2},{4,3},{5,4},{6,5},{7,6},{8,7},{9,8},{10,9},{11,1... | collective-permute-start | bytes 893960 | tf_op jit(solution)/shard_map/ppermute | solution.py:294
  34.3 0.8 %shard_map.84 = (bf16[6,192,256]{2,1,0:T(8,128)(2,1)S(1)}, bf16[6,192,256]{2,1,0:T(8,128)(2,1)S(1)}) custom-call(bf16[3,192,512]{2,1,0:T(8,128)(2,1)S(1)} %collective-permute-done.refs_0_, bf16[3,192,512]{2,1,0:T(8,128)(2,1)S(1)} %collective-permute-done.1.refs_1_.refs_2_, s32[3,32,128]{2,1,0:T(8,128)S(1)} %collective-permute-done.4.refs_2_.refs_4_, ...), custom_call_target="tpu_custom_call" | custom-call | flops 1000000000 | bytes 8000000 | tf_op jit(solution)/shard_map/pallas_call | solution.py:321
  35.1 2.3 %collective-permute-done.9.refs_0_ = bf16[3,289,256]{2,1,0:T(8,128)(2,1)S(1)} collective-permute-done((bf16[3,289,256]{2,1,0:T(8,128)(2,1)S(1)}, bf16[3,289,256]{2,1,0:T(8,128)(2,1)S(1)}, u32[]{:S(2)}, u32[]{:S(2)}) %collective-permute-start.9) | collective-permute-done | bytes 443936 | tf_op jit(solution)/shard_map/ppermute | solution.py:294
  37.5 5.2 %shard_map.86.refs_11_ = f32[512,896]{1,0:T(8,128)S(1)} custom-call(bf16[3,289,256]{2,1,0:T(8,128)(2,1)S(1)} %collective-permute-done.9.refs_0_, bf16[3,289,256]{2,1,0:T(8,128)(2,1)S(1)} %collective-permute-done.10.refs_1_, s32[3,32,128]{2,1,0:T(8,128)S(1)} %pad_add_fusion.refs_3_.refs_1_.refs_2_.refs_4_.refs_5_, ...), custom_call_target="tpu_custom_call" | custom-call | flops 8000000000 | bytes 8000000 | tf_op jit(solution)/shard_map/pallas_call | solution.py:332
  42.7 0.6 shard_map.87
  43.3 1.0 %collective-permute-start.13 = (bf16[6,97,256]{2,1,0:T(8,128)(2,1)S(1)}, bf16[6,97,256]{2,1,0:T(8,128)(2,1)S(1)}, u32[]{:S(2)}, u32[]{:S(2)}) collective-permute-start(bf16[6,97,256]{2,1,0:T(8,128)(2,1)S(1)} %get-tuple-element.42), channel_id=1, source_target_pairs={{16,0},{32,16},{48,32},{64,48},{80,64},{96,80},{112,96},{0,112},{1... | collective-permute-start | bytes 893960 | tf_op jit(solution)/shard_map/ppermute | solution.py:294
  44.3 0.4 collective-permute-start.12
  44.7 0.2 collective-permute-start.11
  44.9 0.8 %collective-permute-start.6 = (bf16[6,192,256]{2,1,0:T(8,128)(2,1)S(1)}, bf16[6,192,256]{2,1,0:T(8,128)(2,1)S(1)}, u32[]{:S(2)}, u32[]{:S(2)}) collective-permute-start(bf16[6,192,256]{2,1,0:T(8,128)(2,1)S(1)} %get-tuple-element.33), channel_id=1, source_target_pairs={{112,0},{0,16},{16,32},{32,48},{48,64},{64,80},{80,96},{96,112},{1... | collective-permute-start | bytes 1769480 | tf_op jit(solution)/shard_map/ppermute | solution.py:294
  45.6 6.1 %shard_map.88.refs_11_ = f32[512,896]{1,0:T(8,128)S(1)} custom-call(bf16[3,192,512]{2,1,0:T(8,128)(2,1)S(1)} %collective-permute-done.refs_0_, bf16[3,97,512]{2,1,0:T(8,128)(2,1)S(1)} %collective-permute-done.7.refs_0_.refs_1_, bf16[3,192,512]{2,1,0:T(8,128)(2,1)S(1)} %collective-permute-done.1.refs_1_.refs_2_, ...), custom_call_target="tpu_custom_call" | custom-call | flops 8000000000 | bytes 8000000 | tf_op jit(solution)/shard_map/pallas_call | solution.py:337
  51.7 0.7 collective-permute-done.11.refs_1_
  52.3 2.8 %collective-permute-done.12.refs_2_ = bf16[6,192,256]{2,1,0:T(8,128)(2,1)S(1)} collective-permute-done((bf16[6,192,256]{2,1,0:T(8,128)(2,1)S(1)}, bf16[6,192,256]{2,1,0:T(8,128)(2,1)S(1)}, u32[]{:S(2)}, u32[]{:S(2)}) %collective-permute-start.12) | collective-permute-done | bytes 589856 | tf_op jit(solution)/shard_map/ppermute | solution.py:294
  55.2 3.5 %collective-permute-done.6.refs_0_ = bf16[6,192,256]{2,1,0:T(8,128)(2,1)S(1)} collective-permute-done((bf16[6,192,256]{2,1,0:T(8,128)(2,1)S(1)}, bf16[6,192,256]{2,1,0:T(8,128)(2,1)S(1)}, u32[]{:S(2)}, u32[]{:S(2)}) %collective-permute-start.6) | collective-permute-done | bytes 589856 | tf_op jit(solution)/shard_map/ppermute | solution.py:294
  58.6 10.8 %shard_map.89 = bf16[3,289,512]{2,1,0:T(8,128)(2,1)} custom-call(bf16[6,192,256]{2,1,0:T(8,128)(2,1)S(1)} %collective-permute-done.6.refs_0_, bf16[6,97,256]{2,1,0:T(8,128)(2,1)S(1)} %collective-permute-done.11.refs_1_, bf16[6,192,256]{2,1,0:T(8,128)(2,1)S(1)} %collective-permute-done.12.refs_2_, bf16[6,97,256]{2,1,0:T(8,128)(2,1)S(1)} %collective-permute-done.13.refs_3_, ...), custom_call_target="tpu_custom_call" | custom-call | flops 16000000000 | bytes 8000000 | tf_op jit(solution)/shard_map/pallas_call | solution.py:338
  (20 shorter events, 0.1 us)
Async XLA Ops:
  1.6 15.5 %collective-permute-start.2 = (s32[32,128]{1,0:T(8,128)S(1)}, s32[32,128]{1,0:T(8,128)S(1)}, u32[]{:S(2)}, u32[]{:S(2)}) collective-permute-start(s32[32,128]{1,0:T(8,128)S(1)} %add_add_fusion), channel_id=1, source_target_pairs={{112,0},{0,16},{16,32},{32,48},{48,64},{64,80},{80,96},{96,112},{1... | collective-permute-start | bytes 49160 | tf_op jit(solution)/shard_map/ppermute | solution.py:294
  1.6 15.5 %collective-permute-start.3 = (s32[32,128]{1,0:T(8,128)S(1)}, s32[32,128]{1,0:T(8,128)S(1)}, u32[]{:S(2)}, u32[]{:S(2)}) collective-permute-start(s32[32,128]{1,0:T(8,128)S(1)} %add_add_fusion), channel_id=1, source_target_pairs={{16,0},{32,16},{48,32},{64,48},{80,64},{96,80},{112,96},{0,112},{1... | collective-permute-start | bytes 49160 | tf_op jit(solution)/shard_map/ppermute | solution.py:294
  5.7 23.3 %collective-permute-start = (bf16[3,192,512]{2,1,0:T(8,128)(2,1)S(1)}, bf16[3,192,512]{2,1,0:T(8,128)(2,1)S(1)}, u32[]{:S(2)}, u32[]{:S(2)}) collective-permute-start(bf16[3,192,512]{2,1,0:T(8,128)(2,1)S(1)} %slice.10), channel_id=1, source_target_pairs={{15,0},{0,1},{1,2},{2,3},{3,4},{4,5},{5,6},{6,7},{7,8},{8,9},{9,10... | collective-permute-start | bytes 1769480 | tf_op jit(solution)/shard_map/ppermute | solution.py:294
  7.4 26.9 %collective-permute-start.1 = (bf16[3,192,512]{2,1,0:T(8,128)(2,1)S(1)}, bf16[3,192,512]{2,1,0:T(8,128)(2,1)S(1)}, u32[]{:S(2)}, u32[]{:S(2)}) collective-permute-start(bf16[3,192,512]{2,1,0:T(8,128)(2,1)S(1)} %slice.10), channel_id=1, source_target_pairs={{1,0},{2,1},{3,2},{4,3},{5,4},{6,5},{7,6},{8,7},{9,8},{10,9},{11,1... | collective-permute-start | bytes 1769480 | tf_op jit(solution)/shard_map/ppermute | solution.py:294
  12.5 2.9 %copy-start.1 = (bf16[289,289]{1,0:T(8,128)(2,1)S(1)}, bf16[289,289]{1,0:T(8,128)(2,1)}, u32[]{:S(2)}) copy-start(bf16[289,289]{1,0:T(8,128)(2,1)} %trans_ref.1) | copy-start | bytes 501130
  12.5 2.9 %copy-start.2 = (bf16[289,289]{1,0:T(8,128)(2,1)S(1)}, bf16[289,289]{1,0:T(8,128)(2,1)}, u32[]{:S(2)}) copy-start(bf16[289,289]{1,0:T(8,128)(2,1)} %self_ref.1) | copy-start | bytes 501130
  15.3 7.2 %copy-start = (bf16[3,289,1,1,512]{4,1,3,2,0:T(8,128)(2,1)S(1)}, bf16[3,289,1,1,512]{4,1,3,2,0:T(8,128)(2,1)}, u32[]{:S(2)}) copy-start(bf16[3,289,1,1,512]{4,1,3,2,0:T(8,128)(2,1)} %param.8) | copy-start | bytes 2663428
  17.1 10.6 %collective-permute-start.4 = (s32[3,32,128]{2,1,0:T(8,128)S(1)}, s32[3,32,128]{2,1,0:T(8,128)S(1)}, u32[]{:S(2)}, u32[]{:S(2)}) collective-permute-start(s32[3,32,128]{2,1,0:T(8,128)S(1)} %pad_add_fusion.refs_3_.refs_1_.refs_2_.refs_4_.refs_5_), channel_id=1, source_target_pairs={{15,0},{0,1},{1,2},{2,3},{3,4},{4,5},{5,6},{6,7},{7,8},{8,9},{9,10... | collective-permute-start | bytes 147464 | tf_op jit(solution)/shard_map/ppermute | solution.py:294
  17.2 10.5 %collective-permute-start.5 = (s32[3,32,128]{2,1,0:T(8,128)S(1)}, s32[3,32,128]{2,1,0:T(8,128)S(1)}, u32[]{:S(2)}, u32[]{:S(2)}) collective-permute-start(s32[3,32,128]{2,1,0:T(8,128)S(1)} %pad_add_fusion.refs_3_.refs_1_.refs_2_.refs_4_.refs_5_), channel_id=1, source_target_pairs={{1,0},{2,1},{3,2},{4,3},{5,4},{6,5},{7,6},{8,7},{9,8},{10,9},{11,1... | collective-permute-start | bytes 147464 | tf_op jit(solution)/shard_map/ppermute | solution.py:294
  28.4 6.8 %collective-permute-start.10 = (bf16[3,289,256]{2,1,0:T(8,128)(2,1)S(1)}, bf16[3,289,256]{2,1,0:T(8,128)(2,1)S(1)}, u32[]{:S(2)}, u32[]{:S(2)}) collective-permute-start(bf16[3,289,256]{2,1,0:T(8,128)(2,1)S(1)} %get-tuple-element.35), channel_id=1, source_target_pairs={{16,0},{32,16},{48,32},{64,48},{80,64},{96,80},{112,96},{0,112},{1... | collective-permute-start | bytes 1331720 | tf_op jit(solution)/shard_map/ppermute | solution.py:294
  28.4 9.1 %collective-permute-start.9 = (bf16[3,289,256]{2,1,0:T(8,128)(2,1)S(1)}, bf16[3,289,256]{2,1,0:T(8,128)(2,1)S(1)}, u32[]{:S(2)}, u32[]{:S(2)}) collective-permute-start(bf16[3,289,256]{2,1,0:T(8,128)(2,1)S(1)} %get-tuple-element.34), channel_id=1, source_target_pairs={{112,0},{0,16},{16,32},{32,48},{48,64},{64,80},{80,96},{96,112},{1... | collective-permute-start | bytes 1331720 | tf_op jit(solution)/shard_map/ppermute | solution.py:294
  28.9 13.8 %collective-permute-start.7 = (bf16[3,97,512]{2,1,0:T(8,128)(2,1)S(1)}, bf16[3,97,512]{2,1,0:T(8,128)(2,1)S(1)}, u32[]{:S(2)}, u32[]{:S(2)}) collective-permute-start(bf16[3,97,512]{2,1,0:T(8,128)(2,1)S(1)} %slice.11), channel_id=1, source_target_pairs={{15,0},{0,1},{1,2},{2,3},{3,4},{4,5},{5,6},{6,7},{7,8},{8,9},{9,10... | collective-permute-start | bytes 893960 | tf_op jit(solution)/shard_map/ppermute | solution.py:294
  29.0 13.7 %collective-permute-start.8 = (bf16[3,97,512]{2,1,0:T(8,128)(2,1)S(1)}, bf16[3,97,512]{2,1,0:T(8,128)(2,1)S(1)}, u32[]{:S(2)}, u32[]{:S(2)}) collective-permute-start(bf16[3,97,512]{2,1,0:T(8,128)(2,1)S(1)} %slice.11), channel_id=1, source_target_pairs={{1,0},{2,1},{3,2},{4,3},{5,4},{6,5},{7,6},{8,7},{9,8},{10,9},{11,1... | collective-permute-start | bytes 893960 | tf_op jit(solution)/shard_map/ppermute | solution.py:294
  43.3 9.0 %collective-permute-start.13 = (bf16[6,97,256]{2,1,0:T(8,128)(2,1)S(1)}, bf16[6,97,256]{2,1,0:T(8,128)(2,1)S(1)}, u32[]{:S(2)}, u32[]{:S(2)}) collective-permute-start(bf16[6,97,256]{2,1,0:T(8,128)(2,1)S(1)} %get-tuple-element.42), channel_id=1, source_target_pairs={{16,0},{32,16},{48,32},{64,48},{80,64},{96,80},{112,96},{0,112},{1... | collective-permute-start | bytes 893960 | tf_op jit(solution)/shard_map/ppermute | solution.py:294
  44.3 10.8 %collective-permute-start.12 = (bf16[6,192,256]{2,1,0:T(8,128)(2,1)S(1)}, bf16[6,192,256]{2,1,0:T(8,128)(2,1)S(1)}, u32[]{:S(2)}, u32[]{:S(2)}) collective-permute-start(bf16[6,192,256]{2,1,0:T(8,128)(2,1)S(1)} %get-tuple-element.36), channel_id=1, source_target_pairs={{16,0},{32,16},{48,32},{64,48},{80,64},{96,80},{112,96},{0,112},{1... | collective-permute-start | bytes 1769480 | tf_op jit(solution)/shard_map/ppermute | solution.py:294
  44.7 7.6 %collective-permute-start.11 = (bf16[6,97,256]{2,1,0:T(8,128)(2,1)S(1)}, bf16[6,97,256]{2,1,0:T(8,128)(2,1)S(1)}, u32[]{:S(2)}, u32[]{:S(2)}) collective-permute-start(bf16[6,97,256]{2,1,0:T(8,128)(2,1)S(1)} %get-tuple-element.41), channel_id=1, source_target_pairs={{112,0},{0,16},{16,32},{32,48},{48,64},{64,80},{80,96},{96,112},{1... | collective-permute-start | bytes 893960 | tf_op jit(solution)/shard_map/ppermute | solution.py:294
  44.9 13.8 %collective-permute-start.6 = (bf16[6,192,256]{2,1,0:T(8,128)(2,1)S(1)}, bf16[6,192,256]{2,1,0:T(8,128)(2,1)S(1)}, u32[]{:S(2)}, u32[]{:S(2)}) collective-permute-start(bf16[6,192,256]{2,1,0:T(8,128)(2,1)S(1)} %get-tuple-element.33), channel_id=1, source_target_pairs={{112,0},{0,16},{16,32},{32,48},{48,64},{64,80},{80,96},{96,112},{1... | collective-permute-start | bytes 1769480 | tf_op jit(solution)/shard_map/ppermute | solution.py:294

commit v4 on v3

--- a/solution.py
+++ b/solution.py
@@ -12,7 +12,6 @@
 
 K = 289
 MAIN = 256
-CUT = 192
 REST = K - MAIN
 TAIL = 128
 WIDE = 3 * MAIN + TAIL
@@ -23,9 +22,12 @@
 PAIR = 2 * SLOTS
 GROUP = 2 * CAP
 ROWS = NR * GROUP
-OWN, PARTNER, ROT, META = 0, 9, 18, 32
+HEAD = 16
+BASE = 32
+OWN, PARTNER, ROT = 0, 2, 4
 COLUMNS = (slice(0, 256), slice(256, 512), slice(512, 768), slice(768, 896))
 VMEM_LIMIT = 28 * 1024 * 1024
+PACK_LIMIT = 62 * 1024 * 1024
 
 
 def nt(a, b):
@@ -123,50 +125,73 @@
         tail[:, 3 * MAIN :] = tail_block(source[MAIN:, MAIN:])
 
 
-def meta_row(metas, dx, dy, row):
-    meta = metas[dy + 1]
-    return meta[dx + 1 if meta.shape[0] == 3 else 0, row : row + 1, :]
-
-
-def pick_kernel(rows, count, *refs):
-    sources, metas = refs[:count], refs[count : count + 3]
-    to_left, to_right = refs[count + 3 :]
-    for i, (source, dy) in enumerate(zip(sources, rows)):
-        for ex, out in ((-1, to_left), (1, to_right)):
+def head_row(ref, first, what, row):
+    def part(number):
+        lanes = slice(number % 4 * SLOTS, (number % 4 + 1) * SLOTS)
+        return ref[first + number // 4, :HEAD, lanes].astype(F32)[row : row + 1]
+
+    if what == ROT:
+        return part(ROT).astype(jnp.int32)
+    return (part(what) * BASE + part(what + 1)).astype(jnp.int32)
+
+
+def head_digits(index):
+    high = index // BASE
+    return high.astype(F32).astype(BF), (index - high * BASE).astype(F32).astype(BF)
+
+
+def pack_kernel(*refs):
+    sources, out, held, done = refs[:5], refs[5], refs[6:11], refs[11]
+    copies = [pltpu.make_async_copy(src, dst, done.at[i]) for i, (src, dst) in enumerate(zip(sources, held))]
+    for copy in copies:
+        copy.start()
+    for copy in copies:
+        copy.wait()
+    count_ref, own_ref, partner_ref, rot_ref, here_ref = held
+    empty = [jnp.zeros((HEAD - 9, SLOTS), jnp.int32)]
+    own = jnp.concatenate([own_ref[o] for o in range(9)] + empty, axis=0)
+    partner = jnp.concatenate([partner_ref[o] for o in range(9)] + empty, axis=0)
+    slot = iota((1, SLOTS), 1)
+    live = [jnp.where(slot < count_ref[0, o], rot_ref[o], NR) for o in range(9)]
+    rot = jnp.concatenate(live + empty, axis=0).astype(F32).astype(BF)
+    out[0, :HEAD, :] = jnp.concatenate(head_digits(own) + head_digits(partner), axis=1)
+    out[1, :HEAD, :] = jnp.concatenate([rot, jnp.zeros((HEAD, CELLS - SLOTS), BF)], axis=1)
+    out[2, :HEAD, :] = jnp.zeros((HEAD, CELLS), BF)
+    for c in range(3):
+        out[c, HEAD:, :] = here_ref[c]
+
+
+def pick_kernel(left, right, high, low, to_left, to_right):
+    for i, (source, dy) in enumerate(((low, -1), (high, 1))):
+        for ex, target, out in ((-1, left, to_left), (1, right, to_right)):
             o = offset_of(-ex, dy)
-            table = pick_table(meta_row(metas, ex, 0, PARTNER + o), meta_row(metas, 0, dy, OWN + 8 - o))
+            table = pick_table(head_row(target, 0, PARTNER, o), head_row(source, 0, OWN, 8 - o))
             for c in range(3):
-                out[3 * i + c] = nn(source[c], table).astype(BF)
-
-
-def column_source(kind, arrays, s, dx, dy):
-    if kind == "here":
-        return [[arrays[0][c]] for c in range(3)]
-    if kind == "sides":
-        return [[arrays[s][c]] for c in range(3)]
-    if kind == "rows":
-        return [[arrays[2 * s][c], arrays[2 * s + 1][c]] for c in range(3)]
-    low, high = arrays[:2] if dx < 0 else arrays[2:]
-    which = 0 if dy < 0 else 3
-    return [[low[which + c], high[which + c]] for c in range(3)]
+                out[3 * i + c, HEAD:, :] = nn(source[c, HEAD:, :], table).astype(BF)
+            digits = [jnp.broadcast_to(d, (HEAD, SLOTS)) for d in head_digits(head_row(source, 0, PARTNER, 8 - o))]
+            rot = jnp.broadcast_to(head_row(source, 0, ROT, 8 - o).astype(F32).astype(BF), (HEAD, SLOTS))
+            out[3 * i, :HEAD, :] = jnp.concatenate(digits, axis=1)
+            out[3 * i + 1, :HEAD, :] = jnp.concatenate([rot, rot], axis=1)
+            out[3 * i + 2, :HEAD, :] = jnp.zeros((HEAD, PAIR), BF)
 
 
 PHASES = {
-    "here": (((0, 0),), 1),
-    "sides": (((-1, 0), (1, 0)), 2),
-    "rows": (((0, -1), (0, 1)), 4),
-    "corners": (((-1, -1), (-1, 1), (1, -1), (1, 1)), 4),
+    "line": ((0, 0), (-1, 0), (1, 0)),
+    "rows": ((0, -1), (0, 1)),
+    "corners": ((-1, -1), (-1, 1), (1, -1), (1, 1)),
 }
 
 
 def phase_kernel(kind, *refs):
-    sources, inputs = PHASES[kind]
-    first, last, whole = kind == "here", kind == "corners", kind in ("here", "rows")
+    sources = PHASES[kind]
+    first, last = kind == "line", kind == "corners"
     m = len(sources)
-    arrays, refs = refs[:inputs], refs[inputs:]
-    metas = refs[:3]
-    rot_ref, rot_tail, trans_main, trans_tail = refs[3:7]
-    refs = refs[7:]
+    mine, refs = refs[0], refs[1:]
+    arrays, refs = refs[:2], refs[2:]
+    if first:
+        arrays = (mine, *arrays)
+    rot_ref, rot_tail, trans_main, trans_tail = refs[:4]
+    refs = refs[4:]
     if first:
         self_main, self_tail = refs[:2]
         refs = refs[2:]
@@ -176,35 +201,39 @@
     out, picked, grouped, turned, places_to = refs[:5]
     acc = refs[5] if last else out
 
-    def slot_rows(dx, dy, mine, theirs):
+    def place_of(s):
+        dx, dy = sources[s]
         o = offset_of(dx, dy)
-        return meta_row(metas, 0, 0, mine + o), meta_row(metas, dx, dy, theirs + 8 - o)
+        if last:
+            return arrays[0 if dx < 0 else 1], (0 if dy < 0 else 3), o, 0
+        return arrays[s], 0, o, 8 - o
+
+    def slot_pair(s, mine_what, their_what):
+        array, start, o, row = place_of(s)
+        if last and their_what == PARTNER:
+            their_what = OWN
+        return head_row(mine, 0, mine_what, o), head_row(array, start, their_what, row)
 
     if first:
         unit = eye(CELLS)
-        here = arrays[0]
-        parts = [nt(unit, here[c, :MAIN, :]).astype(BF) for c in range(3)]
-        parts.append(nt(unit, tail_of([here[c, MAIN:, :] for c in range(3)])).astype(BF))
+        parts = [nt(unit, mine[c, HEAD : HEAD + MAIN, :]).astype(BF) for c in range(3)]
+        parts.append(nt(unit, tail_of([mine[c, HEAD + MAIN :, :] for c in range(3)])).astype(BF))
         for lanes, part in zip(COLUMNS, apply_dense(jnp.concatenate(parts, axis=1), self_main, self_tail)):
             acc[:, lanes] = part
 
     rots = []
-    for dx, dy in sources:
-        rots.extend(slot_rows(dx, dy, ROT, ROT))
+    for s in range(m):
+        rots.extend(slot_pair(s, ROT, ROT))
     places = positions(rots)
 
-    for s, (dx, dy) in enumerate(sources):
-        taken = column_source(kind, arrays, s, dx, dy)
-        if whole:
-            table = pick_table(*slot_rows(dx, dy, PARTNER, OWN))
+    for s in range(m):
+        array, start = place_of(s)[:2]
+        taken = [array[start + c, HEAD:, :] for c in range(3)]
+        if not last:
+            table = pick_table(*slot_pair(s, PARTNER, OWN))
             for c in range(3):
-                start = 0
-                for piece in taken[c]:
-                    picked[c, start : start + piece.shape[0]] = nn(piece, table).astype(BF)
-                    start += piece.shape[0]
+                picked[c] = nn(taken[c], table).astype(BF)
             taken = [picked[c] for c in range(3)]
-        else:
-            taken = [jnp.concatenate(pieces, axis=0) for pieces in taken]
         row_ids = iota((ROWS, SLOTS), 0)
         own_place, partner_place = places[2 * s], places[2 * s + 1]
         place = jnp.concatenate([where_one(row_ids == own_place), where_one(row_ids == partner_place)], axis=1)
@@ -216,11 +245,11 @@
         grouped[:, lanes, 3 * MAIN :] = (
             nt(place, tail_of([t[MAIN:] for t in taken])).astype(BF).reshape(NR, GROUP, TAIL)
         )
-        own_to, partner_to = slot_rows(dx, dy, OWN, PARTNER)
+        own_to, partner_to = slot_pair(s, OWN, PARTNER)
         to = jnp.concatenate([own_to, partner_to], axis=1) + 1
-        digits = jnp.concatenate([to // 32, to % 32, jnp.zeros((6, PAIR), jnp.int32)], axis=0)
+        digits = jnp.concatenate([to // BASE, to % BASE, jnp.zeros((6, PAIR), jnp.int32)], axis=0)
         back = nt(digits.astype(F32).astype(BF), place)
-        goal = (back[0:1] * 32.0 + back[1:2]).astype(jnp.int32) - 1
+        goal = (back[0:1] * BASE + back[1:2]).astype(jnp.int32) - 1
         places_to[:, s * ROWS : (s + 1) * ROWS] = where_one(iota((CELLS, ROWS), 0) == goal)
 
     size = m * GROUP
@@ -261,18 +290,19 @@
             out[c, MAIN:, :] = nt(gather, tail).astype(BF)
 
 
-def vmem_call(kernel, out_shape, scratch=(), flops=0):
+def vmem_call(kernel, out_shape, scratch=(), limit=VMEM_LIMIT, **options):
     return pl.pallas_call(
         kernel,
         out_shape=out_shape,
         scratch_shapes=list(scratch),
-        compiler_params=pltpu.CompilerParams(vmem_limit_bytes=VMEM_LIMIT),
-        cost_estimate=pl.CostEstimate(flops=flops, bytes_accessed=8_000_000, transcendentals=0),
+        compiler_params=pltpu.CompilerParams(vmem_limit_bytes=limit),
+        cost_estimate=pl.CostEstimate(flops=1000, bytes_accessed=1000, transcendentals=0),
+        **options,
     )
 
 
 def phase_call(kind):
-    m, last = len(PHASES[kind][0]), kind == "corners"
+    m, last = len(PHASES[kind]), kind == "corners"
     if last:
         out = jax.ShapeDtypeStruct((3, K, CELLS), BF)
     else:
@@ -286,7 +316,7 @@
     if last:
         scratch.append(pltpu.VMEM((CELLS, WIDE), F32))
     kernel = functools.partial(phase_kernel, kind)
-    return vmem_call(kernel, out, scratch, flops=m * 4_000_000_000)
+    return vmem_call(kernel, out, scratch)
 
 
 def shift(block, axis, distance):
@@ -296,46 +326,38 @@
 
 def local(traction, self_operator, translation, rotations, own_cell, partner_cell, rot_index, block_count):
     here = traction.reshape(3, K, CELLS)
-    live = iota((9, SLOTS), 1) < block_count.reshape(9, 1)
-    rot = jnp.where(live, rot_index.reshape(9, SLOTS), NR)
-    meta = jnp.concatenate(
-        [own_cell.reshape(9, SLOTS), partner_cell.reshape(9, SLOTS), rot, jnp.zeros((META - 27, SLOTS), jnp.int32)]
-    )
-    low_a, high_a = shift(here[:, :CUT], "gy", 1), shift(here[:, :CUT], "gy", -1)
-    low_b, high_b = shift(here[:, CUT:], "gy", 1), shift(here[:, CUT:], "gy", -1)
-    mine = meta[None]
-    meta = jnp.stack([shift(meta, "gx", 1), meta, shift(meta, "gx", -1)])
-    meta_low, meta_high = shift(meta, "gy", 1), shift(meta, "gy", -1)
+    slots = [a.reshape(9, 1, SLOTS) for a in (own_cell, partner_cell, rot_index)]
+    mine = vmem_call(
+        pack_kernel,
+        jax.ShapeDtypeStruct((3, HEAD + K, CELLS), BF),
+        [pltpu.SMEM((1, 9), jnp.int32)]
+        + [pltpu.VMEM((9, 1, SLOTS), jnp.int32)] * 3
+        + [pltpu.VMEM((3, K, CELLS), BF), pltpu.SemaphoreType.DMA((5,))],
+        limit=PACK_LIMIT,
+        in_specs=[pl.BlockSpec(memory_space=pl.ANY)] * 5,
+    )(block_count.reshape(1, 9), *slots, here)
+    left, right = shift(mine, "gx", 1), shift(mine, "gx", -1)
+    high = shift(mine, "gy", -1)
+    low = shift(mine, "gy", 1)
+    after = lax.optimization_barrier
 
     dense = [
         jax.ShapeDtypeStruct((3, MAIN, MAIN + TAIL), BF),
         jax.ShapeDtypeStruct((TAIL, WIDE), BF),
     ]
     rot_tail, *dense = vmem_call(
-        prep_kernel, [jax.ShapeDtypeStruct((NR, TAIL, TAIL), BF)] + dense + dense, flops=100_000_000
+        prep_kernel, [jax.ShapeDtypeStruct((NR, TAIL, TAIL), BF)] + dense + dense
     )(rotations, translation, self_operator)
     weights = (rotations, rot_tail, *dense[:2])
 
-    def pick(sources, rows, metas):
-        picked = jax.ShapeDtypeStruct((3 * len(rows), sources[0].shape[1], PAIR), BF)
-        to_left, to_right = vmem_call(
-            functools.partial(pick_kernel, rows, len(rows)), (picked, picked), flops=1_000_000_000
-        )(*sources, *metas)
-        return to_left, shift(to_right, "gx", 1), shift(to_left, "gx", -1)
-
-    after = lax.optimization_barrier
-    acc = phase_call("here")(here, mine, mine, mine, *weights, *dense[2:])
-    meta, meta_low, meta_high, acc = after((meta, meta_low, meta_high, acc))
-    _, from_left, from_right = pick((here,), (0,), (meta, meta, meta))
-    done, left_a, right_a = pick((low_a, high_a), (-1, 1), (meta_low, meta, meta_high))
-    meta, done = after((meta, done))
-    acc = phase_call("sides")(from_left, from_right, meta, meta, meta, *weights, acc)
-    meta_low, meta_high, acc = after((meta_low, meta_high, acc))
-    done, left_b, right_b = pick((low_b, high_b), (-1, 1), (meta_low, meta, meta_high))
-    meta, done = after((meta, done))
-    metas = (meta_low, meta, meta_high)
-    acc = phase_call("rows")(low_a, low_b, high_a, high_b, *metas, *weights, acc)
-    velocity = phase_call("corners")(left_a, left_b, right_a, right_b, *metas, *weights, acc)
+    acc = phase_call("line")(mine, left, right, *weights, *dense[2:])
+    acc, high, low = after((acc, high, low))
+    picked = jax.ShapeDtypeStruct((6, HEAD + K, PAIR), BF)
+    to_left, to_right = vmem_call(pick_kernel, (picked, picked))(left, right, high, low)
+    far_left, far_right = shift(to_right, "gx", 1), shift(to_left, "gx", -1)
+    to_left, high, low = after((to_left, high, low))
+    acc = phase_call("rows")(mine, low, high, *weights, acc)
+    velocity = phase_call("corners")(mine, far_left, far_right, *weights, acc)
     return velocity.reshape(3, K, 1, 1, CELLS)
 
 

time: 69.7 us -> 59.4 us (0.85); the launches traced: 69.5 us -> 58.5 us
  starting transfers between devices: 23.3 us -> 11.7 us
  waiting for transfers between devices: 9.33 us -> 11.9 us
  local copies, waits for them, and re-layouts: 4.76 us -> 2.8 us
  Pallas kernels: 31 us -> 32 us
  other arithmetic: 0.91 us -> 0 us
    ppermute x14 -> x6, starting transfers between devices: 23.3 us -> 11.7 us  [shift(): lax.ppermute(block, axis, [((i - distance) % count, i) for i in range(cou...]
    ppermute x14 -> x6, waiting for transfers between devices: 9.33 us -> 11.9 us  [shift(): lax.ppermute(block, axis, [((i - distance) % count, i) for i in range(cou...]
    slice x2 -> x0, local copies, waits for them, and re-layouts: 1.12 us -> none  [the longest x1 1.1 us: local(): here[:, :CUT]]
    pallas_call x7 -> x5, Pallas kernels: 29.3 us -> 30.2 us  [the longest x1 10.7 us: local(): velocity = phase_call('corners')(mine, far_left, far_right, *weights, acc)]
    select_n x1 -> x0, other arithmetic: 0.76 us -> none  [local(): rot = jnp.where(live, rot_index.reshape(9, SLOTS), NR)]
    unnamed x8 -> x7, local copies, waits for them, and re-layouts: 3.56 us -> 2.8 us
  transfers between devices with their start and end apart: 14 -> 6, of which waited for: 4 -> 4; matrix products, arithmetic and copies ran while one was open for 6% -> 5% of each run, Pallas kernels for 28% -> 30%
where the time goes in v4:
time: 59.4 us; the launch traced here: 58.5 us
  Pallas kernels  32 us (54%)
  waiting for transfers between devices  11.9 us (20%)
  starting transfers between devices  11.7 us (20%)
  local copies, waits for them, and re-layouts  2.8 us (5%)
    ppermute x6, waiting for transfers between devices, shift(): lax.ppermute(block, axis, [((i - distance) % count, i) for i in range(cou...  11.9 us
    ppermute x6, starting transfers between devices, shift(): lax.ppermute(block, axis, [((i - distance) % count, i) for i in range(cou...  11.7 us
    pallas_call x1, Pallas kernels, local(): velocity = phase_call('corners')(mine, far_left, far_right, *weights, acc)  10.7 us
    pallas_call x1, Pallas kernels, local(): acc = phase_call('line')(mine, left, right, *weights, *dense[2:])  9.74 us
    pallas_call x1, Pallas kernels, local(): acc = phase_call('rows')(mine, low, high, *weights, acc)  6.36 us
    unnamed x7, local copies, waits for them, and re-layouts  2.8 us
    pallas_call x1, Pallas kernels, local(): vmem_call(pack_kernel, jax.ShapeDtypeStruct((3, HEAD + K, CELLS), BF), [p...  2.28 us
    pallas_call x1, Pallas kernels, local(): vmem_call(prep_kernel, [jax.ShapeDtypeStruct((NR, TAIL, TAIL), BF)] + den...  1.73 us
  transfers between devices with their start and end apart: 6, of which 4 were waited for; matrix products, arithmetic and copies ran while one was open for 5% of the time, Pallas kernels for 30%

profile of v4, /device:TPU:0, one launch (start us, length us, event | category | flops | bytes accessed | tf_op | source)
XLA Modules:
  0.0 58.5 jit_solution(12781527069209686566)
XLA Ops:
  0.0 2.3 %shard_map.82.refs_0_ = bf16[3,305,512]{2,1,0:T(8,128)(2,1)} custom-call(s32[1,9]{1,0:T(1,128)} %bitcast.12, s32[9,1,128]{2,1,0:T(1,128)} %bitcast.9, s32[9,1,128]{2,1,0:T(1,128)} %bitcast.10, s32[9,1,128]{2,1,0:T(1,128)} %bitcast.11, bf16[3,289,512]{2,1,0:T(8,128)(2,1)} %bitcast.8), custom_call_target="tpu_custom_call" | custom-call | flops 1000 | bytes 1000 | tf_op jit(solution)/shard_map/pallas_call | solution.py:330
  2.3 0.0 copy-start.1
  2.3 0.0 copy-start.2
  2.3 2.3 %collective-permute-start.1 = (bf16[3,305,512]{2,1,0:T(8,128)(2,1)}, bf16[3,305,512]{2,1,0:T(8,128)(2,1)S(1)}, u32[]{:S(2)}, u32[]{:S(2)}) collective-permute-start(bf16[3,305,512]{2,1,0:T(8,128)(2,1)} %shard_map.82.refs_0_), channel_id=1, source_target_pairs={{16,0},{32,16},{48,32},{64,48},{80,64},{96,80},{112,96},{0,112},{1... | collective-permute-start | bytes 2810888 | tf_op jit(solution)/shard_map/ppermute | solution.py:324
  4.6 0.0 collective-permute-start
  4.6 1.6 %collective-permute-start.3 = (bf16[3,305,512]{2,1,0:T(8,128)(2,1)}, bf16[3,305,512]{2,1,0:T(8,128)(2,1)S(1)}, u32[]{:S(2)}, u32[]{:S(2)}) collective-permute-start(bf16[3,305,512]{2,1,0:T(8,128)(2,1)} %shard_map.82.refs_0_), channel_id=1, source_target_pairs={{15,0},{0,1},{1,2},{2,3},{3,4},{4,5},{5,6},{6,7},{7,8},{8,9},{9,10... | collective-permute-start | bytes 2810888 | tf_op jit(solution)/shard_map/ppermute | solution.py:324
  6.2 4.9 %collective-permute-start.2 = (bf16[3,305,512]{2,1,0:T(8,128)(2,1)}, bf16[3,305,512]{2,1,0:T(8,128)(2,1)S(1)}, u32[]{:S(2)}, u32[]{:S(2)}) collective-permute-start(bf16[3,305,512]{2,1,0:T(8,128)(2,1)} %shard_map.82.refs_0_), channel_id=1, source_target_pairs={{1,0},{2,1},{3,2},{4,3},{5,4},{6,5},{7,6},{8,7},{9,8},{10,9},{11,1... | collective-permute-start | bytes 2810888 | tf_op jit(solution)/shard_map/ppermute | solution.py:324
  11.1 2.8 %copy.10.rot_ref.refs_3_ = bf16[16,289,289]{2,1,0:T(8,128)(2,1)S(1)} copy(bf16[16,289,289]{2,0,1:T(8,128)(2,1)} %param.11) | data formatting | bytes 5345344 | tf_op args[3]
  13.9 0.0 copy-done.1
  13.9 0.0 copy-done.2
  13.9 0.0 copy-start
  13.9 1.7 %shard_map.83 = (bf16[16,128,128]{2,1,0:T(8,128)(2,1)S(1)}, bf16[3,256,384]{2,1,0:T(8,128)(2,1)S(1)}, bf16[128,896]{1,0:T(8,128)(2,1)S(1)}, bf16[3,256,384]{2,1,0:T(8,128)(2,1)S(1)}, bf16[128,896]{1,0:T(8,128)(2,1)S(1)}) custom-call(bf16[16,289,289]{2,1,0:T(8,128)(2,1)S(1)} %copy.10.rot_ref.refs_3_, bf16[289,289]{1,0:T(8,128)(2,1)S(1)} %copy-done.1, ...), custom_call_target="tpu_custom_call" | custom-call | flops 1000 | bytes 1000 | tf_op jit(solution)/shard_map/pallas_call | solution.py:348
  15.7 0.6 %collective-permute-done.1.refs_2_.right = bf16[3,305,512]{2,1,0:T(8,128)(2,1)S(1)} collective-permute-done((bf16[3,305,512]{2,1,0:T(8,128)(2,1)}, bf16[3,305,512]{2,1,0:T(8,128)(2,1)S(1)}, u32[]{:S(2)}, u32[]{:S(2)}) %collective-permute-start.1) | collective-permute-done | bytes 936992 | tf_op jit(solution)/shard_map/ppermute | solution.py:324
  16.3 3.0 %collective-permute-done.refs_1_.left = bf16[3,305,512]{2,1,0:T(8,128)(2,1)S(1)} collective-permute-done((bf16[3,305,512]{2,1,0:T(8,128)(2,1)}, bf16[3,305,512]{2,1,0:T(8,128)(2,1)S(1)}, u32[]{:S(2)}, u32[]{:S(2)}) %collective-permute-start) | collective-permute-done | bytes 936992 | tf_op jit(solution)/shard_map/ppermute | solution.py:324
  19.3 0.0 copy-done
  19.3 9.7 %shard_map.84.refs_7_ = f32[512,896]{1,0:T(8,128)S(1)} custom-call(bf16[3,305,512]{2,1,0:T(8,128)(2,1)S(1)} %copy-done, bf16[3,305,512]{2,1,0:T(8,128)(2,1)S(1)} %collective-permute-done.refs_1_.left, bf16[3,305,512]{2,1,0:T(8,128)(2,1)S(1)} %collective-permute-done.1.refs_2_.right, bf16[16,289,289]{2,1,0:T(8,128)(2,1)S(1)} %copy.10.rot_ref.refs_3_, ...), custom_call_target="tpu_custom_call" | custom-call | flops 1000 | bytes 1000 | tf_op jit(solution)/shard_map/pallas_call | solution.py:353
  29.0 3.1 %collective-permute-done.3.low.refs_1_ = bf16[3,305,512]{2,1,0:T(8,128)(2,1)S(1)} collective-permute-done((bf16[3,305,512]{2,1,0:T(8,128)(2,1)}, bf16[3,305,512]{2,1,0:T(8,128)(2,1)S(1)}, u32[]{:S(2)}, u32[]{:S(2)}) %collective-permute-start.3) | collective-permute-done | bytes 936992 | tf_op jit(solution)/shard_map/ppermute | solution.py:324
  32.2 0.0 collective-permute-done.2.high.refs_2_
  32.2 1.1 %shard_map.85 = (bf16[6,305,256]{2,1,0:T(8,128)(2,1)S(1)}, bf16[6,305,256]{2,1,0:T(8,128)(2,1)S(1)}) custom-call(bf16[3,305,512]{2,1,0:T(8,128)(2,1)S(1)} %collective-permute-done.refs_1_.left, bf16[3,305,512]{2,1,0:T(8,128)(2,1)S(1)} %collective-permute-done.1.refs_2_.right, bf16[3,305,512]{2,1,0:T(8,128)(2,1)S(1)} %collective-permute-done.2.high.refs_2_, ...), custom_call_target="tpu_custom_call" | custom-call | flops 1000 | bytes 1000 | tf_op jit(solution)/shard_map/pallas_call | solution.py:356
  33.3 0.0 collective-permute-start.4
  33.3 2.9 %collective-permute-start.5 = (bf16[6,305,256]{2,1,0:T(8,128)(2,1)S(1)}, bf16[6,305,256]{2,1,0:T(8,128)(2,1)S(1)}, u32[]{:S(2)}, u32[]{:S(2)}) collective-permute-start(bf16[6,305,256]{2,1,0:T(8,128)(2,1)S(1)} %get-tuple-element.25), channel_id=1, source_target_pairs={{16,0},{32,16},{48,32},{64,48},{80,64},{96,80},{112,96},{0,112},{1... | collective-permute-start | bytes 2810888 | tf_op jit(solution)/shard_map/ppermute | solution.py:324
  36.3 6.4 %shard_map.86.refs_7_ = f32[512,896]{1,0:T(8,128)S(1)} custom-call(bf16[3,305,512]{2,1,0:T(8,128)(2,1)S(1)} %copy-done, bf16[3,305,512]{2,1,0:T(8,128)(2,1)S(1)} %collective-permute-done.3.low.refs_1_, bf16[3,305,512]{2,1,0:T(8,128)(2,1)S(1)} %collective-permute-done.2.high.refs_2_, bf16[16,289,289]{2,1,0:T(8,128)(2,1)S(1)} %copy.10.rot_ref.refs_3_, ...), custom_call_target="tpu_custom_call" | custom-call | flops 1000 | bytes 1000 | tf_op jit(solution)/shard_map/pallas_call | solution.py:359
  42.7 5.1 %collective-permute-done.4.refs_1_ = bf16[6,305,256]{2,1,0:T(8,128)(2,1)S(1)} collective-permute-done((bf16[6,305,256]{2,1,0:T(8,128)(2,1)S(1)}, bf16[6,305,256]{2,1,0:T(8,128)(2,1)S(1)}, u32[]{:S(2)}, u32[]{:S(2)}) %collective-permute-start.4) | collective-permute-done | bytes 936992 | tf_op jit(solution)/shard_map/ppermute | solution.py:324
  47.8 0.0 collective-permute-done.5.refs_2_
  47.8 10.7 %shard_map.87 = bf16[3,289,512]{2,1,0:T(8,128)(2,1)} custom-call(bf16[3,305,512]{2,1,0:T(8,128)(2,1)S(1)} %copy-done, bf16[6,305,256]{2,1,0:T(8,128)(2,1)S(1)} %collective-permute-done.4.refs_1_, bf16[6,305,256]{2,1,0:T(8,128)(2,1)S(1)} %collective-permute-done.5.refs_2_, bf16[16,289,289]{2,1,0:T(8,128)(2,1)S(1)} %copy.10.rot_ref.refs_3_, ...), custom_call_target="tpu_custom_call" | custom-call | flops 1000 | bytes 1000 | tf_op jit(solution)/shard_map/pallas_call | solution.py:360
Async XLA Ops:
  2.3 11.6 %copy-start.1 = (bf16[289,289]{1,0:T(8,128)(2,1)S(1)}, bf16[289,289]{1,0:T(8,128)(2,1)}, u32[]{:S(2)}) copy-start(bf16[289,289]{1,0:T(8,128)(2,1)} %trans_ref.1) | copy-start | bytes 501130
  2.3 11.6 %copy-start.2 = (bf16[289,289]{1,0:T(8,128)(2,1)S(1)}, bf16[289,289]{1,0:T(8,128)(2,1)}, u32[]{:S(2)}) copy-start(bf16[289,289]{1,0:T(8,128)(2,1)} %self_ref.1) | copy-start | bytes 501130
  2.3 14.0 %collective-permute-start.1 = (bf16[3,305,512]{2,1,0:T(8,128)(2,1)}, bf16[3,305,512]{2,1,0:T(8,128)(2,1)S(1)}, u32[]{:S(2)}, u32[]{:S(2)}) collective-permute-start(bf16[3,305,512]{2,1,0:T(8,128)(2,1)} %shard_map.82.refs_0_), channel_id=1, source_target_pairs={{16,0},{32,16},{48,32},{64,48},{80,64},{96,80},{112,96},{0,112},{1... | collective-permute-start | bytes 2810888 | tf_op jit(solution)/shard_map/ppermute | solution.py:324
  4.6 14.7 %collective-permute-start = (bf16[3,305,512]{2,1,0:T(8,128)(2,1)}, bf16[3,305,512]{2,1,0:T(8,128)(2,1)S(1)}, u32[]{:S(2)}, u32[]{:S(2)}) collective-permute-start(bf16[3,305,512]{2,1,0:T(8,128)(2,1)} %shard_map.82.refs_0_), channel_id=1, source_target_pairs={{112,0},{0,16},{16,32},{32,48},{48,64},{64,80},{80,96},{96,112},{1... | collective-permute-start | bytes 2810888 | tf_op jit(solution)/shard_map/ppermute | solution.py:324
  4.6 27.6 %collective-permute-start.3 = (bf16[3,305,512]{2,1,0:T(8,128)(2,1)}, bf16[3,305,512]{2,1,0:T(8,128)(2,1)S(1)}, u32[]{:S(2)}, u32[]{:S(2)}) collective-permute-start(bf16[3,305,512]{2,1,0:T(8,128)(2,1)} %shard_map.82.refs_0_), channel_id=1, source_target_pairs={{15,0},{0,1},{1,2},{2,3},{3,4},{4,5},{5,6},{6,7},{7,8},{8,9},{9,10... | collective-permute-start | bytes 2810888 | tf_op jit(solution)/shard_map/ppermute | solution.py:324
  6.2 26.0 %collective-permute-start.2 = (bf16[3,305,512]{2,1,0:T(8,128)(2,1)}, bf16[3,305,512]{2,1,0:T(8,128)(2,1)S(1)}, u32[]{:S(2)}, u32[]{:S(2)}) collective-permute-start(bf16[3,305,512]{2,1,0:T(8,128)(2,1)} %shard_map.82.refs_0_), channel_id=1, source_target_pairs={{1,0},{2,1},{3,2},{4,3},{5,4},{6,5},{7,6},{8,7},{9,8},{10,9},{11,1... | collective-permute-start | bytes 2810888 | tf_op jit(solution)/shard_map/ppermute | solution.py:324
  13.9 5.4 %copy-start = (bf16[3,305,512]{2,1,0:T(8,128)(2,1)S(1)}, bf16[3,305,512]{2,1,0:T(8,128)(2,1)}, u32[]{:S(2)}) copy-start(bf16[3,305,512]{2,1,0:T(8,128)(2,1)} %shard_map.82.refs_0_) | copy-start | bytes 2810884
  33.3 14.5 %collective-permute-start.4 = (bf16[6,305,256]{2,1,0:T(8,128)(2,1)S(1)}, bf16[6,305,256]{2,1,0:T(8,128)(2,1)S(1)}, u32[]{:S(2)}, u32[]{:S(2)}) collective-permute-start(bf16[6,305,256]{2,1,0:T(8,128)(2,1)S(1)} %get-tuple-element.24), channel_id=1, source_target_pairs={{112,0},{0,16},{16,32},{32,48},{48,64},{64,80},{80,96},{96,112},{1... | collective-permute-start | bytes 2810888 | tf_op jit(solution)/shard_map/ppermute | solution.py:324
  33.3 14.5 %collective-permute-start.5 = (bf16[6,305,256]{2,1,0:T(8,128)(2,1)S(1)}, bf16[6,305,256]{2,1,0:T(8,128)(2,1)S(1)}, u32[]{:S(2)}, u32[]{:S(2)}) collective-permute-start(bf16[6,305,256]{2,1,0:T(8,128)(2,1)S(1)} %get-tuple-element.25), channel_id=1, source_target_pairs={{16,0},{32,16},{48,32},{64,48},{80,64},{96,80},{112,96},{0,112},{1... | collective-permute-start | bytes 2810888 | tf_op jit(solution)/shard_map/ppermute | solution.py:324

commit v5 on v4

v5 whole, which is shorter than its diff:
```python
import functools

import jax
import jax.numpy as jnp
from jax import lax
from jax.experimental import pallas as pl
from jax.experimental.pallas import tpu as pltpu
from jax.sharding import PartitionSpec as P

BF = jnp.bfloat16
F32 = jnp.float32

K = 289
MAIN = 256
REST = K - MAIN
TAIL = 128
WIDE = 3 * MAIN + TAIL
CELLS = 512
SLOTS = 128
NR = 16
CAP = 16
PAIR = 2 * SLOTS
GROUP = 2 * CAP
ROWS = NR * GROUP
HEAD = 16
HEAD_AT = WIDE - HEAD
BASE = 32
OWN, PARTNER = 0, 2
ROT = 9
ODD = 12
COLUMNS = (slice(0, 256), slice(256, 512), slice(512, 768), slice(768, 896))
VMEM_LIMIT = 28 * 1024 * 1024
HERE_COST = 30_000_000_000
PACK_LIMIT = 62 * 1024 * 1024


def nt(a, b):
    return lax.dot_general(a, b, (((1,), (1,)), ((), ())), preferred_element_type=F32)


def nn(a, b):
    return jnp.dot(a, b, preferred_element_type=F32)


def iota(shape, dim):
    return lax.broadcasted_iota(jnp.int32, shape, dim)


def where_one(condition):
    return jnp.where(condition, 1.0, 0.0).astype(BF)


def eye(size):
    return where_one(iota((size, size), 0) == iota((size, size), 1))


def spread(c):
    return where_one(iota((TAIL, REST), 0) == iota((TAIL, REST), 1) + c * REST)


def offset_of(dx, dy):
    return (dx + 1) * 3 + dy + 1


def offsets(side, dy):
    return offset_of(side, dy), offset_of(-side, dy)


def choose(even, side, dy, read, theirs=False):
    first, second = [8 - o if theirs else o for o in offsets(side, dy)]
    return read(first) if first == second else jnp.where(even, read(first), read(second))


def parity_lanes(width, start):
    k = iota((1, width), 1) + start
    degree = jnp.zeros((1, width), jnp.int32)
    for level in range(1, 17):
        degree = degree + jnp.where(k >= level * level, 1, 0)
    return 1.0 - 2.0 * (degree % 2).astype(F32)


def side_signs(width, start):
    signs = jnp.broadcast_to(parity_lanes(width, start), (GROUP, width))
    return jnp.where(iota((GROUP, width), 0) >= CAP, signs, 1.0)


def pick_table(own_side, partner_side):
    cells = iota((CELLS, SLOTS), 0)
    return jnp.concatenate([where_one(cells == own_side), where_one(cells == partner_side)], axis=1)


def positions(rots):
    marks = [where_one(iota((NR, SLOTS), 0) == rot) for rot in rots]
    earlier = where_one(iota((SLOTS, SLOTS), 0) < iota((SLOTS, SLOTS), 1))
    ranks = nn(jnp.concatenate(marks, axis=0), earlier)
    places = []
    for j, mark in enumerate(marks):
        base = (iota((NR, SLOTS), 0) * GROUP + (j % 2) * CAP + 1).astype(F32)
        values = mark.astype(F32) * (ranks[j * NR : (j + 1) * NR] + base)
        places.append(jnp.sum(values, axis=0, keepdims=True).astype(jnp.int32) - 1)
    return places


def apply_dense(block, main_ref, tail_ref):
    tail = block[:, 3 * MAIN :]
    outs = [
        nt(jnp.concatenate([block[:, c * MAIN : (c + 1) * MAIN], tail], axis=1), main_ref[c]) for c in range(3)
    ]
    return outs + [nt(block, tail_ref[...])]


def split_lanes(block):
    return [block[:, c * MAIN : (c + 1) * MAIN] for c in range(3)], block[:, 3 * MAIN :]


def prep_kernel(rot_ref, trans_ref, self_ref, rot_tail, *pieces):
    fold = where_one((iota((TAIL, REST), 0) % REST == iota((TAIL, REST), 1)) & (iota((TAIL, REST), 0) < 3 * REST))
    same = (iota((TAIL, TAIL), 0) // REST) == (iota((TAIL, TAIL), 1) // REST)

    def tail_block(block):
        return jnp.where(same, nt(nn(fold, block).astype(BF), fold), 0.0).astype(BF)

    for r in range(NR):
        rot_tail[r] = tail_block(rot_ref[r, MAIN:, MAIN:])
    for source, (main, tail) in ((trans_ref, pieces[:2]), (self_ref, pieces[2:])):
        for c in range(3):
            main[c, :, :MAIN] = source[:MAIN, :MAIN]
            main[c, :, MAIN:] = nt(source[:MAIN, MAIN:], spread(c)).astype(BF)
            tail[:, c * MAIN : (c + 1) * MAIN] = nn(spread(c), source[MAIN:, :MAIN]).astype(BF)
        tail[:, 3 * MAIN :] = tail_block(source[MAIN:, MAIN:])


def head_part(ref, at, row, block):
    lanes = slice(block * SLOTS, (block + 1) * SLOTS)
    return ref[at : at + HEAD, lanes].astype(F32)[row : row + 1]


def head_cells(ref, what, row, at=HEAD_AT):
    return (head_part(ref, at, row, what) * BASE + head_part(ref, at, row, what + 1)).astype(jnp.int32)


def head_rots(ref, o):
    return head_part(ref, HEAD_AT, ROT + o // 4, o % 4).astype(jnp.int32)


def is_even(mine):
    return head_part(mine, HEAD_AT, ODD, 0) < 0.5


def head_digits(index):
    high = index // BASE
    return high.astype(F32).astype(BF), (index - high * BASE).astype(F32).astype(BF)


def pack_kernel(count_ref, own_ref, partner_ref, rot_ref, here_ref, out, *scratch):
    held, tail, arrived, sent = scratch[:5], scratch[5], scratch[6], scratch[7]
    copies = [
        pltpu.make_async_copy(src, dst, arrived.at[i])
        for i, (src, dst) in enumerate(zip((count_ref, own_ref, partner_ref, rot_ref, here_ref), held))
    ]
    for copy in copies:
        copy.start()
    for copy in copies:
        copy.wait()
    count, own, partner, rot, here = held
    mains = [
        pltpu.make_async_copy(here.at[c, :MAIN], out.at[c * MAIN : (c + 1) * MAIN], sent.at[c]) for c in range(3)
    ]
    for copy in mains:
        copy.start()
    rest = nn(spread(0), here[0, MAIN:]) + nn(spread(1), here[1, MAIN:]) + nn(spread(2), here[2, MAIN:])
    tail[...] = rest.astype(BF)
    cells = [jnp.concatenate([ref[o] for o in range(9)], axis=0) for ref in (own, partner)]
    digits = jnp.concatenate([d.astype(F32) for index in cells for d in head_digits(index)], axis=1)
    slot = iota((1, SLOTS), 1)
    live = [jnp.where(slot < count[0, o], rot[o], NR).astype(F32) for o in range(9)]
    live.extend([jnp.zeros((1, SLOTS), F32)] * 3)
    rots = [jnp.concatenate(live[4 * i : 4 * i + 4], axis=1) for i in range(3)]
    odd = lax.rem(lax.axis_index("gx"), 2)
    rows = iota((HEAD - ODD, CELLS), 0)
    flags = jnp.where((rows == 0) & (rows + odd > 0), 1.0, 0.0)
    tail[TAIL - HEAD :] = jnp.concatenate([digits, *rots, flags], axis=0).astype(BF)
    last = pltpu.make_async_copy(tail, out.at[3 * MAIN :], sent.at[3])
    last.start()
    for copy in mains + [last]:
        copy.wait()


def pick_kernel(mine, near, off, high, low, to_near, to_off):
    even = is_even(mine)
    for i, (source, dy) in enumerate(((low, -1), (high, 1))):
        for side, target, out in ((-1, near, to_near), (1, off, to_off)):
            wanted = choose(even, side, dy, lambda o: head_cells(target, PARTNER, o))
            owners = choose(even, side, dy, lambda o: head_cells(source, OWN, o), True)
            out[i * WIDE : (i + 1) * WIDE] = nn(source[...], pick_table(wanted, owners)).astype(BF)
            digits = head_digits(choose(even, side, dy, lambda o: head_cells(source, PARTNER, o), True))
            cells = jnp.concatenate([d.astype(F32) for d in digits], axis=1)
            rot = choose(even, side, dy, lambda o: head_rots(source, o), True).astype(F32)
            row = iota((HEAD, PAIR), 0)
            head = jnp.where(row == 0, cells, jnp.where(row == 1, jnp.concatenate([rot, rot], axis=1), 0.0))
            out[i * WIDE + HEAD_AT : (i + 1) * WIDE] = head.astype(BF)


PHASES = {
    "here": ((0, 0),),
    "sides": ((1, 0), (-1, 0)),
    "middle": ((0, -1), (0, 1), (1, -1), (1, 1)),
    "end": ((-1, -1), (-1, 1)),
}


def phase_kernel(kind, *refs):
    sources = PHASES[kind]
    first, last = kind == "here", kind == "end"
    m = len(sources)
    mine = refs[0]
    even = is_even(mine)
    count = {"here": 1, "sides": 3, "middle": 4, "end": 2}[kind]
    arrays, refs = refs[:count], refs[count:]
    rot_ref, rot_tail, trans_main, trans_tail = refs[:4]
    refs = refs[4:]
    if first:
        self_main, self_tail = refs[:2]
        refs = refs[2:]
    else:
        acc_in = refs[0]
        refs = refs[1:]
    out, grouped, turned, places_to = refs[:4]
    sums = refs[4] if last else out

    def forwarded(s):
        side, dy = sources[s]
        return side and dy

    def other(s):
        side, dy = sources[s]
        if forwarded(s):
            return arrays[-1], (0 if dy < 0 else WIDE)
        return arrays[s if first else s + 1], 0

    def cell_pair(s, mine_what, their_what):
        array, start = other(s)
        ours = choose(even, *sources[s], lambda o: head_cells(mine, mine_what, o))
        if forwarded(s):
            return ours, head_cells(array, OWN, 0, start + HEAD_AT)
        return ours, choose(even, *sources[s], lambda o: head_cells(array, their_what, o), True)

    def rot_pair(s):
        array, start = other(s)
        ours = choose(even, *sources[s], lambda o: head_rots(mine, o))
        if forwarded(s):
            return ours, head_part(array, start + HEAD_AT, 1, 0).astype(jnp.int32)
        return ours, choose(even, *sources[s], lambda o: head_rots(array, o), True)

    if first:
        rows = nt(eye(CELLS), mine[...]).astype(BF)
        for lanes, part in zip(COLUMNS, apply_dense(rows, self_main, self_tail)):
            out[:, lanes] = part

    rots = []
    for s in range(m):
        rots.extend(rot_pair(s))
    places = positions(rots)

    for s in range(m):
        array, start = other(s)
        if forwarded(s):
            taken = array[start : start + WIDE]
        else:
            table = pick_table(*cell_pair(s, PARTNER, OWN))
            taken = nn(array[...], table).astype(BF)
        row_ids = iota((ROWS, SLOTS), 0)
        own_place, partner_place = places[2 * s], places[2 * s + 1]
        place = jnp.concatenate([where_one(row_ids == own_place), where_one(row_ids == partner_place)], axis=1)
        lanes = slice(s * GROUP, (s + 1) * GROUP)
        grouped[:, lanes, :] = nt(place, taken).astype(BF).reshape(NR, GROUP, WIDE)
        own_to, partner_to = cell_pair(s, OWN, PARTNER)
        to = jnp.concatenate([own_to, partner_to], axis=1) + 1
        digits = jnp.concatenate([to // BASE, to % BASE, jnp.zeros((6, PAIR), jnp.int32)], axis=0)
        back = nt(digits.astype(F32).astype(BF), place)
        goal = (back[0:1] * BASE + back[1:2]).astype(jnp.int32) - 1
        places_to[:, s * ROWS : (s + 1) * ROWS] = where_one(iota((CELLS, ROWS), 0) == goal)

    size = m * GROUP
    main_signs = side_signs(MAIN, 0)
    tail_signs = side_signs(TAIL, MAIN)

    def turn(r, source, target, dot):
        block = source[r]
        mains, tail = split_lanes(block)
        turned_main = dot(jnp.concatenate(mains, axis=0), rot_ref[r, :MAIN, :MAIN])
        turned_main = (turned_main.reshape(3 * m, GROUP, MAIN) * main_signs[None]).reshape(3 * size, MAIN)
        for c in range(3):
            target[r, :, c * MAIN : (c + 1) * MAIN] = turned_main[c * size : (c + 1) * size].astype(BF)
        target[r, :, 3 * MAIN :] = dot(tail, rot_tail[r]).astype(BF)

    for r in range(NR):
        turn(r, grouped, turned, nt)

    block = turned[...].reshape(NR * size, WIDE)
    for lanes, part in zip(COLUMNS, apply_dense(block, trans_main, trans_tail)):
        grouped[:, :, lanes] = part.astype(BF).reshape(NR, size, lanes.stop - lanes.start)

    for r in range(NR):
        turn(r, grouped, turned, nn)

    for lanes in COLUMNS:
        width = lanes.stop - lanes.start
        back = [turned[:, s * GROUP : (s + 1) * GROUP, lanes].reshape(ROWS, width) for s in range(m)]
        total = nn(places_to[...], jnp.concatenate(back, axis=0))
        sums[:, lanes] = total + (sums[:, lanes] if first else acc_in[:, lanes])
    if last:
        tail = sums[:, 3 * MAIN :].astype(BF)
        unit = eye(MAIN)
        for c in range(3):
            out[c, :MAIN, :] = nt(unit, sums[:, c * MAIN : (c + 1) * MAIN].astype(BF)).astype(BF)
            gather = where_one(iota((REST, TAIL), 1) == iota((REST, TAIL), 0) + c * REST)
            out[c, MAIN:, :] = nt(gather, tail).astype(BF)


def vmem_call(kernel, out_shape, scratch=(), limit=VMEM_LIMIT, cost=1000, **options):
    return pl.pallas_call(
        kernel,
        out_shape=out_shape,
        scratch_shapes=list(scratch),
        compiler_params=pltpu.CompilerParams(vmem_limit_bytes=limit),
        cost_estimate=pl.CostEstimate(flops=cost, bytes_accessed=1000, transcendentals=0),
        **options,
    )


def phase_call(kind):
    m, last = len(PHASES[kind]), kind == "end"
    if last:
        out = jax.ShapeDtypeStruct((3, K, CELLS), BF)
    else:
        out = jax.ShapeDtypeStruct((CELLS, WIDE), F32)
    scratch = [
        pltpu.VMEM((NR, m * GROUP, WIDE), BF),
        pltpu.VMEM((NR, m * GROUP, WIDE), BF),
        pltpu.VMEM((CELLS, m * ROWS), BF),
    ]
    if last:
        scratch.append(pltpu.VMEM((CELLS, WIDE), F32))
    cost = HERE_COST if kind == "here" else 1000
    return vmem_call(functools.partial(phase_kernel, kind), out, scratch, cost=cost)


def swap(block, first):
    count = lax.axis_size("gx")
    return lax.ppermute(block, "gx", [(i, (i + (first if i % 2 == 0 else -first)) % count) for i in range(count)])


def shift(block, axis, distance):
    count = lax.axis_size(axis)
    return lax.ppermute(block, axis, [((i - distance) % count, i) for i in range(count)])


def local(traction, self_operator, translation, rotations, own_cell, partner_cell, rot_index, block_count):
    here = traction.reshape(3, K, CELLS)
    slots = [a.reshape(9, 1, SLOTS) for a in (own_cell, partner_cell, rot_index)]
    there = pl.BlockSpec(memory_space=pl.ANY)
    mine = vmem_call(
        pack_kernel,
        jax.ShapeDtypeStruct((WIDE, CELLS), BF),
        [pltpu.SMEM((1, 9), jnp.int32)]
        + [pltpu.VMEM((9, 1, SLOTS), jnp.int32)] * 3
        + [pltpu.VMEM((3, K, CELLS), BF), pltpu.VMEM((TAIL, CELLS), BF)]
        + [pltpu.SemaphoreType.DMA((5,)), pltpu.SemaphoreType.DMA((4,))],
        limit=PACK_LIMIT,
        in_specs=[there] * 5,
        out_specs=there,
    )(block_count.reshape(1, 9), *slots, here)
    after = lax.optimization_barrier
    near, off = swap(mine, 1), swap(mine, -1)
    high, low = shift(mine, "gy", -1), shift(mine, "gy", 1)

    dense = [
        jax.ShapeDtypeStruct((3, MAIN, MAIN + TAIL), BF),
        jax.ShapeDtypeStruct((TAIL, WIDE), BF),
    ]
    rot_tail, *dense = vmem_call(
        prep_kernel, [jax.ShapeDtypeStruct((NR, TAIL, TAIL), BF)] + dense + dense
    )(rotations, translation, self_operator)
    weights = (rotations, rot_tail, *dense[:2])

    acc = phase_call("here")(mine, *weights, *dense[2:])
    acc = phase_call("sides")(mine, near, off, *weights, acc)
    acc, high, low = after((acc, high, low))
    picked = jax.ShapeDtypeStruct((2 * WIDE, PAIR), BF)
    to_near, to_off = vmem_call(pick_kernel, (picked, picked))(mine, near, off, high, low)
    far_near, far_off = swap(to_near, 1), swap(to_off, -1)
    acc = phase_call("middle")(mine, low, high, far_near, *weights, acc)
    velocity = phase_call("end")(mine, far_off, *weights, acc)
    return velocity.reshape(3, K, 1, 1, CELLS)


def solution(mesh):
    return jax.shard_map(
        local,
        mesh=mesh,
        in_specs=(
            P(None, None, "gx", "gy", None),
            P(),
            P(),
            P(),
            P("gx", "gy", None, None),
            P("gx", "gy", None, None),
            P("gx", "gy", None, None, None),
            P("gx", "gy", None),
        ),
        out_specs=P(None, None, "gx", "gy", None),
        check_vma=False,
    )
```

time: 59.4 us -> 52 us (0.88)
  waiting for transfers between devices: 11.9 us -> 4.32 us
    ppermute x6 -> x2, waiting for transfers between devices: 11.9 us -> 0.17 us  [shift(): lax.ppermute(block, axis, [((i - distance) % count, i) for i in range(cou...]
    ppermute x0 -> x4, starting transfers between devices: none -> 5.04 us  [swap(): lax.ppermute(block, 'gx', [(i, (i + (first if i % 2 == 0 else -first)) %...]
    ppermute x6 -> x2, starting transfers between devices: 11.7 us -> 6.72 us  [shift(): lax.ppermute(block, axis, [((i - distance) % count, i) for i in range(cou...]
    ppermute x0 -> x4, waiting for transfers between devices: none -> 4.15 us  [swap(): lax.ppermute(block, 'gx', [(i, (i + (first if i % 2 == 0 else -first)) %...]
    pallas_call x5 -> x6, Pallas kernels: 30.2 us -> 30.6 us  [the longest x1 9.87 us: local(): acc = phase_call('middle')(mine, low, high, far_near, *weights, acc)]
  transfers between devices with their start and end apart: 6 -> 6, of which waited for: 4 -> 3; matrix products, arithmetic and copies ran while one was open for 5% -> 5% of each run, Pallas kernels for 30% -> 44%
where the time goes in v5:
time: 52 us; the launch traced here: 51.3 us
  Pallas kernels  32.4 us (62%)
  starting transfers between devices  11.8 us (23%)
  waiting for transfers between devices  4.32 us (8%)
  local copies, waits for them, and re-layouts  2.8 us (5%)
    pallas_call x1, Pallas kernels, local(): acc = phase_call('middle')(mine, low, high, far_near, *weights, acc)  9.87 us
    ppermute x2, starting transfers between devices, shift(): lax.ppermute(block, axis, [((i - distance) % count, i) for i in range(cou...  6.72 us
    pallas_call x1, Pallas kernels, local(): velocity = phase_call('end')(mine, far_off, *weights, acc)  6.36 us
    pallas_call x1, Pallas kernels, local(): acc = phase_call('sides')(mine, near, off, *weights, acc)  6.06 us
    ppermute x4, starting transfers between devices, swap(): lax.ppermute(block, 'gx', [(i, (i + (first if i % 2 == 0 else -first)) %...  5.04 us
    pallas_call x1, Pallas kernels, local(): acc = phase_call('here')(mine, *weights, *dense[2:])  4.98 us
    ppermute x4, waiting for transfers between devices, swap(): lax.ppermute(block, 'gx', [(i, (i + (first if i % 2 == 0 else -first)) %...  4.15 us
    unnamed x7, local copies, waits for them, and re-layouts  2.8 us
  transfers between devices with their start and end apart: 6, of which 3 were waited for; matrix products, arithmetic and copies ran while one was open for 5% of the time, Pallas kernels for 44%

profile of v5, /device:TPU:0, one launch (start us, length us, event | category | flops | bytes accessed | tf_op | source)
XLA Modules:
  0.0 51.3 jit_solution(15746277885284772763)
XLA Ops:
  0.0 2.2 %shard_map.82.refs_0_.mine = bf16[896,512]{1,0:T(8,128)(2,1)} custom-call(s32[1,9]{1,0:T(1,128)} %bitcast.12, s32[9,1,128]{2,1,0:T(1,128)} %bitcast.9, s32[9,1,128]{2,1,0:T(1,128)} %bitcast.10, s32[9,1,128]{2,1,0:T(1,128)} %bitcast.11, bf16[3,289,512]{2,1,0:T(8,128)(2,1)} %bitcast.8), custom_call_target="tpu_custom_call" | custom-call | flops 1000 | bytes 1000 | tf_op jit(solution)/shard_map/pallas_call | solution.py:363
  2.2 0.0 copy-start.1
  2.3 0.0 copy-start.2
  2.3 1.7 %collective-permute-start.3 = (bf16[896,512]{1,0:T(8,128)(2,1)}, bf16[896,512]{1,0:T(8,128)(2,1)S(1)}, u32[]{:S(2)}, u32[]{:S(2)}) collective-permute-start(bf16[896,512]{1,0:T(8,128)(2,1)} %shard_map.82.refs_0_.mine), channel_id=1, source_target_pairs={{15,0},{0,1},{1,2},{2,3},{3,4},{4,5},{5,6},{6,7},{7,8},{8,9},{9,10... | collective-permute-start | bytes 2752520 | tf_op jit(solution)/shard_map/ppermute | solution.py:356
  4.0 5.0 %collective-permute-start.2 = (bf16[896,512]{1,0:T(8,128)(2,1)}, bf16[896,512]{1,0:T(8,128)(2,1)S(1)}, u32[]{:S(2)}, u32[]{:S(2)}) collective-permute-start(bf16[896,512]{1,0:T(8,128)(2,1)} %shard_map.82.refs_0_.mine), channel_id=1, source_target_pairs={{1,0},{2,1},{3,2},{4,3},{5,4},{6,5},{7,6},{8,7},{9,8},{10,9},{11,1... | collective-permute-start | bytes 2752520 | tf_op jit(solution)/shard_map/ppermute | solution.py:356
  9.0 1.9 %collective-permute-start.1 = (bf16[896,512]{1,0:T(8,128)(2,1)}, bf16[896,512]{1,0:T(8,128)(2,1)S(1)}, u32[]{:S(2)}, u32[]{:S(2)}) collective-permute-start(bf16[896,512]{1,0:T(8,128)(2,1)} %shard_map.82.refs_0_.mine), channel_id=1, source_target_pairs={{0,112},{16,32},{32,16},{48,64},{64,48},{80,96},{96,80},{112,0},{1... | collective-permute-start | bytes 2752520 | tf_op jit(solution)/shard_map/ppermute | solution.py:351
  10.9 0.0 collective-permute-start
  10.9 2.8 %copy.11.rot_ref.refs_1_.refs_3_.refs_4_.refs_2_ = bf16[16,289,289]{2,1,0:T(8,128)(2,1)S(1)} copy(bf16[16,289,289]{2,0,1:T(8,128)(2,1)} %param.11) | data formatting | bytes 5345344 | tf_op args[3]
  13.7 0.0 copy-done.1
  13.7 0.0 copy-done.2
  13.7 0.0 copy-start
  13.7 1.7 %shard_map.83 = (bf16[16,128,128]{2,1,0:T(8,128)(2,1)S(1)}, bf16[3,256,384]{2,1,0:T(8,128)(2,1)S(1)}, bf16[128,896]{1,0:T(8,128)(2,1)S(1)}, bf16[3,256,384]{2,1,0:T(8,128)(2,1)S(1)}, bf16[128,896]{1,0:T(8,128)(2,1)S(1)}) custom-call(bf16[16,289,289]{2,1,0:T(8,128)(2,1)S(1)} %copy.11.rot_ref.refs_1_.refs_3_.refs_4_.refs_2_, bf16[289,289]{1,0:T(8,128)(2,1)S(1)} %copy-done.1, ...), custom_call_target="tpu_custom_call" | custom-call | flops 1000 | bytes 1000 | tf_op jit(solution)/shard_map/pallas_call | solution.py:382
  15.5 0.0 copy-done
  15.5 5.0 %shard_map.84.refs_7_ = f32[512,896]{1,0:T(8,128)S(1)} custom-call(bf16[896,512]{1,0:T(8,128)(2,1)S(1)} %copy-done, bf16[16,289,289]{2,1,0:T(8,128)(2,1)S(1)} %copy.11.rot_ref.refs_1_.refs_3_.refs_4_.refs_2_, bf16[16,128,128]{2,1,0:T(8,128)(2,1)S(1)} %get-tuple-element.15.refs_2_.refs_4_.refs_5_.refs_3_, ...), custom_call_target="tpu_custom_call" | custom-call | flops 30000001024 | bytes 1000 | tf_op jit(solution)/shard_map/pallas_call | solution.py:387
  20.5 2.8 %collective-permute-done.1.refs_2_.off = bf16[896,512]{1,0:T(8,128)(2,1)S(1)} collective-permute-done((bf16[896,512]{1,0:T(8,128)(2,1)}, bf16[896,512]{1,0:T(8,128)(2,1)S(1)}, u32[]{:S(2)}, u32[]{:S(2)}) %collective-permute-start.1) | collective-permute-done | bytes 917536 | tf_op jit(solution)/shard_map/ppermute | solution.py:351
  23.2 0.0 collective-permute-done.refs_1_.near
  23.2 6.1 %shard_map.85.refs_8_ = f32[512,896]{1,0:T(8,128)S(1)} custom-call(bf16[896,512]{1,0:T(8,128)(2,1)S(1)} %copy-done, bf16[896,512]{1,0:T(8,128)(2,1)S(1)} %collective-permute-done.refs_1_.near, bf16[896,512]{1,0:T(8,128)(2,1)S(1)} %collective-permute-done.1.refs_2_.off, bf16[16,289,289]{2,1,0:T(8,128)(2,1)S(1)} %copy.11.rot_ref.refs_1_.refs_3_.refs_4_.refs_2_, ...), custom_call_target="tpu_custom_call" | custom-call | flops 1000 | bytes 1000 | tf_op jit(solution)/shard_map/pallas_call | solution.py:388
  29.3 0.2 collective-permute-done.3.low.refs_1_
  29.5 0.0 collective-permute-done.2.high.refs_2_
  29.5 1.1 %shard_map.86 = (bf16[1792,256]{1,0:T(8,128)(2,1)S(1)}, bf16[1792,256]{1,0:T(8,128)(2,1)S(1)}) custom-call(bf16[896,512]{1,0:T(8,128)(2,1)S(1)} %copy-done, bf16[896,512]{1,0:T(8,128)(2,1)S(1)} %collective-permute-done.refs_1_.near, bf16[896,512]{1,0:T(8,128)(2,1)S(1)} %collective-permute-done.1.refs_2_.off, ...), custom_call_target="tpu_custom_call" | custom-call | flops 1000 | bytes 1000 | tf_op jit(solution)/shard_map/pallas_call | solution.py:391
  30.6 0.3 collective-permute-start.5
  30.9 2.9 %collective-permute-start.4 = (bf16[1792,256]{1,0:T(8,128)(2,1)S(1)}, bf16[1792,256]{1,0:T(8,128)(2,1)S(1)}, u32[]{:S(2)}, u32[]{:S(2)}) collective-permute-start(bf16[1792,256]{1,0:T(8,128)(2,1)S(1)} %get-tuple-element.22), channel_id=1, source_target_pairs={{0,112},{16,32},{32,16},{48,64},{64,48},{80,96},{96,80},{112,0},{1... | collective-permute-start | bytes 2752520 | tf_op jit(solution)/shard_map/ppermute | solution.py:351
  33.7 0.0 collective-permute-done.5.refs_3_
  33.7 9.9 %shard_map.87.refs_6_ = f32[512,896]{1,0:T(8,128)S(1)} custom-call(bf16[896,512]{1,0:T(8,128)(2,1)S(1)} %copy-done, bf16[896,512]{1,0:T(8,128)(2,1)S(1)} %collective-permute-done.3.low.refs_1_, bf16[896,512]{1,0:T(8,128)(2,1)S(1)} %collective-permute-done.2.high.refs_2_, bf16[1792,256]{1,0:T(8,128)(2,1)S(1)} %collective-permute-done.5.refs_3_, ...), custom_call_target="tpu_custom_call" | custom-call | flops 1000 | bytes 1000 | tf_op jit(solution)/shard_map/pallas_call | solution.py:393
  43.6 1.4 %collective-permute-done.4.refs_1_ = bf16[1792,256]{1,0:T(8,128)(2,1)S(1)} collective-permute-done((bf16[1792,256]{1,0:T(8,128)(2,1)S(1)}, bf16[1792,256]{1,0:T(8,128)(2,1)S(1)}, u32[]{:S(2)}, u32[]{:S(2)}) %collective-permute-start.4) | collective-permute-done | bytes 917536 | tf_op jit(solution)/shard_map/ppermute | solution.py:351
  45.0 6.4 %shard_map.88 = bf16[3,289,512]{2,1,0:T(8,128)(2,1)} custom-call(bf16[896,512]{1,0:T(8,128)(2,1)S(1)} %copy-done, bf16[1792,256]{1,0:T(8,128)(2,1)S(1)} %collective-permute-done.4.refs_1_, bf16[16,289,289]{2,1,0:T(8,128)(2,1)S(1)} %copy.11.rot_ref.refs_1_.refs_3_.refs_4_.refs_2_, bf16[16,128,128]{2,1,0:T(8,128)(2,1)S(1)} %get-tuple-element.15.refs_2_.refs_4_.refs_5_.refs_3_, ...), custom_call_target="tpu_custom_call" | custom-call | flops 1000 | bytes 1000 | tf_op jit(solution)/shard_map/pallas_call | solution.py:394
Async XLA Ops:
  2.2 11.5 %copy-start.1 = (bf16[289,289]{1,0:T(8,128)(2,1)S(1)}, bf16[289,289]{1,0:T(8,128)(2,1)}, u32[]{:S(2)}) copy-start(bf16[289,289]{1,0:T(8,128)(2,1)} %trans_ref.1) | copy-start | bytes 501130
  2.3 11.5 %copy-start.2 = (bf16[289,289]{1,0:T(8,128)(2,1)S(1)}, bf16[289,289]{1,0:T(8,128)(2,1)}, u32[]{:S(2)}) copy-start(bf16[289,289]{1,0:T(8,128)(2,1)} %self_ref.1) | copy-start | bytes 501130
  2.3 27.2 %collective-permute-start.3 = (bf16[896,512]{1,0:T(8,128)(2,1)}, bf16[896,512]{1,0:T(8,128)(2,1)S(1)}, u32[]{:S(2)}, u32[]{:S(2)}) collective-permute-start(bf16[896,512]{1,0:T(8,128)(2,1)} %shard_map.82.refs_0_.mine), channel_id=1, source_target_pairs={{15,0},{0,1},{1,2},{2,3},{3,4},{4,5},{5,6},{6,7},{7,8},{8,9},{9,10... | collective-permute-start | bytes 2752520 | tf_op jit(solution)/shard_map/ppermute | solution.py:356
  4.0 25.5 %collective-permute-start.2 = (bf16[896,512]{1,0:T(8,128)(2,1)}, bf16[896,512]{1,0:T(8,128)(2,1)S(1)}, u32[]{:S(2)}, u32[]{:S(2)}) collective-permute-start(bf16[896,512]{1,0:T(8,128)(2,1)} %shard_map.82.refs_0_.mine), channel_id=1, source_target_pairs={{1,0},{2,1},{3,2},{4,3},{5,4},{6,5},{7,6},{8,7},{9,8},{10,9},{11,1... | collective-permute-start | bytes 2752520 | tf_op jit(solution)/shard_map/ppermute | solution.py:356
  9.0 14.2 %collective-permute-start.1 = (bf16[896,512]{1,0:T(8,128)(2,1)}, bf16[896,512]{1,0:T(8,128)(2,1)S(1)}, u32[]{:S(2)}, u32[]{:S(2)}) collective-permute-start(bf16[896,512]{1,0:T(8,128)(2,1)} %shard_map.82.refs_0_.mine), channel_id=1, source_target_pairs={{0,112},{16,32},{32,16},{48,64},{64,48},{80,96},{96,80},{112,0},{1... | collective-permute-start | bytes 2752520 | tf_op jit(solution)/shard_map/ppermute | solution.py:351
  10.9 12.3 %collective-permute-start = (bf16[896,512]{1,0:T(8,128)(2,1)}, bf16[896,512]{1,0:T(8,128)(2,1)S(1)}, u32[]{:S(2)}, u32[]{:S(2)}) collective-permute-start(bf16[896,512]{1,0:T(8,128)(2,1)} %shard_map.82.refs_0_.mine), channel_id=1, source_target_pairs={{0,16},{16,0},{32,48},{48,32},{64,80},{80,64},{96,112},{112,96},{1... | collective-permute-start | bytes 2752520 | tf_op jit(solution)/shard_map/ppermute | solution.py:351
  13.7 1.7 %copy-start = (bf16[896,512]{1,0:T(8,128)(2,1)S(1)}, bf16[896,512]{1,0:T(8,128)(2,1)}, u32[]{:S(2)}) copy-start(bf16[896,512]{1,0:T(8,128)(2,1)} %shard_map.82.refs_0_.mine) | copy-start | bytes 2752516
  30.6 3.1 %collective-permute-start.5 = (bf16[1792,256]{1,0:T(8,128)(2,1)S(1)}, bf16[1792,256]{1,0:T(8,128)(2,1)S(1)}, u32[]{:S(2)}, u32[]{:S(2)}) collective-permute-start(bf16[1792,256]{1,0:T(8,128)(2,1)S(1)} %get-tuple-element.23), channel_id=1, source_target_pairs={{0,16},{16,0},{32,48},{48,32},{64,80},{80,64},{96,112},{112,96},{1... | collective-permute-start | bytes 2752520 | tf_op jit(solution)/shard_map/ppermute | solution.py:351
  30.9 14.1 %collective-permute-start.4 = (bf16[1792,256]{1,0:T(8,128)(2,1)S(1)}, bf16[1792,256]{1,0:T(8,128)(2,1)S(1)}, u32[]{:S(2)}, u32[]{:S(2)}) collective-permute-start(bf16[1792,256]{1,0:T(8,128)(2,1)S(1)} %get-tuple-element.22), channel_id=1, source_target_pairs={{0,112},{16,32},{32,16},{48,64},{64,48},{80,96},{96,80},{112,0},{1... | collective-permute-start | bytes 2752520 | tf_op jit(solution)/shard_map/ppermute | solution.py:351

commit v6 on v5

--- a/solution.py
+++ b/solution.py
@@ -22,8 +22,11 @@
 PAIR = 2 * SLOTS
 GROUP = 2 * CAP
 ROWS = NR * GROUP
-HEAD = 16
-HEAD_AT = WIDE - HEAD
+LONG = 880
+SLAB = 16
+SLAB_AT = LONG - SLAB
+HEAD = 13
+ABOVE = SLAB - HEAD
 BASE = 32
 OWN, PARTNER = 0, 2
 ROT = 9
@@ -120,8 +123,10 @@
     def tail_block(block):
         return jnp.where(same, nt(nn(fold, block).astype(BF), fold), 0.0).astype(BF)
 
+    rot_tail[...] = jnp.zeros(rot_tail.shape, BF)
     for r in range(NR):
-        rot_tail[r] = tail_block(rot_ref[r, MAIN:, MAIN:])
+        place = slice(r % 2 * TAIL, (r % 2 + 1) * TAIL)
+        rot_tail[r // 2, place, place] = tail_block(rot_ref[r, MAIN:, MAIN:])
     for source, (main, tail) in ((trans_ref, pieces[:2]), (self_ref, pieces[2:])):
         for c in range(3):
             main[c, :, :MAIN] = source[:MAIN, :MAIN]
@@ -132,19 +137,19 @@
 
 def head_part(ref, at, row, block):
     lanes = slice(block * SLOTS, (block + 1) * SLOTS)
-    return ref[at : at + HEAD, lanes].astype(F32)[row : row + 1]
-
-
-def head_cells(ref, what, row, at=HEAD_AT):
+    return ref[at : at + SLAB, lanes].astype(F32)[row + ABOVE : row + ABOVE + 1]
+
+
+def head_cells(ref, what, row, at=SLAB_AT):
     return (head_part(ref, at, row, what) * BASE + head_part(ref, at, row, what + 1)).astype(jnp.int32)
 
 
 def head_rots(ref, o):
-    return head_part(ref, HEAD_AT, ROT + o // 4, o % 4).astype(jnp.int32)
+    return head_part(ref, SLAB_AT, ROT + o // 4, o % 4).astype(jnp.int32)
 
 
 def is_even(mine):
-    return head_part(mine, HEAD_AT, ODD, 0) < 0.5
+    return head_part(mine, SLAB_AT, ODD, 0) < 0.5
 
 
 def head_digits(index):
@@ -154,22 +159,23 @@
 
 def pack_kernel(count_ref, own_ref, partner_ref, rot_ref, here_ref, out, *scratch):
     held, tail, arrived, sent = scratch[:5], scratch[5], scratch[6], scratch[7]
-    copies = [
-        pltpu.make_async_copy(src, dst, arrived.at[i])
-        for i, (src, dst) in enumerate(zip((count_ref, own_ref, partner_ref, rot_ref, here_ref), held))
+    count, own, partner, rot, here = held
+    bodies = [pltpu.make_async_copy(here_ref.at[c], here.at[c], arrived.at[c]) for c in range(3)]
+    small = [
+        pltpu.make_async_copy(src, dst, arrived.at[3 + i])
+        for i, (src, dst) in enumerate(zip((count_ref, own_ref, partner_ref, rot_ref), held))
     ]
-    for copy in copies:
+    for copy in bodies + small:
         copy.start()
-    for copy in copies:
-        copy.wait()
-    count, own, partner, rot, here = held
-    mains = [
+    sends = [
         pltpu.make_async_copy(here.at[c, :MAIN], out.at[c * MAIN : (c + 1) * MAIN], sent.at[c]) for c in range(3)
     ]
-    for copy in mains:
-        copy.start()
+    for body, send in zip(bodies, sends):
+        body.wait()
+        send.start()
+    for copy in small:
+        copy.wait()
     rest = nn(spread(0), here[0, MAIN:]) + nn(spread(1), here[1, MAIN:]) + nn(spread(2), here[2, MAIN:])
-    tail[...] = rest.astype(BF)
     cells = [jnp.concatenate([ref[o] for o in range(9)], axis=0) for ref in (own, partner)]
     digits = jnp.concatenate([d.astype(F32) for index in cells for d in head_digits(index)], axis=1)
     slot = iota((1, SLOTS), 1)
@@ -177,12 +183,12 @@
     live.extend([jnp.zeros((1, SLOTS), F32)] * 3)
     rots = [jnp.concatenate(live[4 * i : 4 * i + 4], axis=1) for i in range(3)]
     odd = lax.rem(lax.axis_index("gx"), 2)
-    rows = iota((HEAD - ODD, CELLS), 0)
-    flags = jnp.where((rows == 0) & (rows + odd > 0), 1.0, 0.0)
-    tail[TAIL - HEAD :] = jnp.concatenate([digits, *rots, flags], axis=0).astype(BF)
+    flags = jnp.where(iota((1, CELLS), 0) + odd > 0, 1.0, 0.0)
+    head = jnp.concatenate([jnp.zeros((3 * REST, CELLS), F32), digits, *rots, flags], axis=0)
+    tail[...] = (rest[: LONG - 3 * MAIN] + head).astype(BF)
     last = pltpu.make_async_copy(tail, out.at[3 * MAIN :], sent.at[3])
     last.start()
-    for copy in mains + [last]:
+    for copy in sends + [last]:
         copy.wait()
 
 
@@ -192,13 +198,15 @@
         for side, target, out in ((-1, near, to_near), (1, off, to_off)):
             wanted = choose(even, side, dy, lambda o: head_cells(target, PARTNER, o))
             owners = choose(even, side, dy, lambda o: head_cells(source, OWN, o), True)
-            out[i * WIDE : (i + 1) * WIDE] = nn(source[...], pick_table(wanted, owners)).astype(BF)
+            picked = nn(source[...], pick_table(wanted, owners))
+            out[i * LONG : i * LONG + SLAB_AT] = picked[:SLAB_AT].astype(BF)
             digits = head_digits(choose(even, side, dy, lambda o: head_cells(source, PARTNER, o), True))
             cells = jnp.concatenate([d.astype(F32) for d in digits], axis=1)
             rot = choose(even, side, dy, lambda o: head_rots(source, o), True).astype(F32)
-            row = iota((HEAD, PAIR), 0)
+            row = iota((SLAB, PAIR), 0) - ABOVE
             head = jnp.where(row == 0, cells, jnp.where(row == 1, jnp.concatenate([rot, rot], axis=1), 0.0))
-            out[i * WIDE + HEAD_AT : (i + 1) * WIDE] = head.astype(BF)
+            slab = jnp.where(row < 0, picked[SLAB_AT:], head)
+            out[i * LONG + SLAB_AT : (i + 1) * LONG] = slab.astype(BF)
 
 
 PHASES = {
@@ -235,25 +243,26 @@
     def other(s):
         side, dy = sources[s]
         if forwarded(s):
-            return arrays[-1], (0 if dy < 0 else WIDE)
+            return arrays[-1], (0 if dy < 0 else LONG)
         return arrays[s if first else s + 1], 0
 
     def cell_pair(s, mine_what, their_what):
         array, start = other(s)
         ours = choose(even, *sources[s], lambda o: head_cells(mine, mine_what, o))
         if forwarded(s):
-            return ours, head_cells(array, OWN, 0, start + HEAD_AT)
+            return ours, head_cells(array, OWN, 0, start + SLAB_AT)
         return ours, choose(even, *sources[s], lambda o: head_cells(array, their_what, o), True)
 
     def rot_pair(s):
         array, start = other(s)
         ours = choose(even, *sources[s], lambda o: head_rots(mine, o))
         if forwarded(s):
-            return ours, head_part(array, start + HEAD_AT, 1, 0).astype(jnp.int32)
+            return ours, head_part(array, start + SLAB_AT, 1, 0).astype(jnp.int32)
         return ours, choose(even, *sources[s], lambda o: head_rots(array, o), True)
 
     if first:
-        rows = nt(eye(CELLS), mine[...]).astype(BF)
+        whole = jnp.concatenate([mine[...], jnp.zeros((WIDE - LONG, CELLS), BF)], axis=0)
+        rows = nt(eye(CELLS), whole).astype(BF)
         for lanes, part in zip(COLUMNS, apply_dense(rows, self_main, self_tail)):
             out[:, lanes] = part
 
@@ -265,7 +274,7 @@
     for s in range(m):
         array, start = other(s)
         if forwarded(s):
-            taken = array[start : start + WIDE]
+            taken = array[start : start + LONG]
         else:
             table = pick_table(*cell_pair(s, PARTNER, OWN))
             taken = nn(array[...], table).astype(BF)
@@ -273,6 +282,7 @@
         own_place, partner_place = places[2 * s], places[2 * s + 1]
         place = jnp.concatenate([where_one(row_ids == own_place), where_one(row_ids == partner_place)], axis=1)
         lanes = slice(s * GROUP, (s + 1) * GROUP)
+        taken = jnp.concatenate([taken, jnp.zeros((WIDE - LONG, PAIR), BF)], axis=0)
         grouped[:, lanes, :] = nt(place, taken).astype(BF).reshape(NR, GROUP, WIDE)
         own_to, partner_to = cell_pair(s, OWN, PARTNER)
         to = jnp.concatenate([own_to, partner_to], axis=1) + 1
@@ -283,26 +293,29 @@
 
     size = m * GROUP
     main_signs = side_signs(MAIN, 0)
-    tail_signs = side_signs(TAIL, MAIN)
-
-    def turn(r, source, target, dot):
-        block = source[r]
-        mains, tail = split_lanes(block)
-        turned_main = dot(jnp.concatenate(mains, axis=0), rot_ref[r, :MAIN, :MAIN])
-        turned_main = (turned_main.reshape(3 * m, GROUP, MAIN) * main_signs[None]).reshape(3 * size, MAIN)
-        for c in range(3):
-            target[r, :, c * MAIN : (c + 1) * MAIN] = turned_main[c * size : (c + 1) * size].astype(BF)
-        target[r, :, 3 * MAIN :] = dot(tail, rot_tail[r]).astype(BF)
-
-    for r in range(NR):
-        turn(r, grouped, turned, nt)
+
+    def turn(pair, source, target, dot):
+        tails = []
+        for r in (2 * pair, 2 * pair + 1):
+            mains, tail = split_lanes(source[r])
+            tails.append(tail)
+            turned_main = dot(jnp.concatenate(mains, axis=0), rot_ref[r, :MAIN, :MAIN])
+            turned_main = (turned_main.reshape(3 * m, GROUP, MAIN) * main_signs[None]).reshape(3 * size, MAIN)
+            for c in range(3):
+                target[r, :, c * MAIN : (c + 1) * MAIN] = turned_main[c * size : (c + 1) * size].astype(BF)
+        both = dot(jnp.concatenate(tails, axis=1), rot_tail[pair]).astype(BF)
+        target[2 * pair, :, 3 * MAIN :] = both[:, :TAIL]
+        target[2 * pair + 1, :, 3 * MAIN :] = both[:, TAIL:]
+
+    for pair in range(NR // 2):
+        turn(pair, grouped, turned, nt)
 
     block = turned[...].reshape(NR * size, WIDE)
     for lanes, part in zip(COLUMNS, apply_dense(block, trans_main, trans_tail)):
         grouped[:, :, lanes] = part.astype(BF).reshape(NR, size, lanes.stop - lanes.start)
 
-    for r in range(NR):
-        turn(r, grouped, turned, nn)
+    for pair in range(NR // 2):
+        turn(pair, grouped, turned, nn)
 
     for lanes in COLUMNS:
         width = lanes.stop - lanes.start
@@ -310,12 +323,11 @@
         total = nn(places_to[...], jnp.concatenate(back, axis=0))
         sums[:, lanes] = total + (sums[:, lanes] if first else acc_in[:, lanes])
     if last:
-        tail = sums[:, 3 * MAIN :].astype(BF)
-        unit = eye(MAIN)
+        tail = sums[:, 3 * MAIN :].astype(BF).T
         for c in range(3):
-            out[c, :MAIN, :] = nt(unit, sums[:, c * MAIN : (c + 1) * MAIN].astype(BF)).astype(BF)
+            out[c, :MAIN, :] = sums[:, c * MAIN : (c + 1) * MAIN].astype(BF).T
             gather = where_one(iota((REST, TAIL), 1) == iota((REST, TAIL), 0) + c * REST)
-            out[c, MAIN:, :] = nt(gather, tail).astype(BF)
+            out[c, MAIN:, :] = nn(gather, tail).astype(BF)
 
 
 def vmem_call(kernel, out_shape, scratch=(), limit=VMEM_LIMIT, cost=1000, **options):
@@ -362,11 +374,11 @@
     there = pl.BlockSpec(memory_space=pl.ANY)
     mine = vmem_call(
         pack_kernel,
-        jax.ShapeDtypeStruct((WIDE, CELLS), BF),
+        jax.ShapeDtypeStruct((LONG, CELLS), BF),
         [pltpu.SMEM((1, 9), jnp.int32)]
         + [pltpu.VMEM((9, 1, SLOTS), jnp.int32)] * 3
-        + [pltpu.VMEM((3, K, CELLS), BF), pltpu.VMEM((TAIL, CELLS), BF)]
-        + [pltpu.SemaphoreType.DMA((5,)), pltpu.SemaphoreType.DMA((4,))],
+        + [pltpu.VMEM((3, K, CELLS), BF), pltpu.VMEM((LONG - 3 * MAIN, CELLS), BF)]
+        + [pltpu.SemaphoreType.DMA((7,)), pltpu.SemaphoreType.DMA((4,))],
         limit=PACK_LIMIT,
         in_specs=[there] * 5,
         out_specs=there,
@@ -380,14 +392,14 @@
         jax.ShapeDtypeStruct((TAIL, WIDE), BF),
     ]
     rot_tail, *dense = vmem_call(
-        prep_kernel, [jax.ShapeDtypeStruct((NR, TAIL, TAIL), BF)] + dense + dense
+        prep_kernel, [jax.ShapeDtypeStruct((NR // 2, 2 * TAIL, 2 * TAIL), BF)] + dense + dense
     )(rotations, translation, self_operator)
     weights = (rotations, rot_tail, *dense[:2])
 
     acc = phase_call("here")(mine, *weights, *dense[2:])
     acc = phase_call("sides")(mine, near, off, *weights, acc)
     acc, high, low = after((acc, high, low))
-    picked = jax.ShapeDtypeStruct((2 * WIDE, PAIR), BF)
+    picked = jax.ShapeDtypeStruct((2 * LONG, PAIR), BF)
     to_near, to_off = vmem_call(pick_kernel, (picked, picked))(mine, near, off, high, low)
     far_near, far_off = swap(to_near, 1), swap(to_off, -1)
     acc = phase_call("middle")(mine, low, high, far_near, *weights, acc)

time: 52 us -> 51.1 us (0.983)
  Pallas kernels: 32.4 us -> 30.9 us
  waiting for transfers between devices: 4.32 us -> 4.89 us
    pallas_call x1, Pallas kernels: 9.87 us -> 9.28 us  [local(): acc = phase_call('middle')(mine, low, high, far_near, *weights, acc)]
  transfers between devices with their start and end apart: 6 -> 6, of which waited for: 3 -> 3; matrix products, arithmetic and copies ran while one was open for 5% -> 6% of each run, Pallas kernels for 44% -> 43%
where the time goes in v6:
time: 51.1 us; the launch traced here: 50.4 us
  Pallas kernels  30.9 us (60%)
  starting transfers between devices  11.8 us (23%)
  waiting for transfers between devices  4.89 us (10%)
  local copies, waits for them, and re-layouts  2.81 us (5%)
    pallas_call x1, Pallas kernels, local(): acc = phase_call('middle')(mine, low, high, far_near, *weights, acc)  9.28 us
    ppermute x2, starting transfers between devices, shift(): lax.ppermute(block, axis, [((i - distance) % count, i) for i in range(cou...  6.72 us
    pallas_call x1, Pallas kernels, local(): velocity = phase_call('end')(mine, far_off, *weights, acc)  6.1 us
    pallas_call x1, Pallas kernels, local(): acc = phase_call('sides')(mine, near, off, *weights, acc)  5.61 us
    ppermute x4, starting transfers between devices, swap(): lax.ppermute(block, 'gx', [(i, (i + (first if i % 2 == 0 else -first)) %...  5.04 us
    pallas_call x1, Pallas kernels, local(): acc = phase_call('here')(mine, *weights, *dense[2:])  4.93 us
    ppermute x4, waiting for transfers between devices, swap(): lax.ppermute(block, 'gx', [(i, (i + (first if i % 2 == 0 else -first)) %...  4.45 us
    unnamed x7, local copies, waits for them, and re-layouts  2.81 us
  transfers between devices with their start and end apart: 6, of which 3 were waited for; matrix products, arithmetic and copies ran while one was open for 6% of the time, Pallas kernels for 43%

profile of v6, /device:TPU:0, one launch (start us, length us, event | category | flops | bytes accessed | tf_op | source)
XLA Modules:
  0.0 50.4 jit_solution(7798214574019423315)
XLA Ops:
  0.0 2.1 %shard_map.82.refs_0_.mine = bf16[880,512]{1,0:T(8,128)(2,1)} custom-call(s32[1,9]{1,0:T(1,128)} %bitcast.12, s32[9,1,128]{2,1,0:T(1,128)} %bitcast.9, s32[9,1,128]{2,1,0:T(1,128)} %bitcast.10, s32[9,1,128]{2,1,0:T(1,128)} %bitcast.11, bf16[3,289,512]{2,1,0:T(8,128)(2,1)} %bitcast.8), custom_call_target="tpu_custom_call" | custom-call | flops 1000 | bytes 1000 | tf_op jit(solution)/shard_map/pallas_call | solution.py:375
  2.1 0.0 copy-start.1
  2.2 0.0 copy-start.2
  2.2 1.7 %collective-permute-start.3 = (bf16[880,512]{1,0:T(8,128)(2,1)}, bf16[880,512]{1,0:T(8,128)(2,1)S(1)}, u32[]{:S(2)}, u32[]{:S(2)}) collective-permute-start(bf16[880,512]{1,0:T(8,128)(2,1)} %shard_map.82.refs_0_.mine), channel_id=1, source_target_pairs={{15,0},{0,1},{1,2},{2,3},{3,4},{4,5},{5,6},{6,7},{7,8},{8,9},{9,10... | collective-permute-start | bytes 2703368 | tf_op jit(solution)/shard_map/ppermute | solution.py:368
  3.9 5.0 %collective-permute-start.2 = (bf16[880,512]{1,0:T(8,128)(2,1)}, bf16[880,512]{1,0:T(8,128)(2,1)S(1)}, u32[]{:S(2)}, u32[]{:S(2)}) collective-permute-start(bf16[880,512]{1,0:T(8,128)(2,1)} %shard_map.82.refs_0_.mine), channel_id=1, source_target_pairs={{1,0},{2,1},{3,2},{4,3},{5,4},{6,5},{7,6},{8,7},{9,8},{10,9},{11,1... | collective-permute-start | bytes 2703368 | tf_op jit(solution)/shard_map/ppermute | solution.py:368
  8.9 1.9 %collective-permute-start.1 = (bf16[880,512]{1,0:T(8,128)(2,1)}, bf16[880,512]{1,0:T(8,128)(2,1)S(1)}, u32[]{:S(2)}, u32[]{:S(2)}) collective-permute-start(bf16[880,512]{1,0:T(8,128)(2,1)} %shard_map.82.refs_0_.mine), channel_id=1, source_target_pairs={{0,112},{16,32},{32,16},{48,64},{64,48},{80,96},{96,80},{112,0},{1... | collective-permute-start | bytes 2703368 | tf_op jit(solution)/shard_map/ppermute | solution.py:363
  10.8 0.0 collective-permute-start
  10.8 2.8 %copy.11.rot_ref.refs_1_.refs_3_.refs_4_.refs_2_ = bf16[16,289,289]{2,1,0:T(8,128)(2,1)S(1)} copy(bf16[16,289,289]{2,0,1:T(8,128)(2,1)} %param.11) | data formatting | bytes 5345344 | tf_op args[3]
  13.6 0.0 copy-done.1
  13.6 0.0 copy-done.2
  13.6 0.0 copy-start
  13.6 1.7 %shard_map.83 = (bf16[8,256,256]{2,1,0:T(8,128)(2,1)S(1)}, bf16[3,256,384]{2,1,0:T(8,128)(2,1)S(1)}, bf16[128,896]{1,0:T(8,128)(2,1)S(1)}, bf16[3,256,384]{2,1,0:T(8,128)(2,1)S(1)}, bf16[128,896]{1,0:T(8,128)(2,1)S(1)}) custom-call(bf16[16,289,289]{2,1,0:T(8,128)(2,1)S(1)} %copy.11.rot_ref.refs_1_.refs_3_.refs_4_.refs_2_, bf16[289,289]{1,0:T(8,128)(2,1)S(1)} %copy-done.1, ...), custom_call_target="tpu_custom_call" | custom-call | flops 1000 | bytes 1000 | tf_op jit(solution)/shard_map/pallas_call | solution.py:394
  15.4 0.0 copy-done
  15.4 4.9 %shard_map.84.refs_7_ = f32[512,896]{1,0:T(8,128)S(1)} custom-call(bf16[880,512]{1,0:T(8,128)(2,1)S(1)} %copy-done, bf16[16,289,289]{2,1,0:T(8,128)(2,1)S(1)} %copy.11.rot_ref.refs_1_.refs_3_.refs_4_.refs_2_, bf16[8,256,256]{2,1,0:T(8,128)(2,1)S(1)} %get-tuple-element.15.refs_2_.refs_4_.refs_5_.refs_3_, ...), custom_call_target="tpu_custom_call" | custom-call | flops 30000001024 | bytes 1000 | tf_op jit(solution)/shard_map/pallas_call | solution.py:399
  20.3 2.7 %collective-permute-done.1.refs_2_.off = bf16[880,512]{1,0:T(8,128)(2,1)S(1)} collective-permute-done((bf16[880,512]{1,0:T(8,128)(2,1)}, bf16[880,512]{1,0:T(8,128)(2,1)S(1)}, u32[]{:S(2)}, u32[]{:S(2)}) %collective-permute-start.1) | collective-permute-done | bytes 901152 | tf_op jit(solution)/shard_map/ppermute | solution.py:363
  23.0 0.0 collective-permute-done.refs_1_.near
  23.0 5.6 %shard_map.85.refs_8_ = f32[512,896]{1,0:T(8,128)S(1)} custom-call(bf16[880,512]{1,0:T(8,128)(2,1)S(1)} %copy-done, bf16[880,512]{1,0:T(8,128)(2,1)S(1)} %collective-permute-done.refs_1_.near, bf16[880,512]{1,0:T(8,128)(2,1)S(1)} %collective-permute-done.1.refs_2_.off, bf16[16,289,289]{2,1,0:T(8,128)(2,1)S(1)} %copy.11.rot_ref.refs_1_.refs_3_.refs_4_.refs_2_, ...), custom_call_target="tpu_custom_call" | custom-call | flops 1000 | bytes 1000 | tf_op jit(solution)/shard_map/pallas_call | solution.py:400
  28.6 0.4 collective-permute-done.3.low.refs_1_
  29.0 0.0 collective-permute-done.2.high.refs_2_
  29.0 1.1 %shard_map.86 = (bf16[1760,256]{1,0:T(8,128)(2,1)S(1)}, bf16[1760,256]{1,0:T(8,128)(2,1)S(1)}) custom-call(bf16[880,512]{1,0:T(8,128)(2,1)S(1)} %copy-done, bf16[880,512]{1,0:T(8,128)(2,1)S(1)} %collective-permute-done.refs_1_.near, bf16[880,512]{1,0:T(8,128)(2,1)S(1)} %collective-permute-done.1.refs_2_.off, ...), custom_call_target="tpu_custom_call" | custom-call | flops 1000 | bytes 1000 | tf_op jit(solution)/shard_map/pallas_call | solution.py:403
  30.1 0.3 collective-permute-start.5
  30.4 2.9 %collective-permute-start.4 = (bf16[1760,256]{1,0:T(8,128)(2,1)S(1)}, bf16[1760,256]{1,0:T(8,128)(2,1)S(1)}, u32[]{:S(2)}, u32[]{:S(2)}) collective-permute-start(bf16[1760,256]{1,0:T(8,128)(2,1)S(1)} %get-tuple-element.22), channel_id=1, source_target_pairs={{0,112},{16,32},{32,16},{48,64},{64,48},{80,96},{96,80},{112,0},{1... | collective-permute-start | bytes 2703368 | tf_op jit(solution)/shard_map/ppermute | solution.py:363
  33.3 0.0 collective-permute-done.5.refs_3_
  33.3 9.3 %shard_map.87.refs_6_ = f32[512,896]{1,0:T(8,128)S(1)} custom-call(bf16[880,512]{1,0:T(8,128)(2,1)S(1)} %copy-done, bf16[880,512]{1,0:T(8,128)(2,1)S(1)} %collective-permute-done.3.low.refs_1_, bf16[880,512]{1,0:T(8,128)(2,1)S(1)} %collective-permute-done.2.high.refs_2_, bf16[1760,256]{1,0:T(8,128)(2,1)S(1)} %collective-permute-done.5.refs_3_, ...), custom_call_target="tpu_custom_call" | custom-call | flops 1000 | bytes 1000 | tf_op jit(solution)/shard_map/pallas_call | solution.py:405
  42.6 1.8 %collective-permute-done.4.refs_1_ = bf16[1760,256]{1,0:T(8,128)(2,1)S(1)} collective-permute-done((bf16[1760,256]{1,0:T(8,128)(2,1)S(1)}, bf16[1760,256]{1,0:T(8,128)(2,1)S(1)}, u32[]{:S(2)}, u32[]{:S(2)}) %collective-permute-start.4) | collective-permute-done | bytes 901152 | tf_op jit(solution)/shard_map/ppermute | solution.py:363
  44.3 6.1 %shard_map.88 = bf16[3,289,512]{2,1,0:T(8,128)(2,1)} custom-call(bf16[880,512]{1,0:T(8,128)(2,1)S(1)} %copy-done, bf16[1760,256]{1,0:T(8,128)(2,1)S(1)} %collective-permute-done.4.refs_1_, bf16[16,289,289]{2,1,0:T(8,128)(2,1)S(1)} %copy.11.rot_ref.refs_1_.refs_3_.refs_4_.refs_2_, bf16[8,256,256]{2,1,0:T(8,128)(2,1)S(1)} %get-tuple-element.15.refs_2_.refs_4_.refs_5_.refs_3_, ...), custom_call_target="tpu_custom_call" | custom-call | flops 1000 | bytes 1000 | tf_op jit(solution)/shard_map/pallas_call | solution.py:406
Async XLA Ops:
  2.1 11.5 %copy-start.1 = (bf16[289,289]{1,0:T(8,128)(2,1)S(1)}, bf16[289,289]{1,0:T(8,128)(2,1)}, u32[]{:S(2)}) copy-start(bf16[289,289]{1,0:T(8,128)(2,1)} %trans_ref.1) | copy-start | bytes 501130
  2.2 11.5 %copy-start.2 = (bf16[289,289]{1,0:T(8,128)(2,1)S(1)}, bf16[289,289]{1,0:T(8,128)(2,1)}, u32[]{:S(2)}) copy-start(bf16[289,289]{1,0:T(8,128)(2,1)} %self_ref.1) | copy-start | bytes 501130
  2.2 26.8 %collective-permute-start.3 = (bf16[880,512]{1,0:T(8,128)(2,1)}, bf16[880,512]{1,0:T(8,128)(2,1)S(1)}, u32[]{:S(2)}, u32[]{:S(2)}) collective-permute-start(bf16[880,512]{1,0:T(8,128)(2,1)} %shard_map.82.refs_0_.mine), channel_id=1, source_target_pairs={{15,0},{0,1},{1,2},{2,3},{3,4},{4,5},{5,6},{6,7},{7,8},{8,9},{9,10... | collective-permute-start | bytes 2703368 | tf_op jit(solution)/shard_map/ppermute | solution.py:368
  3.9 25.1 %collective-permute-start.2 = (bf16[880,512]{1,0:T(8,128)(2,1)}, bf16[880,512]{1,0:T(8,128)(2,1)S(1)}, u32[]{:S(2)}, u32[]{:S(2)}) collective-permute-start(bf16[880,512]{1,0:T(8,128)(2,1)} %shard_map.82.refs_0_.mine), channel_id=1, source_target_pairs={{1,0},{2,1},{3,2},{4,3},{5,4},{6,5},{7,6},{8,7},{9,8},{10,9},{11,1... | collective-permute-start | bytes 2703368 | tf_op jit(solution)/shard_map/ppermute | solution.py:368
  8.9 14.1 %collective-permute-start.1 = (bf16[880,512]{1,0:T(8,128)(2,1)}, bf16[880,512]{1,0:T(8,128)(2,1)S(1)}, u32[]{:S(2)}, u32[]{:S(2)}) collective-permute-start(bf16[880,512]{1,0:T(8,128)(2,1)} %shard_map.82.refs_0_.mine), channel_id=1, source_target_pairs={{0,112},{16,32},{32,16},{48,64},{64,48},{80,96},{96,80},{112,0},{1... | collective-permute-start | bytes 2703368 | tf_op jit(solution)/shard_map/ppermute | solution.py:363
  10.8 12.1 %collective-permute-start = (bf16[880,512]{1,0:T(8,128)(2,1)}, bf16[880,512]{1,0:T(8,128)(2,1)S(1)}, u32[]{:S(2)}, u32[]{:S(2)}) collective-permute-start(bf16[880,512]{1,0:T(8,128)(2,1)} %shard_map.82.refs_0_.mine), channel_id=1, source_target_pairs={{0,16},{16,0},{32,48},{48,32},{64,80},{80,64},{96,112},{112,96},{1... | collective-permute-start | bytes 2703368 | tf_op jit(solution)/shard_map/ppermute | solution.py:363
  13.6 1.7 %copy-start = (bf16[880,512]{1,0:T(8,128)(2,1)S(1)}, bf16[880,512]{1,0:T(8,128)(2,1)}, u32[]{:S(2)}) copy-start(bf16[880,512]{1,0:T(8,128)(2,1)} %shard_map.82.refs_0_.mine) | copy-start | bytes 2703364
  30.1 3.1 %collective-permute-start.5 = (bf16[1760,256]{1,0:T(8,128)(2,1)S(1)}, bf16[1760,256]{1,0:T(8,128)(2,1)S(1)}, u32[]{:S(2)}, u32[]{:S(2)}) collective-permute-start(bf16[1760,256]{1,0:T(8,128)(2,1)S(1)} %get-tuple-element.23), channel_id=1, source_target_pairs={{0,16},{16,0},{32,48},{48,32},{64,80},{80,64},{96,112},{112,96},{1... | collective-permute-start | bytes 2703368 | tf_op jit(solution)/shard_map/ppermute | solution.py:363
  30.4 13.9 %collective-permute-start.4 = (bf16[1760,256]{1,0:T(8,128)(2,1)S(1)}, bf16[1760,256]{1,0:T(8,128)(2,1)S(1)}, u32[]{:S(2)}, u32[]{:S(2)}) collective-permute-start(bf16[1760,256]{1,0:T(8,128)(2,1)S(1)} %get-tuple-element.22), channel_id=1, source_target_pairs={{0,112},{16,32},{32,16},{48,64},{64,48},{80,96},{96,80},{112,0},{1... | collective-permute-start | bytes 2703368 | tf_op jit(solution)/shard_map/ppermute | solution.py:363

commit v7 on v6

--- a/solution.py
+++ b/solution.py
@@ -29,7 +29,8 @@
 ABOVE = SLAB - HEAD
 BASE = 32
 OWN, PARTNER = 0, 2
-ROT = 9
+CODE = 9
+DEAD = NR * CAP
 ODD = 12
 COLUMNS = (slice(0, 256), slice(256, 512), slice(512, 768), slice(768, 896))
 VMEM_LIMIT = 28 * 1024 * 1024
@@ -92,16 +93,19 @@
     return jnp.concatenate([where_one(cells == own_side), where_one(cells == partner_side)], axis=1)
 
 
-def positions(rots):
+def ranks_of(rots):
     marks = [where_one(iota((NR, SLOTS), 0) == rot) for rot in rots]
     earlier = where_one(iota((SLOTS, SLOTS), 0) < iota((SLOTS, SLOTS), 1))
-    ranks = nn(jnp.concatenate(marks, axis=0), earlier)
-    places = []
-    for j, mark in enumerate(marks):
-        base = (iota((NR, SLOTS), 0) * GROUP + (j % 2) * CAP + 1).astype(F32)
-        values = mark.astype(F32) * (ranks[j * NR : (j + 1) * NR] + base)
-        places.append(jnp.sum(values, axis=0, keepdims=True).astype(jnp.int32) - 1)
-    return places
+    counts = nn(jnp.concatenate(marks, axis=0), earlier)
+    return [
+        jnp.sum(mark.astype(F32) * counts[o * NR : (o + 1) * NR], axis=0, keepdims=True).astype(jnp.int32)
+        for o, mark in enumerate(marks)
+    ]
+
+
+def place_rows(codes):
+    rows = [code + code // CAP * CAP + side * CAP for side, code in enumerate(codes)]
+    return [jnp.where(code >= DEAD, -1, row) for code, row in zip(codes, rows)]
 
 
 def apply_dense(block, main_ref, tail_ref):
@@ -144,8 +148,8 @@
     return (head_part(ref, at, row, what) * BASE + head_part(ref, at, row, what + 1)).astype(jnp.int32)
 
 
-def head_rots(ref, o):
-    return head_part(ref, SLAB_AT, ROT + o // 4, o % 4).astype(jnp.int32)
+def head_codes(ref, o):
+    return head_part(ref, SLAB_AT, CODE + o // 4, o % 4).astype(jnp.int32)
 
 
 def is_even(mine):
@@ -160,31 +164,33 @@
 def pack_kernel(count_ref, own_ref, partner_ref, rot_ref, here_ref, out, *scratch):
     held, tail, arrived, sent = scratch[:5], scratch[5], scratch[6], scratch[7]
     count, own, partner, rot, here = held
-    bodies = [pltpu.make_async_copy(here_ref.at[c], here.at[c], arrived.at[c]) for c in range(3)]
     small = [
         pltpu.make_async_copy(src, dst, arrived.at[3 + i])
         for i, (src, dst) in enumerate(zip((count_ref, own_ref, partner_ref, rot_ref), held))
     ]
-    for copy in bodies + small:
+    bodies = [pltpu.make_async_copy(here_ref.at[c], here.at[c], arrived.at[c]) for c in range(3)]
+    for copy in small + bodies:
         copy.start()
+    for copy in small:
+        copy.wait()
+    slot = iota((1, SLOTS), 1)
+    live = [slot < count[0, o] for o in range(9)]
+    ranks = ranks_of([rot[o] for o in range(9)])
+    codes = [jnp.where(live[o], rot[o] * CAP + ranks[o], DEAD).astype(F32) for o in range(9)]
+    codes.extend([jnp.zeros((1, SLOTS), F32)] * 3)
+    code_rows = [jnp.concatenate(codes[4 * i : 4 * i + 4], axis=1) for i in range(3)]
+    cells = [jnp.concatenate([ref[o] for o in range(9)], axis=0) for ref in (own, partner)]
+    digits = jnp.concatenate([d.astype(F32) for index in cells for d in head_digits(index)], axis=1)
+    odd = lax.rem(lax.axis_index("gx"), 2)
+    flags = jnp.where(iota((1, CELLS), 0) + odd > 0, 1.0, 0.0)
+    head = jnp.concatenate([jnp.zeros((3 * REST, CELLS), F32), digits, *code_rows, flags], axis=0)
     sends = [
         pltpu.make_async_copy(here.at[c, :MAIN], out.at[c * MAIN : (c + 1) * MAIN], sent.at[c]) for c in range(3)
     ]
     for body, send in zip(bodies, sends):
         body.wait()
         send.start()
-    for copy in small:
-        copy.wait()
     rest = nn(spread(0), here[0, MAIN:]) + nn(spread(1), here[1, MAIN:]) + nn(spread(2), here[2, MAIN:])
-    cells = [jnp.concatenate([ref[o] for o in range(9)], axis=0) for ref in (own, partner)]
-    digits = jnp.concatenate([d.astype(F32) for index in cells for d in head_digits(index)], axis=1)
-    slot = iota((1, SLOTS), 1)
-    live = [jnp.where(slot < count[0, o], rot[o], NR).astype(F32) for o in range(9)]
-    live.extend([jnp.zeros((1, SLOTS), F32)] * 3)
-    rots = [jnp.concatenate(live[4 * i : 4 * i + 4], axis=1) for i in range(3)]
-    odd = lax.rem(lax.axis_index("gx"), 2)
-    flags = jnp.where(iota((1, CELLS), 0) + odd > 0, 1.0, 0.0)
-    head = jnp.concatenate([jnp.zeros((3 * REST, CELLS), F32), digits, *rots, flags], axis=0)
     tail[...] = (rest[: LONG - 3 * MAIN] + head).astype(BF)
     last = pltpu.make_async_copy(tail, out.at[3 * MAIN :], sent.at[3])
     last.start()
@@ -202,7 +208,7 @@
             out[i * LONG : i * LONG + SLAB_AT] = picked[:SLAB_AT].astype(BF)
             digits = head_digits(choose(even, side, dy, lambda o: head_cells(source, PARTNER, o), True))
             cells = jnp.concatenate([d.astype(F32) for d in digits], axis=1)
-            rot = choose(even, side, dy, lambda o: head_rots(source, o), True).astype(F32)
+            rot = choose(even, side, dy, lambda o: head_codes(source, o), True).astype(F32)
             row = iota((SLAB, PAIR), 0) - ABOVE
             head = jnp.where(row == 0, cells, jnp.where(row == 1, jnp.concatenate([rot, rot], axis=1), 0.0))
             slab = jnp.where(row < 0, picked[SLAB_AT:], head)
@@ -233,8 +239,7 @@
     else:
         acc_in = refs[0]
         refs = refs[1:]
-    out, grouped, turned, places_to = refs[:4]
-    sums = refs[4] if last else out
+    out, grouped, turned, places_to = refs
 
     def forwarded(s):
         side, dy = sources[s]
@@ -253,23 +258,18 @@
             return ours, head_cells(array, OWN, 0, start + SLAB_AT)
         return ours, choose(even, *sources[s], lambda o: head_cells(array, their_what, o), True)
 
-    def rot_pair(s):
+    def code_pair(s):
         array, start = other(s)
-        ours = choose(even, *sources[s], lambda o: head_rots(mine, o))
+        ours = choose(even, *sources[s], lambda o: head_codes(mine, o))
         if forwarded(s):
             return ours, head_part(array, start + SLAB_AT, 1, 0).astype(jnp.int32)
-        return ours, choose(even, *sources[s], lambda o: head_rots(array, o), True)
+        return ours, choose(even, *sources[s], lambda o: head_codes(array, o), True)
 
     if first:
         whole = jnp.concatenate([mine[...], jnp.zeros((WIDE - LONG, CELLS), BF)], axis=0)
         rows = nt(eye(CELLS), whole).astype(BF)
         for lanes, part in zip(COLUMNS, apply_dense(rows, self_main, self_tail)):
             out[:, lanes] = part
-
-    rots = []
-    for s in range(m):
-        rots.extend(rot_pair(s))
-    places = positions(rots)
 
     for s in range(m):
         array, start = other(s)
@@ -279,7 +279,7 @@
             table = pick_table(*cell_pair(s, PARTNER, OWN))
             taken = nn(array[...], table).astype(BF)
         row_ids = iota((ROWS, SLOTS), 0)
-        own_place, partner_place = places[2 * s], places[2 * s + 1]
+        own_place, partner_place = place_rows(code_pair(s))
         place = jnp.concatenate([where_one(row_ids == own_place), where_one(row_ids == partner_place)], axis=1)
         lanes = slice(s * GROUP, (s + 1) * GROUP)
         taken = jnp.concatenate([taken, jnp.zeros((WIDE - LONG, PAIR), BF)], axis=0)
@@ -317,17 +317,20 @@
     for pair in range(NR // 2):
         turn(pair, grouped, turned, nn)
 
-    for lanes in COLUMNS:
+    for c, lanes in enumerate(COLUMNS):
         width = lanes.stop - lanes.start
         back = [turned[:, s * GROUP : (s + 1) * GROUP, lanes].reshape(ROWS, width) for s in range(m)]
         total = nn(places_to[...], jnp.concatenate(back, axis=0))
-        sums[:, lanes] = total + (sums[:, lanes] if first else acc_in[:, lanes])
-    if last:
-        tail = sums[:, 3 * MAIN :].astype(BF).T
-        for c in range(3):
-            out[c, :MAIN, :] = sums[:, c * MAIN : (c + 1) * MAIN].astype(BF).T
-            gather = where_one(iota((REST, TAIL), 1) == iota((REST, TAIL), 0) + c * REST)
-            out[c, MAIN:, :] = nn(gather, tail).astype(BF)
+        total = total + (out[:, lanes] if first else acc_in[:, lanes])
+        if not last:
+            out[:, lanes] = total
+        elif c < 3:
+            out[c, :MAIN, :] = total.astype(BF).T
+        else:
+            tail = total.astype(BF).T
+            for part in range(3):
+                gather = where_one(iota((REST, TAIL), 1) == iota((REST, TAIL), 0) + part * REST)
+                out[part, MAIN:, :] = nn(gather, tail).astype(BF)
 
 
 def vmem_call(kernel, out_shape, scratch=(), limit=VMEM_LIMIT, cost=1000, **options):
@@ -352,8 +355,6 @@
         pltpu.VMEM((NR, m * GROUP, WIDE), BF),
         pltpu.VMEM((CELLS, m * ROWS), BF),
     ]
-    if last:
-        scratch.append(pltpu.VMEM((CELLS, WIDE), F32))
     cost = HERE_COST if kind == "here" else 1000
     return vmem_call(functools.partial(phase_kernel, kind), out, scratch, cost=cost)
 

time: 51.1 us -> 50.9 us (level)
  no operation moved by 1% of the time
where the time goes in v7:
time: 50.9 us; the launch traced here: 50.4 us
  Pallas kernels  30.8 us (61%)
  starting transfers between devices  11.6 us (23%)
  waiting for transfers between devices  5.12 us (10%)
  local copies, waits for them, and re-layouts  2.81 us (6%)
    pallas_call x1, Pallas kernels, local(): acc = phase_call('middle')(mine, low, high, far_near, *weights, acc)  9.27 us
    ppermute x2, starting transfers between devices, shift(): lax.ppermute(block, axis, [((i - distance) % count, i) for i in range(cou...  6.72 us
    pallas_call x1, Pallas kernels, local(): velocity = phase_call('end')(mine, far_off, *weights, acc)  6.01 us
    pallas_call x1, Pallas kernels, local(): acc = phase_call('sides')(mine, near, off, *weights, acc)  5.63 us
    pallas_call x1, Pallas kernels, local(): acc = phase_call('here')(mine, *weights, *dense[2:])  4.87 us
    ppermute x4, starting transfers between devices, swap(): lax.ppermute(block, 'gx', [(i, (i + (first if i % 2 == 0 else -first)) %...  4.87 us
    ppermute x4, waiting for transfers between devices, swap(): lax.ppermute(block, 'gx', [(i, (i + (first if i % 2 == 0 else -first)) %...  4.69 us
    unnamed x7, local copies, waits for them, and re-layouts  2.81 us
  transfers between devices with their start and end apart: 6, of which 3 were waited for; matrix products, arithmetic and copies ran while one was open for 6% of the time, Pallas kernels for 43%

profile of v7, /device:TPU:0, one launch (start us, length us, event | category | flops | bytes accessed | tf_op | source)
XLA Modules:
  0.0 50.4 jit_solution(1012382937564481147)
XLA Ops:
  0.0 2.2 %shard_map.82.refs_0_.mine = bf16[880,512]{1,0:T(8,128)(2,1)} custom-call(s32[1,9]{1,0:T(1,128)} %bitcast.12, s32[9,1,128]{2,1,0:T(1,128)} %bitcast.9, s32[9,1,128]{2,1,0:T(1,128)} %bitcast.10, s32[9,1,128]{2,1,0:T(1,128)} %bitcast.11, bf16[3,289,512]{2,1,0:T(8,128)(2,1)} %bitcast.8), custom_call_target="tpu_custom_call" | custom-call | flops 1000 | bytes 1000 | tf_op jit(solution)/shard_map/pallas_call | solution.py:376
  2.2 0.0 copy-start.1
  2.2 0.0 copy-start.2
  2.2 1.7 %collective-permute-start.3 = (bf16[880,512]{1,0:T(8,128)(2,1)}, bf16[880,512]{1,0:T(8,128)(2,1)S(1)}, u32[]{:S(2)}, u32[]{:S(2)}) collective-permute-start(bf16[880,512]{1,0:T(8,128)(2,1)} %shard_map.82.refs_0_.mine), channel_id=1, source_target_pairs={{15,0},{0,1},{1,2},{2,3},{3,4},{4,5},{5,6},{6,7},{7,8},{8,9},{9,10... | collective-permute-start | bytes 2703368 | tf_op jit(solution)/shard_map/ppermute | solution.py:369
  4.0 5.0 %collective-permute-start.2 = (bf16[880,512]{1,0:T(8,128)(2,1)}, bf16[880,512]{1,0:T(8,128)(2,1)S(1)}, u32[]{:S(2)}, u32[]{:S(2)}) collective-permute-start(bf16[880,512]{1,0:T(8,128)(2,1)} %shard_map.82.refs_0_.mine), channel_id=1, source_target_pairs={{1,0},{2,1},{3,2},{4,3},{5,4},{6,5},{7,6},{8,7},{9,8},{10,9},{11,1... | collective-permute-start | bytes 2703368 | tf_op jit(solution)/shard_map/ppermute | solution.py:369
  8.9 1.9 %collective-permute-start.1 = (bf16[880,512]{1,0:T(8,128)(2,1)}, bf16[880,512]{1,0:T(8,128)(2,1)S(1)}, u32[]{:S(2)}, u32[]{:S(2)}) collective-permute-start(bf16[880,512]{1,0:T(8,128)(2,1)} %shard_map.82.refs_0_.mine), channel_id=1, source_target_pairs={{0,112},{16,32},{32,16},{48,64},{64,48},{80,96},{96,80},{112,0},{1... | collective-permute-start | bytes 2703368 | tf_op jit(solution)/shard_map/ppermute | solution.py:364
  10.9 0.0 collective-permute-start
  10.9 2.8 %copy.11.rot_ref.refs_1_.refs_3_.refs_4_.refs_2_ = bf16[16,289,289]{2,1,0:T(8,128)(2,1)S(1)} copy(bf16[16,289,289]{2,0,1:T(8,128)(2,1)} %param.11) | data formatting | bytes 5345344 | tf_op args[3]
  13.7 0.0 copy-done.1
  13.7 0.0 copy-done.2
  13.7 0.0 copy-start
  13.7 1.7 %shard_map.83 = (bf16[8,256,256]{2,1,0:T(8,128)(2,1)S(1)}, bf16[3,256,384]{2,1,0:T(8,128)(2,1)S(1)}, bf16[128,896]{1,0:T(8,128)(2,1)S(1)}, bf16[3,256,384]{2,1,0:T(8,128)(2,1)S(1)}, bf16[128,896]{1,0:T(8,128)(2,1)S(1)}) custom-call(bf16[16,289,289]{2,1,0:T(8,128)(2,1)S(1)} %copy.11.rot_ref.refs_1_.refs_3_.refs_4_.refs_2_, bf16[289,289]{1,0:T(8,128)(2,1)S(1)} %copy-done.1, ...), custom_call_target="tpu_custom_call" | custom-call | flops 1000 | bytes 1000 | tf_op jit(solution)/shard_map/pallas_call | solution.py:395
  15.4 0.0 copy-done
  15.4 4.9 %shard_map.84.refs_7_ = f32[512,896]{1,0:T(8,128)S(1)} custom-call(bf16[880,512]{1,0:T(8,128)(2,1)S(1)} %copy-done, bf16[16,289,289]{2,1,0:T(8,128)(2,1)S(1)} %copy.11.rot_ref.refs_1_.refs_3_.refs_4_.refs_2_, bf16[8,256,256]{2,1,0:T(8,128)(2,1)S(1)} %get-tuple-element.15.refs_2_.refs_4_.refs_5_.refs_3_, ...), custom_call_target="tpu_custom_call" | custom-call | flops 30000001024 | bytes 1000 | tf_op jit(solution)/shard_map/pallas_call | solution.py:400
  20.3 2.7 %collective-permute-done.1.refs_2_.off = bf16[880,512]{1,0:T(8,128)(2,1)S(1)} collective-permute-done((bf16[880,512]{1,0:T(8,128)(2,1)}, bf16[880,512]{1,0:T(8,128)(2,1)S(1)}, u32[]{:S(2)}, u32[]{:S(2)}) %collective-permute-start.1) | collective-permute-done | bytes 901152 | tf_op jit(solution)/shard_map/ppermute | solution.py:364
  23.0 0.0 collective-permute-done.refs_1_.near
  23.0 5.6 %shard_map.85.refs_8_ = f32[512,896]{1,0:T(8,128)S(1)} custom-call(bf16[880,512]{1,0:T(8,128)(2,1)S(1)} %copy-done, bf16[880,512]{1,0:T(8,128)(2,1)S(1)} %collective-permute-done.refs_1_.near, bf16[880,512]{1,0:T(8,128)(2,1)S(1)} %collective-permute-done.1.refs_2_.off, bf16[16,289,289]{2,1,0:T(8,128)(2,1)S(1)} %copy.11.rot_ref.refs_1_.refs_3_.refs_4_.refs_2_, ...), custom_call_target="tpu_custom_call" | custom-call | flops 1000 | bytes 1000 | tf_op jit(solution)/shard_map/pallas_call | solution.py:401
  28.6 0.4 collective-permute-done.3.low.refs_1_
  29.1 0.0 collective-permute-done.2.high.refs_2_
  29.1 1.1 %shard_map.86 = (bf16[1760,256]{1,0:T(8,128)(2,1)S(1)}, bf16[1760,256]{1,0:T(8,128)(2,1)S(1)}) custom-call(bf16[880,512]{1,0:T(8,128)(2,1)S(1)} %copy-done, bf16[880,512]{1,0:T(8,128)(2,1)S(1)} %collective-permute-done.refs_1_.near, bf16[880,512]{1,0:T(8,128)(2,1)S(1)} %collective-permute-done.1.refs_2_.off, ...), custom_call_target="tpu_custom_call" | custom-call | flops 1000 | bytes 1000 | tf_op jit(solution)/shard_map/pallas_call | solution.py:404
  30.2 0.1 collective-permute-start.5
  30.3 2.9 %collective-permute-start.4 = (bf16[1760,256]{1,0:T(8,128)(2,1)S(1)}, bf16[1760,256]{1,0:T(8,128)(2,1)S(1)}, u32[]{:S(2)}, u32[]{:S(2)}) collective-permute-start(bf16[1760,256]{1,0:T(8,128)(2,1)S(1)} %get-tuple-element.22), channel_id=1, source_target_pairs={{0,112},{16,32},{32,16},{48,64},{64,48},{80,96},{96,80},{112,0},{1... | collective-permute-start | bytes 2703368 | tf_op jit(solution)/shard_map/ppermute | solution.py:364
  33.2 0.0 collective-permute-done.5.refs_3_
  33.2 9.3 %shard_map.87.refs_6_ = f32[512,896]{1,0:T(8,128)S(1)} custom-call(bf16[880,512]{1,0:T(8,128)(2,1)S(1)} %copy-done, bf16[880,512]{1,0:T(8,128)(2,1)S(1)} %collective-permute-done.3.low.refs_1_, bf16[880,512]{1,0:T(8,128)(2,1)S(1)} %collective-permute-done.2.high.refs_2_, bf16[1760,256]{1,0:T(8,128)(2,1)S(1)} %collective-permute-done.5.refs_3_, ...), custom_call_target="tpu_custom_call" | custom-call | flops 1000 | bytes 1000 | tf_op jit(solution)/shard_map/pallas_call | solution.py:406
  42.4 2.0 %collective-permute-done.4.refs_1_ = bf16[1760,256]{1,0:T(8,128)(2,1)S(1)} collective-permute-done((bf16[1760,256]{1,0:T(8,128)(2,1)S(1)}, bf16[1760,256]{1,0:T(8,128)(2,1)S(1)}, u32[]{:S(2)}, u32[]{:S(2)}) %collective-permute-start.4) | collective-permute-done | bytes 901152 | tf_op jit(solution)/shard_map/ppermute | solution.py:364
  44.4 6.0 %shard_map.88 = bf16[3,289,512]{2,1,0:T(8,128)(2,1)} custom-call(bf16[880,512]{1,0:T(8,128)(2,1)S(1)} %copy-done, bf16[1760,256]{1,0:T(8,128)(2,1)S(1)} %collective-permute-done.4.refs_1_, bf16[16,289,289]{2,1,0:T(8,128)(2,1)S(1)} %copy.11.rot_ref.refs_1_.refs_3_.refs_4_.refs_2_, bf16[8,256,256]{2,1,0:T(8,128)(2,1)S(1)} %get-tuple-element.15.refs_2_.refs_4_.refs_5_.refs_3_, ...), custom_call_target="tpu_custom_call" | custom-call | flops 1000 | bytes 1000 | tf_op jit(solution)/shard_map/pallas_call | solution.py:407
Async XLA Ops:
  2.2 11.5 %copy-start.1 = (bf16[289,289]{1,0:T(8,128)(2,1)S(1)}, bf16[289,289]{1,0:T(8,128)(2,1)}, u32[]{:S(2)}) copy-start(bf16[289,289]{1,0:T(8,128)(2,1)} %trans_ref.1) | copy-start | bytes 501130
  2.2 11.5 %copy-start.2 = (bf16[289,289]{1,0:T(8,128)(2,1)S(1)}, bf16[289,289]{1,0:T(8,128)(2,1)}, u32[]{:S(2)}) copy-start(bf16[289,289]{1,0:T(8,128)(2,1)} %self_ref.1) | copy-start | bytes 501130
  2.2 26.9 %collective-permute-start.3 = (bf16[880,512]{1,0:T(8,128)(2,1)}, bf16[880,512]{1,0:T(8,128)(2,1)S(1)}, u32[]{:S(2)}, u32[]{:S(2)}) collective-permute-start(bf16[880,512]{1,0:T(8,128)(2,1)} %shard_map.82.refs_0_.mine), channel_id=1, source_target_pairs={{15,0},{0,1},{1,2},{2,3},{3,4},{4,5},{5,6},{6,7},{7,8},{8,9},{9,10... | collective-permute-start | bytes 2703368 | tf_op jit(solution)/shard_map/ppermute | solution.py:369
  4.0 25.1 %collective-permute-start.2 = (bf16[880,512]{1,0:T(8,128)(2,1)}, bf16[880,512]{1,0:T(8,128)(2,1)S(1)}, u32[]{:S(2)}, u32[]{:S(2)}) collective-permute-start(bf16[880,512]{1,0:T(8,128)(2,1)} %shard_map.82.refs_0_.mine), channel_id=1, source_target_pairs={{1,0},{2,1},{3,2},{4,3},{5,4},{6,5},{7,6},{8,7},{9,8},{10,9},{11,1... | collective-permute-start | bytes 2703368 | tf_op jit(solution)/shard_map/ppermute | solution.py:369
  8.9 14.1 %collective-permute-start.1 = (bf16[880,512]{1,0:T(8,128)(2,1)}, bf16[880,512]{1,0:T(8,128)(2,1)S(1)}, u32[]{:S(2)}, u32[]{:S(2)}) collective-permute-start(bf16[880,512]{1,0:T(8,128)(2,1)} %shard_map.82.refs_0_.mine), channel_id=1, source_target_pairs={{0,112},{16,32},{32,16},{48,64},{64,48},{80,96},{96,80},{112,0},{1... | collective-permute-start | bytes 2703368 | tf_op jit(solution)/shard_map/ppermute | solution.py:364
  10.9 12.1 %collective-permute-start = (bf16[880,512]{1,0:T(8,128)(2,1)}, bf16[880,512]{1,0:T(8,128)(2,1)S(1)}, u32[]{:S(2)}, u32[]{:S(2)}) collective-permute-start(bf16[880,512]{1,0:T(8,128)(2,1)} %shard_map.82.refs_0_.mine), channel_id=1, source_target_pairs={{0,16},{16,0},{32,48},{48,32},{64,80},{80,64},{96,112},{112,96},{1... | collective-permute-start | bytes 2703368 | tf_op jit(solution)/shard_map/ppermute | solution.py:364
  13.7 1.7 %copy-start = (bf16[880,512]{1,0:T(8,128)(2,1)S(1)}, bf16[880,512]{1,0:T(8,128)(2,1)}, u32[]{:S(2)}) copy-start(bf16[880,512]{1,0:T(8,128)(2,1)} %shard_map.82.refs_0_.mine) | copy-start | bytes 2703364
  30.2 3.0 %collective-permute-start.5 = (bf16[1760,256]{1,0:T(8,128)(2,1)S(1)}, bf16[1760,256]{1,0:T(8,128)(2,1)S(1)}, u32[]{:S(2)}, u32[]{:S(2)}) collective-permute-start(bf16[1760,256]{1,0:T(8,128)(2,1)S(1)} %get-tuple-element.23), channel_id=1, source_target_pairs={{0,16},{16,0},{32,48},{48,32},{64,80},{80,64},{96,112},{112,96},{1... | collective-permute-start | bytes 2703368 | tf_op jit(solution)/shard_map/ppermute | solution.py:364
  30.3 14.1 %collective-permute-start.4 = (bf16[1760,256]{1,0:T(8,128)(2,1)S(1)}, bf16[1760,256]{1,0:T(8,128)(2,1)S(1)}, u32[]{:S(2)}, u32[]{:S(2)}) collective-permute-start(bf16[1760,256]{1,0:T(8,128)(2,1)S(1)} %get-tuple-element.22), channel_id=1, source_target_pairs={{0,112},{16,32},{32,16},{48,64},{64,48},{80,96},{96,80},{112,0},{1... | collective-permute-start | bytes 2703368 | tf_op jit(solution)/shard_map/ppermute | solution.py:364

commit v8 on v7

--- a/solution.py
+++ b/solution.py
@@ -30,7 +30,6 @@
 BASE = 32
 OWN, PARTNER = 0, 2
 CODE = 9
-DEAD = NR * CAP
 ODD = 12
 COLUMNS = (slice(0, 256), slice(256, 512), slice(512, 768), slice(768, 896))
 VMEM_LIMIT = 28 * 1024 * 1024
@@ -103,9 +102,9 @@
     ]
 
 
-def place_rows(codes):
+def place_rows(codes, lives):
     rows = [code + code // CAP * CAP + side * CAP for side, code in enumerate(codes)]
-    return [jnp.where(code >= DEAD, -1, row) for code, row in zip(codes, rows)]
+    return [jnp.where(live > 0.5, row, -1) for live, row in zip(lives, rows)]
 
 
 def apply_dense(block, main_ref, tail_ref):
@@ -152,6 +151,12 @@
     return head_part(ref, SLAB_AT, CODE + o // 4, o % 4).astype(jnp.int32)
 
 
+def head_live(ref, o):
+    lane = iota((1, SLOTS), 1)
+    count = jnp.sum(jnp.where(lane == o, head_part(ref, SLAB_AT, ODD, 1), 0.0), axis=1, keepdims=True)
+    return jnp.where(lane.astype(F32) < count, 1.0, 0.0)
+
+
 def is_even(mine):
     return head_part(mine, SLAB_AT, ODD, 0) < 0.5
 
@@ -174,16 +179,18 @@
     for copy in small:
         copy.wait()
     slot = iota((1, SLOTS), 1)
-    live = [slot < count[0, o] for o in range(9)]
     ranks = ranks_of([rot[o] for o in range(9)])
-    codes = [jnp.where(live[o], rot[o] * CAP + ranks[o], DEAD).astype(F32) for o in range(9)]
+    codes = [(rot[o] * CAP + ranks[o]).astype(F32) for o in range(9)]
     codes.extend([jnp.zeros((1, SLOTS), F32)] * 3)
     code_rows = [jnp.concatenate(codes[4 * i : 4 * i + 4], axis=1) for i in range(3)]
     cells = [jnp.concatenate([ref[o] for o in range(9)], axis=0) for ref in (own, partner)]
     digits = jnp.concatenate([d.astype(F32) for index in cells for d in head_digits(index)], axis=1)
     odd = lax.rem(lax.axis_index("gx"), 2)
-    flags = jnp.where(iota((1, CELLS), 0) + odd > 0, 1.0, 0.0)
-    head = jnp.concatenate([jnp.zeros((3 * REST, CELLS), F32), digits, *code_rows, flags], axis=0)
+    counts = jnp.zeros((1, SLOTS), jnp.int32)
+    for o in range(9):
+        counts = jnp.where(slot == o, count[0, o], counts)
+    flags = [jnp.where(slot * 0 + odd > 0, 1.0, 0.0), counts.astype(F32), jnp.zeros((1, 2 * SLOTS), F32)]
+    head = jnp.concatenate([jnp.zeros((3 * REST, CELLS), F32), digits, *code_rows, jnp.concatenate(flags, axis=1)], axis=0)
     sends = [
         pltpu.make_async_copy(here.at[c, :MAIN], out.at[c * MAIN : (c + 1) * MAIN], sent.at[c]) for c in range(3)
     ]
@@ -208,9 +215,12 @@
             out[i * LONG : i * LONG + SLAB_AT] = picked[:SLAB_AT].astype(BF)
             digits = head_digits(choose(even, side, dy, lambda o: head_cells(source, PARTNER, o), True))
             cells = jnp.concatenate([d.astype(F32) for d in digits], axis=1)
-            rot = choose(even, side, dy, lambda o: head_codes(source, o), True).astype(F32)
+            code = choose(even, side, dy, lambda o: head_codes(source, o), True).astype(F32)
+            live = choose(even, side, dy, lambda o: head_live(source, o), True)
             row = iota((SLAB, PAIR), 0) - ABOVE
-            head = jnp.where(row == 0, cells, jnp.where(row == 1, jnp.concatenate([rot, rot], axis=1), 0.0))
+            head = jnp.zeros((SLAB, PAIR), F32)
+            for number, line in enumerate((cells, jnp.concatenate([code, code], axis=1), jnp.concatenate([live, live], axis=1))):
+                head = jnp.where(row == number, line, head)
             slab = jnp.where(row < 0, picked[SLAB_AT:], head)
             out[i * LONG + SLAB_AT : (i + 1) * LONG] = slab.astype(BF)
 
@@ -258,12 +268,17 @@
             return ours, head_cells(array, OWN, 0, start + SLAB_AT)
         return ours, choose(even, *sources[s], lambda o: head_cells(array, their_what, o), True)
 
-    def code_pair(s):
+    def place_pair(s):
         array, start = other(s)
-        ours = choose(even, *sources[s], lambda o: head_codes(mine, o))
+        codes = [choose(even, *sources[s], lambda o: head_codes(mine, o))]
+        lives = [choose(even, *sources[s], lambda o: head_live(mine, o))]
         if forwarded(s):
-            return ours, head_part(array, start + SLAB_AT, 1, 0).astype(jnp.int32)
-        return ours, choose(even, *sources[s], lambda o: head_codes(array, o), True)
+            codes.append(head_part(array, start + SLAB_AT, 1, 0).astype(jnp.int32))
+            lives.append(head_part(array, start + SLAB_AT, 2, 0))
+        else:
+            codes.append(choose(even, *sources[s], lambda o: head_codes(array, o), True))
+            lives.append(choose(even, *sources[s], lambda o: head_live(array, o), True))
+        return place_rows(codes, lives)
 
     if first:
         whole = jnp.concatenate([mine[...], jnp.zeros((WIDE - LONG, CELLS), BF)], axis=0)
@@ -279,7 +294,7 @@
             table = pick_table(*cell_pair(s, PARTNER, OWN))
             taken = nn(array[...], table).astype(BF)
         row_ids = iota((ROWS, SLOTS), 0)
-        own_place, partner_place = place_rows(code_pair(s))
+        own_place, partner_place = place_pair(s)
         place = jnp.concatenate([where_one(row_ids == own_place), where_one(row_ids == partner_place)], axis=1)
         lanes = slice(s * GROUP, (s + 1) * GROUP)
         taken = jnp.concatenate([taken, jnp.zeros((WIDE - LONG, PAIR), BF)], axis=0)

time: 50.9 us -> 51.1 us (level)
  no operation moved by 1% of the time
where the time goes in v8:
time: 51.1 us; the launch traced here: 50.4 us
  Pallas kernels  30.8 us (60%)
  starting transfers between devices  11.8 us (23%)
  waiting for transfers between devices  4.94 us (10%)
  local copies, waits for them, and re-layouts  2.81 us (5%)
    pallas_call x1, Pallas kernels, local(): acc = phase_call('middle')(mine, low, high, far_near, *weights, acc)  9.27 us
    ppermute x2, starting transfers between devices, shift(): lax.ppermute(block, axis, [((i - distance) % count, i) for i in range(cou...  6.72 us
    pallas_call x1, Pallas kernels, local(): velocity = phase_call('end')(mine, far_off, *weights, acc)  6.02 us
    pallas_call x1, Pallas kernels, local(): acc = phase_call('sides')(mine, near, off, *weights, acc)  5.62 us
    ppermute x4, starting transfers between devices, swap(): lax.ppermute(block, 'gx', [(i, (i + (first if i % 2 == 0 else -first)) %...  5.05 us
    pallas_call x1, Pallas kernels, local(): acc = phase_call('here')(mine, *weights, *dense[2:])  4.87 us
    ppermute x4, waiting for transfers between devices, swap(): lax.ppermute(block, 'gx', [(i, (i + (first if i % 2 == 0 else -first)) %...  4.5 us
    unnamed x7, local copies, waits for them, and re-layouts  2.81 us
  transfers between devices with their start and end apart: 6, of which 3 were waited for; matrix products, arithmetic and copies ran while one was open for 6% of the time, Pallas kernels for 43%

profile of v8, /device:TPU:0, one launch (start us, length us, event | category | flops | bytes accessed | tf_op | source)
XLA Modules:
  0.0 50.4 jit_solution(17297756344121706231)
XLA Ops:
  0.0 2.2 %shard_map.82.refs_0_.mine = bf16[880,512]{1,0:T(8,128)(2,1)} custom-call(s32[1,9]{1,0:T(1,128)} %bitcast.12, s32[9,1,128]{2,1,0:T(1,128)} %bitcast.9, s32[9,1,128]{2,1,0:T(1,128)} %bitcast.10, s32[9,1,128]{2,1,0:T(1,128)} %bitcast.11, bf16[3,289,512]{2,1,0:T(8,128)(2,1)} %bitcast.8), custom_call_target="tpu_custom_call" | custom-call | flops 1000 | bytes 1000 | tf_op jit(solution)/shard_map/pallas_call | solution.py:391
  2.2 0.0 copy-start.1
  2.2 0.0 copy-start.2
  2.2 1.7 %collective-permute-start.3 = (bf16[880,512]{1,0:T(8,128)(2,1)}, bf16[880,512]{1,0:T(8,128)(2,1)S(1)}, u32[]{:S(2)}, u32[]{:S(2)}) collective-permute-start(bf16[880,512]{1,0:T(8,128)(2,1)} %shard_map.82.refs_0_.mine), channel_id=1, source_target_pairs={{15,0},{0,1},{1,2},{2,3},{3,4},{4,5},{5,6},{6,7},{7,8},{8,9},{9,10... | collective-permute-start | bytes 2703368 | tf_op jit(solution)/shard_map/ppermute | solution.py:384
  4.0 5.0 %collective-permute-start.2 = (bf16[880,512]{1,0:T(8,128)(2,1)}, bf16[880,512]{1,0:T(8,128)(2,1)S(1)}, u32[]{:S(2)}, u32[]{:S(2)}) collective-permute-start(bf16[880,512]{1,0:T(8,128)(2,1)} %shard_map.82.refs_0_.mine), channel_id=1, source_target_pairs={{1,0},{2,1},{3,2},{4,3},{5,4},{6,5},{7,6},{8,7},{9,8},{10,9},{11,1... | collective-permute-start | bytes 2703368 | tf_op jit(solution)/shard_map/ppermute | solution.py:384
  8.9 1.9 %collective-permute-start.1 = (bf16[880,512]{1,0:T(8,128)(2,1)}, bf16[880,512]{1,0:T(8,128)(2,1)S(1)}, u32[]{:S(2)}, u32[]{:S(2)}) collective-permute-start(bf16[880,512]{1,0:T(8,128)(2,1)} %shard_map.82.refs_0_.mine), channel_id=1, source_target_pairs={{0,112},{16,32},{32,16},{48,64},{64,48},{80,96},{96,80},{112,0},{1... | collective-permute-start | bytes 2703368 | tf_op jit(solution)/shard_map/ppermute | solution.py:379
  10.9 0.0 collective-permute-start
  10.9 2.8 %copy.11.rot_ref.refs_1_.refs_3_.refs_4_.refs_2_ = bf16[16,289,289]{2,1,0:T(8,128)(2,1)S(1)} copy(bf16[16,289,289]{2,0,1:T(8,128)(2,1)} %param.11) | data formatting | bytes 5345344 | tf_op args[3]
  13.7 0.0 copy-done.1
  13.7 0.0 copy-done.2
  13.7 0.0 copy-start
  13.7 1.7 %shard_map.83 = (bf16[8,256,256]{2,1,0:T(8,128)(2,1)S(1)}, bf16[3,256,384]{2,1,0:T(8,128)(2,1)S(1)}, bf16[128,896]{1,0:T(8,128)(2,1)S(1)}, bf16[3,256,384]{2,1,0:T(8,128)(2,1)S(1)}, bf16[128,896]{1,0:T(8,128)(2,1)S(1)}) custom-call(bf16[16,289,289]{2,1,0:T(8,128)(2,1)S(1)} %copy.11.rot_ref.refs_1_.refs_3_.refs_4_.refs_2_, bf16[289,289]{1,0:T(8,128)(2,1)S(1)} %copy-done.1, ...), custom_call_target="tpu_custom_call" | custom-call | flops 1000 | bytes 1000 | tf_op jit(solution)/shard_map/pallas_call | solution.py:410
  15.4 0.0 copy-done
  15.4 4.9 %shard_map.84.refs_7_ = f32[512,896]{1,0:T(8,128)S(1)} custom-call(bf16[880,512]{1,0:T(8,128)(2,1)S(1)} %copy-done, bf16[16,289,289]{2,1,0:T(8,128)(2,1)S(1)} %copy.11.rot_ref.refs_1_.refs_3_.refs_4_.refs_2_, bf16[8,256,256]{2,1,0:T(8,128)(2,1)S(1)} %get-tuple-element.15.refs_2_.refs_4_.refs_5_.refs_3_, ...), custom_call_target="tpu_custom_call" | custom-call | flops 30000001024 | bytes 1000 | tf_op jit(solution)/shard_map/pallas_call | solution.py:415
  20.3 2.7 %collective-permute-done.1.refs_2_.off = bf16[880,512]{1,0:T(8,128)(2,1)S(1)} collective-permute-done((bf16[880,512]{1,0:T(8,128)(2,1)}, bf16[880,512]{1,0:T(8,128)(2,1)S(1)}, u32[]{:S(2)}, u32[]{:S(2)}) %collective-permute-start.1) | collective-permute-done | bytes 901152 | tf_op jit(solution)/shard_map/ppermute | solution.py:379
  23.0 0.0 collective-permute-done.refs_1_.near
  23.0 5.6 %shard_map.85.refs_8_ = f32[512,896]{1,0:T(8,128)S(1)} custom-call(bf16[880,512]{1,0:T(8,128)(2,1)S(1)} %copy-done, bf16[880,512]{1,0:T(8,128)(2,1)S(1)} %collective-permute-done.refs_1_.near, bf16[880,512]{1,0:T(8,128)(2,1)S(1)} %collective-permute-done.1.refs_2_.off, bf16[16,289,289]{2,1,0:T(8,128)(2,1)S(1)} %copy.11.rot_ref.refs_1_.refs_3_.refs_4_.refs_2_, ...), custom_call_target="tpu_custom_call" | custom-call | flops 1000 | bytes 1000 | tf_op jit(solution)/shard_map/pallas_call | solution.py:416
  28.6 0.4 collective-permute-done.3.low.refs_1_
  29.1 0.0 collective-permute-done.2.high.refs_2_
  29.1 1.1 %shard_map.86 = (bf16[1760,256]{1,0:T(8,128)(2,1)S(1)}, bf16[1760,256]{1,0:T(8,128)(2,1)S(1)}) custom-call(bf16[880,512]{1,0:T(8,128)(2,1)S(1)} %copy-done, bf16[880,512]{1,0:T(8,128)(2,1)S(1)} %collective-permute-done.refs_1_.near, bf16[880,512]{1,0:T(8,128)(2,1)S(1)} %collective-permute-done.1.refs_2_.off, ...), custom_call_target="tpu_custom_call" | custom-call | flops 1000 | bytes 1000 | tf_op jit(solution)/shard_map/pallas_call | solution.py:419
  30.2 0.3 collective-permute-start.5
  30.5 2.9 %collective-permute-start.4 = (bf16[1760,256]{1,0:T(8,128)(2,1)S(1)}, bf16[1760,256]{1,0:T(8,128)(2,1)S(1)}, u32[]{:S(2)}, u32[]{:S(2)}) collective-permute-start(bf16[1760,256]{1,0:T(8,128)(2,1)S(1)} %get-tuple-element.22), channel_id=1, source_target_pairs={{0,112},{16,32},{32,16},{48,64},{64,48},{80,96},{96,80},{112,0},{1... | collective-permute-start | bytes 2703368 | tf_op jit(solution)/shard_map/ppermute | solution.py:379
  33.3 0.0 collective-permute-done.5.refs_3_
  33.3 9.3 %shard_map.87.refs_6_ = f32[512,896]{1,0:T(8,128)S(1)} custom-call(bf16[880,512]{1,0:T(8,128)(2,1)S(1)} %copy-done, bf16[880,512]{1,0:T(8,128)(2,1)S(1)} %collective-permute-done.3.low.refs_1_, bf16[880,512]{1,0:T(8,128)(2,1)S(1)} %collective-permute-done.2.high.refs_2_, bf16[1760,256]{1,0:T(8,128)(2,1)S(1)} %collective-permute-done.5.refs_3_, ...), custom_call_target="tpu_custom_call" | custom-call | flops 1000 | bytes 1000 | tf_op jit(solution)/shard_map/pallas_call | solution.py:421
  42.6 1.8 %collective-permute-done.4.refs_1_ = bf16[1760,256]{1,0:T(8,128)(2,1)S(1)} collective-permute-done((bf16[1760,256]{1,0:T(8,128)(2,1)S(1)}, bf16[1760,256]{1,0:T(8,128)(2,1)S(1)}, u32[]{:S(2)}, u32[]{:S(2)}) %collective-permute-start.4) | collective-permute-done | bytes 901152 | tf_op jit(solution)/shard_map/ppermute | solution.py:379
  44.4 6.0 %shard_map.88 = bf16[3,289,512]{2,1,0:T(8,128)(2,1)} custom-call(bf16[880,512]{1,0:T(8,128)(2,1)S(1)} %copy-done, bf16[1760,256]{1,0:T(8,128)(2,1)S(1)} %collective-permute-done.4.refs_1_, bf16[16,289,289]{2,1,0:T(8,128)(2,1)S(1)} %copy.11.rot_ref.refs_1_.refs_3_.refs_4_.refs_2_, bf16[8,256,256]{2,1,0:T(8,128)(2,1)S(1)} %get-tuple-element.15.refs_2_.refs_4_.refs_5_.refs_3_, ...), custom_call_target="tpu_custom_call" | custom-call | flops 1000 | bytes 1000 | tf_op jit(solution)/shard_map/pallas_call | solution.py:422
Async XLA Ops:
  2.2 11.5 %copy-start.1 = (bf16[289,289]{1,0:T(8,128)(2,1)S(1)}, bf16[289,289]{1,0:T(8,128)(2,1)}, u32[]{:S(2)}) copy-start(bf16[289,289]{1,0:T(8,128)(2,1)} %trans_ref.1) | copy-start | bytes 501130
  2.2 11.5 %copy-start.2 = (bf16[289,289]{1,0:T(8,128)(2,1)S(1)}, bf16[289,289]{1,0:T(8,128)(2,1)}, u32[]{:S(2)}) copy-start(bf16[289,289]{1,0:T(8,128)(2,1)} %self_ref.1) | copy-start | bytes 501130
  2.2 26.9 %collective-permute-start.3 = (bf16[880,512]{1,0:T(8,128)(2,1)}, bf16[880,512]{1,0:T(8,128)(2,1)S(1)}, u32[]{:S(2)}, u32[]{:S(2)}) collective-permute-start(bf16[880,512]{1,0:T(8,128)(2,1)} %shard_map.82.refs_0_.mine), channel_id=1, source_target_pairs={{15,0},{0,1},{1,2},{2,3},{3,4},{4,5},{5,6},{6,7},{7,8},{8,9},{9,10... | collective-permute-start | bytes 2703368 | tf_op jit(solution)/shard_map/ppermute | solution.py:384
  4.0 25.1 %collective-permute-start.2 = (bf16[880,512]{1,0:T(8,128)(2,1)}, bf16[880,512]{1,0:T(8,128)(2,1)S(1)}, u32[]{:S(2)}, u32[]{:S(2)}) collective-permute-start(bf16[880,512]{1,0:T(8,128)(2,1)} %shard_map.82.refs_0_.mine), channel_id=1, source_target_pairs={{1,0},{2,1},{3,2},{4,3},{5,4},{6,5},{7,6},{8,7},{9,8},{10,9},{11,1... | collective-permute-start | bytes 2703368 | tf_op jit(solution)/shard_map/ppermute | solution.py:384
  8.9 14.1 %collective-permute-start.1 = (bf16[880,512]{1,0:T(8,128)(2,1)}, bf16[880,512]{1,0:T(8,128)(2,1)S(1)}, u32[]{:S(2)}, u32[]{:S(2)}) collective-permute-start(bf16[880,512]{1,0:T(8,128)(2,1)} %shard_map.82.refs_0_.mine), channel_id=1, source_target_pairs={{0,112},{16,32},{32,16},{48,64},{64,48},{80,96},{96,80},{112,0},{1... | collective-permute-start | bytes 2703368 | tf_op jit(solution)/shard_map/ppermute | solution.py:379
  10.9 12.1 %collective-permute-start = (bf16[880,512]{1,0:T(8,128)(2,1)}, bf16[880,512]{1,0:T(8,128)(2,1)S(1)}, u32[]{:S(2)}, u32[]{:S(2)}) collective-permute-start(bf16[880,512]{1,0:T(8,128)(2,1)} %shard_map.82.refs_0_.mine), channel_id=1, source_target_pairs={{0,16},{16,0},{32,48},{48,32},{64,80},{80,64},{96,112},{112,96},{1... | collective-permute-start | bytes 2703368 | tf_op jit(solution)/shard_map/ppermute | solution.py:379
  13.7 1.7 %copy-start = (bf16[880,512]{1,0:T(8,128)(2,1)S(1)}, bf16[880,512]{1,0:T(8,128)(2,1)}, u32[]{:S(2)}) copy-start(bf16[880,512]{1,0:T(8,128)(2,1)} %shard_map.82.refs_0_.mine) | copy-start | bytes 2703364
  30.2 3.1 %collective-permute-start.5 = (bf16[1760,256]{1,0:T(8,128)(2,1)S(1)}, bf16[1760,256]{1,0:T(8,128)(2,1)S(1)}, u32[]{:S(2)}, u32[]{:S(2)}) collective-permute-start(bf16[1760,256]{1,0:T(8,128)(2,1)S(1)} %get-tuple-element.23), channel_id=1, source_target_pairs={{0,16},{16,0},{32,48},{48,32},{64,80},{80,64},{96,112},{112,96},{1... | collective-permute-start | bytes 2703368 | tf_op jit(solution)/shard_map/ppermute | solution.py:379
  30.5 13.9 %collective-permute-start.4 = (bf16[1760,256]{1,0:T(8,128)(2,1)S(1)}, bf16[1760,256]{1,0:T(8,128)(2,1)S(1)}, u32[]{:S(2)}, u32[]{:S(2)}) collective-permute-start(bf16[1760,256]{1,0:T(8,128)(2,1)S(1)} %get-tuple-element.22), channel_id=1, source_target_pairs={{0,112},{16,32},{32,16},{48,64},{64,48},{80,96},{96,80},{112,0},{1... | collective-permute-start | bytes 2703368 | tf_op jit(solution)/shard_map/ppermute | solution.py:379

commit v9 on v8

--- a/solution.py
+++ b/solution.py
@@ -104,7 +104,7 @@
 
 def place_rows(codes, lives):
     rows = [code + code // CAP * CAP + side * CAP for side, code in enumerate(codes)]
-    return [jnp.where(live > 0.5, row, -1) for live, row in zip(lives, rows)]
+    return [jnp.where(live, row, -1) for live, row in zip(lives, rows)]
 
 
 def apply_dense(block, main_ref, tail_ref):
@@ -151,10 +151,11 @@
     return head_part(ref, SLAB_AT, CODE + o // 4, o % 4).astype(jnp.int32)
 
 
-def head_live(ref, o):
+def live_slots(even, side, dy, counts, theirs=False):
     lane = iota((1, SLOTS), 1)
-    count = jnp.sum(jnp.where(lane == o, head_part(ref, SLAB_AT, ODD, 1), 0.0), axis=1, keepdims=True)
-    return jnp.where(lane.astype(F32) < count, 1.0, 0.0)
+    block = choose(even, side, dy, lambda o: o, theirs)
+    count = jnp.sum(jnp.where(lane == block, counts, 0.0), axis=1, keepdims=True)
+    return lane.astype(F32) < count
 
 
 def is_even(mine):
@@ -216,10 +217,11 @@
             digits = head_digits(choose(even, side, dy, lambda o: head_cells(source, PARTNER, o), True))
             cells = jnp.concatenate([d.astype(F32) for d in digits], axis=1)
             code = choose(even, side, dy, lambda o: head_codes(source, o), True).astype(F32)
-            live = choose(even, side, dy, lambda o: head_live(source, o), True)
+            counts = head_part(source, SLAB_AT, ODD, 1)
             row = iota((SLAB, PAIR), 0) - ABOVE
             head = jnp.zeros((SLAB, PAIR), F32)
-            for number, line in enumerate((cells, jnp.concatenate([code, code], axis=1), jnp.concatenate([live, live], axis=1))):
+            doubled = [jnp.concatenate([line, line], axis=1) for line in (code, counts)]
+            for number, line in enumerate((cells, *doubled)):
                 head = jnp.where(row == number, line, head)
             slab = jnp.where(row < 0, picked[SLAB_AT:], head)
             out[i * LONG + SLAB_AT : (i + 1) * LONG] = slab.astype(BF)
@@ -271,13 +273,16 @@
     def place_pair(s):
         array, start = other(s)
         codes = [choose(even, *sources[s], lambda o: head_codes(mine, o))]
-        lives = [choose(even, *sources[s], lambda o: head_live(mine, o))]
         if forwarded(s):
             codes.append(head_part(array, start + SLAB_AT, 1, 0).astype(jnp.int32))
-            lives.append(head_part(array, start + SLAB_AT, 2, 0))
+            counts = head_part(array, start + SLAB_AT, 2, 0)
         else:
             codes.append(choose(even, *sources[s], lambda o: head_codes(array, o), True))
-            lives.append(choose(even, *sources[s], lambda o: head_live(array, o), True))
+            counts = head_part(array, SLAB_AT, ODD, 1)
+        lives = [
+            live_slots(even, *sources[s], head_part(mine, SLAB_AT, ODD, 1)),
+            live_slots(even, *sources[s], counts, True),
+        ]
         return place_rows(codes, lives)
 
     if first:

time: 51.1 us -> 51.1 us (level)
  no operation moved by 1% of the time
where the time goes in v9:
time: 51.1 us; the launch traced here: 50.4 us
  Pallas kernels  30.8 us (60%)
  starting transfers between devices  11.8 us (23%)
  waiting for transfers between devices  4.94 us (10%)
  local copies, waits for them, and re-layouts  2.81 us (5%)
    pallas_call x1, Pallas kernels, local(): acc = phase_call('middle')(mine, low, high, far_near, *weights, acc)  9.27 us
    ppermute x2, starting transfers between devices, shift(): lax.ppermute(block, axis, [((i - distance) % count, i) for i in range(cou...  6.72 us
    pallas_call x1, Pallas kernels, local(): velocity = phase_call('end')(mine, far_off, *weights, acc)  6.01 us
    pallas_call x1, Pallas kernels, local(): acc = phase_call('sides')(mine, near, off, *weights, acc)  5.62 us
    ppermute x4, starting transfers between devices, swap(): lax.ppermute(block, 'gx', [(i, (i + (first if i % 2 == 0 else -first)) %...  5.05 us
    pallas_call x1, Pallas kernels, local(): acc = phase_call('here')(mine, *weights, *dense[2:])  4.87 us
    ppermute x4, waiting for transfers between devices, swap(): lax.ppermute(block, 'gx', [(i, (i + (first if i % 2 == 0 else -first)) %...  4.5 us
    unnamed x7, local copies, waits for them, and re-layouts  2.81 us
  transfers between devices with their start and end apart: 6, of which 3 were waited for; matrix products, arithmetic and copies ran while one was open for 6% of the time, Pallas kernels for 43%

profile of v9, /device:TPU:0, one launch (start us, length us, event | category | flops | bytes accessed | tf_op | source)
XLA Modules:
  0.0 50.4 jit_solution(9538133914463648290)
XLA Ops:
  0.0 2.2 %shard_map.82.refs_0_.mine = bf16[880,512]{1,0:T(8,128)(2,1)} custom-call(s32[1,9]{1,0:T(1,128)} %bitcast.12, s32[9,1,128]{2,1,0:T(1,128)} %bitcast.9, s32[9,1,128]{2,1,0:T(1,128)} %bitcast.10, s32[9,1,128]{2,1,0:T(1,128)} %bitcast.11, bf16[3,289,512]{2,1,0:T(8,128)(2,1)} %bitcast.8), custom_call_target="tpu_custom_call" | custom-call | flops 1000 | bytes 1000 | tf_op jit(solution)/shard_map/pallas_call | solution.py:396
  2.2 0.0 copy-start.1
  2.2 0.0 copy-start.2
  2.2 1.7 %collective-permute-start.3 = (bf16[880,512]{1,0:T(8,128)(2,1)}, bf16[880,512]{1,0:T(8,128)(2,1)S(1)}, u32[]{:S(2)}, u32[]{:S(2)}) collective-permute-start(bf16[880,512]{1,0:T(8,128)(2,1)} %shard_map.82.refs_0_.mine), channel_id=1, source_target_pairs={{15,0},{0,1},{1,2},{2,3},{3,4},{4,5},{5,6},{6,7},{7,8},{8,9},{9,10... | collective-permute-start | bytes 2703368 | tf_op jit(solution)/shard_map/ppermute | solution.py:389
  4.0 5.0 %collective-permute-start.2 = (bf16[880,512]{1,0:T(8,128)(2,1)}, bf16[880,512]{1,0:T(8,128)(2,1)S(1)}, u32[]{:S(2)}, u32[]{:S(2)}) collective-permute-start(bf16[880,512]{1,0:T(8,128)(2,1)} %shard_map.82.refs_0_.mine), channel_id=1, source_target_pairs={{1,0},{2,1},{3,2},{4,3},{5,4},{6,5},{7,6},{8,7},{9,8},{10,9},{11,1... | collective-permute-start | bytes 2703368 | tf_op jit(solution)/shard_map/ppermute | solution.py:389
  8.9 1.9 %collective-permute-start.1 = (bf16[880,512]{1,0:T(8,128)(2,1)}, bf16[880,512]{1,0:T(8,128)(2,1)S(1)}, u32[]{:S(2)}, u32[]{:S(2)}) collective-permute-start(bf16[880,512]{1,0:T(8,128)(2,1)} %shard_map.82.refs_0_.mine), channel_id=1, source_target_pairs={{0,112},{16,32},{32,16},{48,64},{64,48},{80,96},{96,80},{112,0},{1... | collective-permute-start | bytes 2703368 | tf_op jit(solution)/shard_map/ppermute | solution.py:384
  10.9 0.0 collective-permute-start
  10.9 2.8 %copy.11.rot_ref.refs_1_.refs_3_.refs_4_.refs_2_ = bf16[16,289,289]{2,1,0:T(8,128)(2,1)S(1)} copy(bf16[16,289,289]{2,0,1:T(8,128)(2,1)} %param.11) | data formatting | bytes 5345344 | tf_op args[3]
  13.7 0.0 copy-done.1
  13.7 0.0 copy-done.2
  13.7 0.0 copy-start
  13.7 1.7 %shard_map.83 = (bf16[8,256,256]{2,1,0:T(8,128)(2,1)S(1)}, bf16[3,256,384]{2,1,0:T(8,128)(2,1)S(1)}, bf16[128,896]{1,0:T(8,128)(2,1)S(1)}, bf16[3,256,384]{2,1,0:T(8,128)(2,1)S(1)}, bf16[128,896]{1,0:T(8,128)(2,1)S(1)}) custom-call(bf16[16,289,289]{2,1,0:T(8,128)(2,1)S(1)} %copy.11.rot_ref.refs_1_.refs_3_.refs_4_.refs_2_, bf16[289,289]{1,0:T(8,128)(2,1)S(1)} %copy-done.1, ...), custom_call_target="tpu_custom_call" | custom-call | flops 1000 | bytes 1000 | tf_op jit(solution)/shard_map/pallas_call | solution.py:415
  15.4 0.0 copy-done
  15.4 4.9 %shard_map.84.refs_7_ = f32[512,896]{1,0:T(8,128)S(1)} custom-call(bf16[880,512]{1,0:T(8,128)(2,1)S(1)} %copy-done, bf16[16,289,289]{2,1,0:T(8,128)(2,1)S(1)} %copy.11.rot_ref.refs_1_.refs_3_.refs_4_.refs_2_, bf16[8,256,256]{2,1,0:T(8,128)(2,1)S(1)} %get-tuple-element.15.refs_2_.refs_4_.refs_5_.refs_3_, ...), custom_call_target="tpu_custom_call" | custom-call | flops 30000001024 | bytes 1000 | tf_op jit(solution)/shard_map/pallas_call | solution.py:420
  20.3 2.7 %collective-permute-done.1.refs_2_.off = bf16[880,512]{1,0:T(8,128)(2,1)S(1)} collective-permute-done((bf16[880,512]{1,0:T(8,128)(2,1)}, bf16[880,512]{1,0:T(8,128)(2,1)S(1)}, u32[]{:S(2)}, u32[]{:S(2)}) %collective-permute-start.1) | collective-permute-done | bytes 901152 | tf_op jit(solution)/shard_map/ppermute | solution.py:384
  23.0 0.0 collective-permute-done.refs_1_.near
  23.0 5.6 %shard_map.85.refs_8_ = f32[512,896]{1,0:T(8,128)S(1)} custom-call(bf16[880,512]{1,0:T(8,128)(2,1)S(1)} %copy-done, bf16[880,512]{1,0:T(8,128)(2,1)S(1)} %collective-permute-done.refs_1_.near, bf16[880,512]{1,0:T(8,128)(2,1)S(1)} %collective-permute-done.1.refs_2_.off, bf16[16,289,289]{2,1,0:T(8,128)(2,1)S(1)} %copy.11.rot_ref.refs_1_.refs_3_.refs_4_.refs_2_, ...), custom_call_target="tpu_custom_call" | custom-call | flops 1000 | bytes 1000 | tf_op jit(solution)/shard_map/pallas_call | solution.py:421
  28.6 0.4 collective-permute-done.3.low.refs_1_
  29.1 0.0 collective-permute-done.2.high.refs_2_
  29.1 1.1 %shard_map.86 = (bf16[1760,256]{1,0:T(8,128)(2,1)S(1)}, bf16[1760,256]{1,0:T(8,128)(2,1)S(1)}) custom-call(bf16[880,512]{1,0:T(8,128)(2,1)S(1)} %copy-done, bf16[880,512]{1,0:T(8,128)(2,1)S(1)} %collective-permute-done.refs_1_.near, bf16[880,512]{1,0:T(8,128)(2,1)S(1)} %collective-permute-done.1.refs_2_.off, ...), custom_call_target="tpu_custom_call" | custom-call | flops 1000 | bytes 1000 | tf_op jit(solution)/shard_map/pallas_call | solution.py:424
  30.2 0.3 collective-permute-start.5
  30.5 2.9 %collective-permute-start.4 = (bf16[1760,256]{1,0:T(8,128)(2,1)S(1)}, bf16[1760,256]{1,0:T(8,128)(2,1)S(1)}, u32[]{:S(2)}, u32[]{:S(2)}) collective-permute-start(bf16[1760,256]{1,0:T(8,128)(2,1)S(1)} %get-tuple-element.22), channel_id=1, source_target_pairs={{0,112},{16,32},{32,16},{48,64},{64,48},{80,96},{96,80},{112,0},{1... | collective-permute-start | bytes 2703368 | tf_op jit(solution)/shard_map/ppermute | solution.py:384
  33.3 0.0 collective-permute-done.5.refs_3_
  33.3 9.3 %shard_map.87.refs_6_ = f32[512,896]{1,0:T(8,128)S(1)} custom-call(bf16[880,512]{1,0:T(8,128)(2,1)S(1)} %copy-done, bf16[880,512]{1,0:T(8,128)(2,1)S(1)} %collective-permute-done.3.low.refs_1_, bf16[880,512]{1,0:T(8,128)(2,1)S(1)} %collective-permute-done.2.high.refs_2_, bf16[1760,256]{1,0:T(8,128)(2,1)S(1)} %collective-permute-done.5.refs_3_, ...), custom_call_target="tpu_custom_call" | custom-call | flops 1000 | bytes 1000 | tf_op jit(solution)/shard_map/pallas_call | solution.py:426
  42.6 1.8 %collective-permute-done.4.refs_1_ = bf16[1760,256]{1,0:T(8,128)(2,1)S(1)} collective-permute-done((bf16[1760,256]{1,0:T(8,128)(2,1)S(1)}, bf16[1760,256]{1,0:T(8,128)(2,1)S(1)}, u32[]{:S(2)}, u32[]{:S(2)}) %collective-permute-start.4) | collective-permute-done | bytes 901152 | tf_op jit(solution)/shard_map/ppermute | solution.py:384
  44.4 6.0 %shard_map.88 = bf16[3,289,512]{2,1,0:T(8,128)(2,1)} custom-call(bf16[880,512]{1,0:T(8,128)(2,1)S(1)} %copy-done, bf16[1760,256]{1,0:T(8,128)(2,1)S(1)} %collective-permute-done.4.refs_1_, bf16[16,289,289]{2,1,0:T(8,128)(2,1)S(1)} %copy.11.rot_ref.refs_1_.refs_3_.refs_4_.refs_2_, bf16[8,256,256]{2,1,0:T(8,128)(2,1)S(1)} %get-tuple-element.15.refs_2_.refs_4_.refs_5_.refs_3_, ...), custom_call_target="tpu_custom_call" | custom-call | flops 1000 | bytes 1000 | tf_op jit(solution)/shard_map/pallas_call | solution.py:427
Async XLA Ops:
  2.2 11.5 %copy-start.1 = (bf16[289,289]{1,0:T(8,128)(2,1)S(1)}, bf16[289,289]{1,0:T(8,128)(2,1)}, u32[]{:S(2)}) copy-start(bf16[289,289]{1,0:T(8,128)(2,1)} %trans_ref.1) | copy-start | bytes 501130
  2.2 11.5 %copy-start.2 = (bf16[289,289]{1,0:T(8,128)(2,1)S(1)}, bf16[289,289]{1,0:T(8,128)(2,1)}, u32[]{:S(2)}) copy-start(bf16[289,289]{1,0:T(8,128)(2,1)} %self_ref.1) | copy-start | bytes 501130
  2.2 26.9 %collective-permute-start.3 = (bf16[880,512]{1,0:T(8,128)(2,1)}, bf16[880,512]{1,0:T(8,128)(2,1)S(1)}, u32[]{:S(2)}, u32[]{:S(2)}) collective-permute-start(bf16[880,512]{1,0:T(8,128)(2,1)} %shard_map.82.refs_0_.mine), channel_id=1, source_target_pairs={{15,0},{0,1},{1,2},{2,3},{3,4},{4,5},{5,6},{6,7},{7,8},{8,9},{9,10... | collective-permute-start | bytes 2703368 | tf_op jit(solution)/shard_map/ppermute | solution.py:389
  4.0 25.1 %collective-permute-start.2 = (bf16[880,512]{1,0:T(8,128)(2,1)}, bf16[880,512]{1,0:T(8,128)(2,1)S(1)}, u32[]{:S(2)}, u32[]{:S(2)}) collective-permute-start(bf16[880,512]{1,0:T(8,128)(2,1)} %shard_map.82.refs_0_.mine), channel_id=1, source_target_pairs={{1,0},{2,1},{3,2},{4,3},{5,4},{6,5},{7,6},{8,7},{9,8},{10,9},{11,1... | collective-permute-start | bytes 2703368 | tf_op jit(solution)/shard_map/ppermute | solution.py:389
  8.9 14.1 %collective-permute-start.1 = (bf16[880,512]{1,0:T(8,128)(2,1)}, bf16[880,512]{1,0:T(8,128)(2,1)S(1)}, u32[]{:S(2)}, u32[]{:S(2)}) collective-permute-start(bf16[880,512]{1,0:T(8,128)(2,1)} %shard_map.82.refs_0_.mine), channel_id=1, source_target_pairs={{0,112},{16,32},{32,16},{48,64},{64,48},{80,96},{96,80},{112,0},{1... | collective-permute-start | bytes 2703368 | tf_op jit(solution)/shard_map/ppermute | solution.py:384
  10.9 12.1 %collective-permute-start = (bf16[880,512]{1,0:T(8,128)(2,1)}, bf16[880,512]{1,0:T(8,128)(2,1)S(1)}, u32[]{:S(2)}, u32[]{:S(2)}) collective-permute-start(bf16[880,512]{1,0:T(8,128)(2,1)} %shard_map.82.refs_0_.mine), channel_id=1, source_target_pairs={{0,16},{16,0},{32,48},{48,32},{64,80},{80,64},{96,112},{112,96},{1... | collective-permute-start | bytes 2703368 | tf_op jit(solution)/shard_map/ppermute | solution.py:384
  13.7 1.7 %copy-start = (bf16[880,512]{1,0:T(8,128)(2,1)S(1)}, bf16[880,512]{1,0:T(8,128)(2,1)}, u32[]{:S(2)}) copy-start(bf16[880,512]{1,0:T(8,128)(2,1)} %shard_map.82.refs_0_.mine) | copy-start | bytes 2703364
  30.2 3.1 %collective-permute-start.5 = (bf16[1760,256]{1,0:T(8,128)(2,1)S(1)}, bf16[1760,256]{1,0:T(8,128)(2,1)S(1)}, u32[]{:S(2)}, u32[]{:S(2)}) collective-permute-start(bf16[1760,256]{1,0:T(8,128)(2,1)S(1)} %get-tuple-element.23), channel_id=1, source_target_pairs={{0,16},{16,0},{32,48},{48,32},{64,80},{80,64},{96,112},{112,96},{1... | collective-permute-start | bytes 2703368 | tf_op jit(solution)/shard_map/ppermute | solution.py:384
  30.5 13.9 %collective-permute-start.4 = (bf16[1760,256]{1,0:T(8,128)(2,1)S(1)}, bf16[1760,256]{1,0:T(8,128)(2,1)S(1)}, u32[]{:S(2)}, u32[]{:S(2)}) collective-permute-start(bf16[1760,256]{1,0:T(8,128)(2,1)S(1)} %get-tuple-element.22), channel_id=1, source_target_pairs={{0,112},{16,32},{32,16},{48,64},{64,48},{80,96},{96,80},{112,0},{1... | collective-permute-start | bytes 2703368 | tf_op jit(solution)/shard_map/ppermute | solution.py:384
